TPU v7x, 256 devices: a whole 4x4x8 slice. The times are simulated.
256 devices in a mesh: sec: 2 (over core), row: 16 (over x, y), col: 8 (over z).
Axes of the slice: x: 4, y: 4, z: 8, core: 2. Of those that a mesh axis runs over, the one named last changes fastest.
Arguments:
- images: bfloat16 [2, 256, 256, 384], P('sec', 'row', 'col'), may hold values from -6 to 6
- kernel_one: float32 [49, 384], replicated, may hold values from -0.875 to 0.875
- gain_one: float32 [384], replicated, may hold values from 0.5 to 1.5
- shift_one: float32 [384], replicated, may hold values from -3 to 3
- up_one: bfloat16 [384, 1536], P(None, ('sec', 'row', 'col')), may hold values from -0.3125 to 0.3125
- up_bias_one: float32 [1536], replicated, may hold values from -3 to 3
- down_one: bfloat16 [384, 1536], P(None, ('sec', 'row', 'col')), may hold values from -0.15625 to 0.15625
- down_bias_one: float32 [384], replicated, may hold values from -3 to 3
- scale_one: float32 [384], replicated, may hold values from 0.3 to 1.5
- gain_mid: float32 [384], replicated, may hold values from 0.5 to 1.5
- shift_mid: float32 [384], replicated, may hold values from -3 to 3
- merge_weight: bfloat16 [1536, 768], replicated, may hold values from -0.15625 to 0.15625
- merge_bias: float32 [768], replicated, may hold values from -3 to 3
- kernel_two: float32 [49, 768], replicated, may hold values from -0.875 to 0.875
- gain_two: float32 [768], replicated, may hold values from 0.5 to 1.5
- shift_two: float32 [768], replicated, may hold values from -3 to 3
- up_two: bfloat16 [768, 3072], P(None, ('sec', 'row', 'col')), may hold values from -0.21875 to 0.21875
- up_bias_two: float32 [3072], replicated, may hold values from -3 to 3
- down_two: bfloat16 [768, 3072], P(None, ('sec', 'row', 'col')), may hold values from -0.109375 to 0.109375
- down_bias_two: float32 [768], replicated, may hold values from -3 to 3
- scale_two: float32 [768], replicated, may hold values from 0.3 to 1.5
- grad_out: bfloat16 [2, 128, 128, 768], P('sec', 'row', 'col'), may hold values from -6 to 6
Outputs:
- features: bfloat16 [2, 128, 128, 768], P('sec', 'row', 'col')
- input_grad: bfloat16 [2, 256, 256, 384], P('sec', 'row', 'col')
All inputs are finite; a program needn't handle non-finite values.
Results may differ from a plain program's by a relative error of at most 0.02.
Values may be sent and summed in bfloat16 or wider, within the bound.
No kernel may reach another device: no remote copies, remote signals or barrier semaphores. Data moves between devices by JAX's collectives and lax.ppermute only.
A program may use at most 128 MiB of HBM per device.

v0:
```python
import jax
import jax.numpy as jnp
from jax import lax
from jax.experimental import pallas as pl
from jax.experimental.pallas import tpu as pltpu
from jax.sharding import PartitionSpec as P

norm_eps = 1e-06


def exchange(block, axis, dim, width):
    count = lax.axis_size(axis)
    forward = [(i, i + 1) for i in range(count - 1)]
    backward = [(target, source) for source, target in forward]
    low = lax.ppermute(
        lax.slice_in_dim(block, block.shape[dim] - width, None, axis=dim), axis, forward
    )
    high = lax.ppermute(lax.slice_in_dim(block, 0, width, axis=dim), axis, backward)
    return low, high


def halo_of(block, width):
    dim = block.ndim - 2
    top, bottom = exchange(block, "row", 0, 3)

    def edge(first, last):
        parts = [lax.slice_in_dim(part, first, last, axis=dim) for part in (top, block, bottom)]
        return jnp.concatenate(parts, axis=0)

    count = lax.axis_size("col")
    extent = block.shape[dim]
    forward = [(i, i + 1) for i in range(count - 1)]
    backward = [(target, source) for source, target in forward]
    left = lax.ppermute(edge(extent - width, extent), "col", forward)
    right = lax.ppermute(edge(0, width), "col", backward)
    return top, bottom, left, right


def ring_collect(piece, axis, inner, stride):
    count = lax.axis_size(axis)
    found = [piece]
    for shift in range(1, inner):
        pairs = []
        for target in range(count):
            place = (target // stride) % inner
            source = target + ((place + shift) % inner - place) * stride
            pairs.append((source, target))
        found.append(lax.ppermute(piece, axis, pairs))
    return jnp.concatenate(found, axis=0)


def gelu_exact(values):
    return 0.5 * values * (1.0 + lax.erf(values * 0.7071067811865476))


def gelu_slope(values):
    return (
        0.5 * (1.0 + lax.erf(values * 0.7071067811865476))
        + values * jnp.exp(-0.5 * values * values) * 0.3989422804014327
    )


def norm_forward(values, norm_gain, norm_shift):
    center = values - jnp.mean(values, axis=-1, keepdims=True)
    inv_std = lax.rsqrt(jnp.mean(center * center, axis=-1, keepdims=True) + norm_eps)
    scaled = center * inv_std
    return (scaled, inv_std, scaled * norm_gain + norm_shift)


def norm_backward(upstream, scaled, inv_std, norm_gain):
    weighted = upstream * norm_gain
    mean_one = jnp.mean(weighted, axis=-1, keepdims=True)
    mean_two = jnp.mean(weighted * scaled, axis=-1, keepdims=True)
    return inv_std * (weighted - mean_one - scaled * mean_two)


def contract_last(left_side, right_side):
    return lax.dot_general(
        left_side, right_side, (((1,), (1,)), ((), ())), preferred_element_type=jnp.float32
    )


def dense_forward(normed, weights, up_bias, down_bias):
    width = normed.shape[1]
    pre_acts = []
    branch = down_bias
    for part, part_bias in zip(weights, up_bias):
        pre_act = contract_last(normed, part[:, :width]) + part_bias
        hidden = gelu_exact(pre_act).astype(jnp.bfloat16)
        branch = branch + jnp.dot(hidden, part[:, width:], preferred_element_type=jnp.float32)
        pre_acts.append(pre_act)
    return (branch, pre_acts)


def dense_backward(d_branch, pre_acts, weights):
    width = d_branch.shape[1]
    total = 0.0
    for part, pre_act in zip(weights, pre_acts):
        d_hidden = contract_last(d_branch, part[:, width:])
        d_pre = (d_hidden * gelu_slope(pre_act)).astype(jnp.bfloat16)
        total = total + jnp.dot(d_pre, part[:, :width], preferred_element_type=jnp.float32)
    return total


lanes = 128


def fill_rows(frame, source, first, width):
    for row in range(source.shape[0]):
        for tile in range(source.shape[-1] // lanes):
            part = source[row, :, tile * lanes : (tile + 1) * lanes].astype(jnp.float32)
            frame[tile, first + row, 8 : 8 + width, :] = part


def fill_edges(frame, left, right, width):
    for row in range(left.shape[0]):
        for tile in range(left.shape[-1] // lanes):
            span = slice(tile * lanes, (tile + 1) * lanes)
            frame[tile, row, 5:8, :] = left[row, :, span].astype(jnp.float32)
            frame[tile, row, 8 + width : 11 + width, :] = right[row, :, span].astype(jnp.float32)


def fill_parity_rows(frame, source, first):
    halves = source.shape[2]
    for row in range(source.shape[0]):
        for tile in range(source.shape[-1] // lanes):
            for parity in range(2):
                part = source[row, parity, :, tile * lanes : (tile + 1) * lanes]
                frame[tile, first + row, pl.ds(8 + parity, halves, stride=2), :] = part.astype(
                    jnp.float32
                )


def fill_parity_edges(frame, left, right, width):
    for row in range(left.shape[0]):
        for tile in range(left.shape[-1] // lanes):
            span = slice(tile * lanes, (tile + 1) * lanes)
            for parity in range(2):
                for half in range(2):
                    col = 2 * half + parity
                    frame[tile, row, 4 + col : 5 + col, :] = left[
                        row, parity, half : half + 1, span
                    ].astype(jnp.float32)
                    frame[tile, row, 8 + width + col : 9 + width + col, :] = right[
                        row, parity, half : half + 1, span
                    ].astype(jnp.float32)


def depthwise(frame, taps, tile, rows, cols, first, stride, flipped):
    sums = [jnp.zeros((cols, lanes), jnp.float32) for _ in range(rows)]
    span = pl.ds(pl.multiple_of(tile * lanes, lanes), lanes)
    for tap_col in range(7):
        weights = [taps[pl.ds(7 * tap_row + tap_col, 1), span] for tap_row in range(7)]
        start = 5 + first + (6 - tap_col if flipped else tap_col)
        for row in range(rows + 6):
            if stride == 1:
                values = frame[tile, row, pl.ds(start, cols), :]
            else:
                values = frame[tile, row, pl.ds(start, cols, stride=stride), :]
            for tap_row in range(7):
                target = row - (6 - tap_row if flipped else tap_row)
                if 0 <= target < rows:
                    sums[target] = sums[target] + values * weights[tap_row]
    return sums


def norm_rows(values_ref, normed_ref, gain_ref, shift_ref, chunk):
    gain = gain_ref[...]
    shift = shift_ref[...]

    def step(index, carry):
        span = pl.ds(pl.multiple_of(index * chunk, chunk), chunk)
        values = values_ref[span, :].astype(jnp.float32)
        normed_ref[span, :] = norm_forward(values, gain, shift)[2].astype(normed_ref.dtype)
        return carry

    lax.fori_loop(0, values_ref.shape[0] // chunk, step, 0)


def conv_one_kernel(
    tile_ref, top, bottom, left, right, taps, gain, shift, normed, conv, residual, frame
):
    rows, width, channels = tile_ref.shape
    halves = width // 2
    fill_rows(frame, top, 0, width)
    fill_rows(frame, tile_ref, 3, width)
    fill_rows(frame, bottom, 3 + rows, width)
    fill_edges(frame, left, right, width)

    def step(tile, carry):
        span = pl.ds(pl.multiple_of(tile * lanes, lanes), lanes)
        for parity in range(2):
            sums = depthwise(frame, taps, tile, rows, halves, parity, 2, False)
            for row in range(rows):
                place = pl.ds(row * width + parity * halves, halves)
                conv[place, span] = sums[row]
                own = frame[tile, 3 + row, pl.ds(8 + parity, halves, stride=2), :]
                residual[place, span] = own.astype(residual.dtype)
        return carry

    lax.fori_loop(0, channels // lanes, step, 0)
    norm_rows(conv, normed, gain, shift, 64)


def back_one_kernel(tile_ref, top, bottom, left, right, taps, upstream, out, frame, total):
    rows, _, halves, channels = tile_ref.shape
    width = 2 * halves
    fill_parity_rows(frame, top, 0)
    fill_parity_rows(frame, tile_ref, 3)
    fill_parity_rows(frame, bottom, 3 + rows)
    fill_parity_edges(frame, left, right, width)

    def step(tile, carry):
        span = pl.ds(pl.multiple_of(tile * lanes, lanes), lanes)
        for parity in range(2):
            sums = depthwise(frame, taps, tile, rows, halves, parity, 2, True)
            for row in range(rows):
                place = pl.ds(row * width + parity * halves, halves)
                total[row, pl.ds(parity, halves, stride=2), :] = sums[row] + upstream[place, span]
        for row in range(rows):
            out[row, :, span] = total[row].astype(out.dtype)
        return carry

    lax.fori_loop(0, channels // lanes, step, 0)


def conv_two_kernel(tile_ref, top, bottom, left, right, taps, gain, shift, normed, conv, frame):
    rows, width, channels = tile_ref.shape
    fill_rows(frame, top, 0, width)
    fill_rows(frame, tile_ref, 3, width)
    fill_rows(frame, bottom, 3 + rows, width)
    fill_edges(frame, left, right, width)

    def step(tile, carry):
        span = pl.ds(pl.multiple_of(tile * lanes, lanes), lanes)
        sums = depthwise(frame, taps, tile, rows, width, 0, 1, False)
        for row in range(rows):
            conv[pl.ds(row * width, width), span] = sums[row].astype(conv.dtype)
        return carry

    lax.fori_loop(0, channels // lanes, step, 0)
    norm_rows(conv, normed, gain, shift, 64)


def back_two_kernel(tile_ref, top, bottom, left, right, taps, grad, out, frame):
    rows, width, channels = tile_ref.shape
    fill_rows(frame, top, 0, width)
    fill_rows(frame, tile_ref, 3, width)
    fill_rows(frame, bottom, 3 + rows, width)
    fill_edges(frame, left, right, width)

    def step(tile, carry):
        span = pl.ds(pl.multiple_of(tile * lanes, lanes), lanes)
        sums = depthwise(frame, taps, tile, rows, width, 0, 1, True)
        for row in range(rows):
            place = pl.ds(row * width, width)
            d_taps = sums[row].astype(jnp.bfloat16).astype(jnp.float32)
            out[place, span] = (d_taps + grad[place, span].astype(jnp.float32)).astype(out.dtype)
        return carry

    lax.fori_loop(0, channels // lanes, step, 0)


def tile_call(kernel, outputs, rows, width, channels, operands, extra=()):
    whole = pl.BlockSpec(memory_space=pltpu.VMEM)
    frame = pltpu.VMEM((channels // lanes, rows + 6, width + 16, lanes), jnp.float32)
    return pl.pallas_call(
        kernel,
        out_shape=outputs,
        in_specs=[whole] * len(operands),
        out_specs=jax.tree.map(lambda _: whole, outputs),
        scratch_shapes=[frame, *extra],
        compiler_params=pltpu.CompilerParams(vmem_limit_bytes=32 * 1024 * 1024),
    )(*operands)


def on_device(
    images,
    kernel_one,
    gain_one,
    shift_one,
    up_one,
    up_bias_one,
    down_one,
    down_bias_one,
    scale_one,
    gain_mid,
    shift_mid,
    merge_weight,
    merge_bias,
    kernel_two,
    gain_two,
    shift_two,
    up_two,
    up_bias_two,
    down_two,
    down_bias_two,
    scale_two,
    grad_out,
):
    micro_count, tile_rows, tile_cols, width_one = images.shape
    width_two = merge_weight.shape[1]
    half_rows = tile_rows // 2
    half_cols = tile_cols // 2
    rows_one = micro_count * tile_rows * tile_cols
    rows_two = micro_count * half_rows * half_cols

    swap = [(0, 1), (1, 0)]
    side = lax.axis_index("sec")
    row_count = lax.axis_size("row")
    col_count = lax.axis_size("col")
    inner = 4 if row_count % 4 == 0 else row_count
    outer = row_count // inner

    def both_halves(own):
        return (own, lax.ppermute(own, "sec", swap))

    def rolled(bias, roll_rows):
        grid = bias.reshape(2, outer, inner, col_count, -1)
        grid = jnp.concatenate([grid, grid], axis=3)
        row_index = lax.axis_index("row")
        start = (0, 0)
        if roll_rows:
            grid = jnp.concatenate([grid, grid], axis=1)
            grid = jnp.concatenate([grid, grid], axis=2)
            start = (row_index // inner, row_index % inner)
        sizes = (1, outer, inner, col_count, grid.shape[4])
        tail = (*start, lax.axis_index("col"), 0)
        return tuple(
            lax.dynamic_slice(grid, (half, *tail), sizes).reshape(-1) for half in (side, 1 - side)
        )

    share_two = up_two.shape[1]
    packed_one = jnp.concatenate([up_one.T, down_one.T], axis=1)
    packed = jnp.concatenate([up_two.T, down_two.T, packed_one], axis=0)
    column = ring_collect(packed[None], "col", col_count, 1)
    part_one = column[:, 2 * share_two :].reshape(-1, 2 * width_one)
    part_two = jnp.concatenate(
        [
            column[:, :share_two].reshape(-1, width_two),
            column[:, share_two : 2 * share_two].reshape(-1, width_two),
        ],
        axis=1,
    )
    own_two = lax.all_gather(part_two, "row", axis=0, tiled=True)
    own_one = ring_collect(ring_collect(part_one, "row", inner, 1), "row", outer, inner)
    pair_one = both_halves(own_one)
    pair_two = both_halves(own_two)
    bias_one = rolled(up_bias_one, True)
    bias_two = rolled(up_bias_two, False)

    image_tile = images.reshape(tile_rows, tile_cols, width_one)
    normed_one, conv_one, images_par = tile_call(
        conv_one_kernel,
        (
            jax.ShapeDtypeStruct((rows_one, width_one), jnp.bfloat16),
            jax.ShapeDtypeStruct((rows_one, width_one), jnp.float32),
            jax.ShapeDtypeStruct((rows_one, width_one), jnp.bfloat16),
        ),
        tile_rows,
        tile_cols,
        width_one,
        (image_tile, *halo_of(image_tile, 3), kernel_one, gain_one[None], shift_one[None]),
    )
    scaled_one, inv_one, _ = norm_forward(conv_one, gain_one, shift_one)
    branch_one, pre_one = dense_forward(normed_one, pair_one, bias_one, down_bias_one)
    section_out = (
        images_par.astype(jnp.float32) + scale_one * branch_one
    ).astype(jnp.bfloat16)
    scaled_mid, inv_mid, normed_mid = norm_forward(
        section_out.astype(jnp.float32), gain_mid, shift_mid
    )
    patches = normed_mid.astype(jnp.bfloat16).reshape(
        micro_count * half_rows, 4, half_cols, width_one
    )
    patches = jnp.concatenate(
        [patches[:, place].reshape(rows_two, width_one) for place in range(4)], axis=1
    )
    merged = (
        jnp.dot(patches, merge_weight, preferred_element_type=jnp.float32) + merge_bias
    ).astype(jnp.bfloat16)
    merged_tile = merged.reshape(half_rows, half_cols, width_two)
    normed_two, conv_two = tile_call(
        conv_two_kernel,
        (
            jax.ShapeDtypeStruct((rows_two, width_two), jnp.bfloat16),
            jax.ShapeDtypeStruct((rows_two, width_two), jnp.bfloat16),
        ),
        half_rows,
        half_cols,
        width_two,
        (merged_tile, *halo_of(merged_tile, 3), kernel_two, gain_two[None], shift_two[None]),
    )
    scaled_two, inv_two, _ = norm_forward(conv_two.astype(jnp.float32), gain_two, shift_two)
    branch_two, pre_two = dense_forward(normed_two, pair_two, bias_two, down_bias_two)
    features = (merged.astype(jnp.float32) + scale_two * branch_two).astype(jnp.bfloat16)
    grad_rows = grad_out.reshape(rows_two, width_two)
    d_branch_two = (grad_rows.astype(jnp.float32) * scale_two).astype(jnp.bfloat16)
    d_normed_two = dense_backward(d_branch_two, pre_two, pair_two)
    d_conv_two = norm_backward(d_normed_two, scaled_two, inv_two, gain_two).astype(jnp.bfloat16)
    back_tile = d_conv_two.reshape(half_rows, half_cols, width_two)
    d_merged = tile_call(
        back_two_kernel,
        jax.ShapeDtypeStruct((rows_two, width_two), jnp.bfloat16),
        half_rows,
        half_cols,
        width_two,
        (back_tile, *halo_of(back_tile, 3), kernel_two, grad_rows),
    )
    d_patches = contract_last(d_merged, merge_weight)
    d_normed_mid = jnp.stack(
        [
            d_patches[:, place * width_one : (place + 1) * width_one].reshape(
                micro_count * half_rows, half_cols, width_one
            )
            for place in range(4)
        ],
        axis=1,
    ).reshape(rows_one, width_one)
    upstream_one = norm_backward(d_normed_mid, scaled_mid, inv_mid, gain_mid)
    d_branch_one = (upstream_one * scale_one).astype(jnp.bfloat16)
    d_normed_one = dense_backward(d_branch_one, pre_one, pair_one)
    d_conv_one = norm_backward(d_normed_one, scaled_one, inv_one, gain_one).astype(jnp.bfloat16)
    d_conv_one = d_conv_one.reshape(tile_rows, 2, half_cols, width_one)
    input_grad = tile_call(
        back_one_kernel,
        jax.ShapeDtypeStruct((tile_rows, tile_cols, width_one), jnp.bfloat16),
        tile_rows,
        tile_cols,
        width_one,
        (d_conv_one, *halo_of(d_conv_one, 2), kernel_one, upstream_one),
        (pltpu.VMEM((tile_rows, tile_cols, lanes), jnp.float32),),
    ).reshape(images.shape)
    return (features.reshape(micro_count, half_rows, half_cols, width_two), input_grad)


def solution(mesh):
    in_specs = (
        P("sec", "row", "col", None),
        P(),
        P(),
        P(),
        P(None, ("sec", "row", "col")),
        P(),
        P(None, ("sec", "row", "col")),
        P(),
        P(),
        P(),
        P(),
        P(),
        P(),
        P(),
        P(),
        P(),
        P(None, ("sec", "row", "col")),
        P(),
        P(None, ("sec", "row", "col")),
        P(),
        P(),
        P("sec", "row", "col", None),
    )
    out_specs = (P("sec", "row", "col", None), P("sec", "row", "col", None))
    return jax.shard_map(
        on_device, mesh=mesh, in_specs=in_specs, out_specs=out_specs, check_vma=False
    )
```

profile of v0, /device:TPU:2, one launch (start us, length us, event | category | flops | bytes accessed | tf_op | source)
XLA Modules:
  0.0 220.4 jit_solution(12953127987164952628)
XLA Ops:
  8.2 5.9 %collective-permute-start.4 = (bf16[1,30,768]{2,1,0:T(8,128)(2,1)S(1)}, bf16[1,30,768]{2,1,0:T(8,128)(2,1)S(1)}, u32[]{:S(2)}, u32[]{:S(2)}) collective-permute-start(bf16[1,30,768]{2,1,0:T(8,128)(2,1)S(1)} %get-tuple-element.17), channel_id=1, source_target_pairs={{1,0},{2,1},{3,2},{4,3},{5,4},{6,5},{7,6},{0,7},{9,8},{10,9},{11,1... | collective-permute-start | bytes 138248 | tf_op jit(solution)/shard_map/ppermute | solution.py:48
  14.1 4.4 %collective-permute-start.8 = (bf16[1,30,768]{2,1,0:T(8,128)(2,1)S(1)}, bf16[1,30,768]{2,1,0:T(8,128)(2,1)S(1)}, u32[]{:S(2)}, u32[]{:S(2)}) collective-permute-start(bf16[1,30,768]{2,1,0:T(8,128)(2,1)S(1)} %get-tuple-element.17), channel_id=1, source_target_pairs={{5,0},{6,1},{7,2},{0,3},{1,4},{2,5},{3,6},{4,7},{13,8},{14,9},{15,... | collective-permute-start | bytes 138248 | tf_op jit(solution)/shard_map/ppermute | solution.py:48
  20.6 4.1 %collective-permute-start.5 = (bf16[1,30,768]{2,1,0:T(8,128)(2,1)S(1)}, bf16[1,30,768]{2,1,0:T(8,128)(2,1)S(1)}, u32[]{:S(2)}, u32[]{:S(2)}) collective-permute-start(bf16[1,30,768]{2,1,0:T(8,128)(2,1)S(1)} %get-tuple-element.17), channel_id=1, source_target_pairs={{2,0},{3,1},{4,2},{5,3},{6,4},{7,5},{0,6},{1,7},{10,8},{11,9},{12,... | collective-permute-start | bytes 138248 | tf_op jit(solution)/shard_map/ppermute | solution.py:48
  29.4 3.3 %collective-permute-done.6 = bf16[1,30,768]{2,1,0:T(8,128)(2,1)S(1)} collective-permute-done((bf16[1,30,768]{2,1,0:T(8,128)(2,1)S(1)}, bf16[1,30,768]{2,1,0:T(8,128)(2,1)S(1)}, u32[]{:S(2)}, u32[]{:S(2)}) %collective-permute-start.6) | collective-permute-done | bytes 46112 | tf_op jit(solution)/shard_map/ppermute | solution.py:48
  35.1 4.9 %collective-permute-start.1 = (bf16[3,32,384]{2,1,0:T(8,128)(2,1)}, bf16[3,32,384]{2,1,0:T(8,128)(2,1)S(1)}, u32[]{:S(2)}, u32[]{:S(2)}) collective-permute-start(bf16[3,32,384]{2,1,0:T(8,128)(2,1)} %get-tuple-element.34), channel_id=1, source_target_pairs={{8,0},{16,8},{24,16},{32,24},{40,32},{48,40},{56,48},{64,56},{72,6... | collective-permute-start | bytes 221192 | tf_op jit(solution)/shard_map/ppermute | solution.py:18
  47.0 5.0 %collective-permute-start.12 = (bf16[48,768]{1,0:T(8,128)(2,1)S(1)}, bf16[48,768]{1,0:T(8,128)(2,1)S(1)}, u32[]{:S(2)}, u32[]{:S(2)}) collective-permute-start(bf16[48,768]{1,0:T(8,128)(2,1)S(1)} %reshape.138), channel_id=1, source_target_pairs={{16,0},{24,8},{0,16},{8,24},{48,32},{56,40},{32,48},{40,56},{80,64... | collective-permute-start | bytes 221192 | tf_op jit(solution)/shard_map/ppermute | solution.py:48
  52.6 4.3 %collective-permute-done.11 = bf16[48,768]{1,0:T(8,128)(2,1)S(1)} collective-permute-done((bf16[48,768]{1,0:T(8,128)(2,1)S(1)}, bf16[48,768]{1,0:T(8,128)(2,1)S(1)}, u32[]{:S(2)}, u32[]{:S(2)}) %collective-permute-start.11) | collective-permute-done | bytes 73760 | tf_op jit(solution)/shard_map/ppermute | solution.py:48
  63.0 5.3 %collective-permute-done.14 = bf16[192,768]{1,0:T(8,128)(2,1)S(1)} collective-permute-done((bf16[192,768]{1,0:T(8,128)(2,1)S(1)}, bf16[192,768]{1,0:T(8,128)(2,1)S(1)}, u32[]{:S(2)}, u32[]{:S(2)}) %collective-permute-start.14) | collective-permute-done | bytes 294944 | tf_op jit(solution)/shard_map/ppermute | solution.py:48
  69.0 5.3 %collective-permute-done.15 = bf16[192,768]{1,0:T(8,128)(2,1)S(1)} collective-permute-done((bf16[192,768]{1,0:T(8,128)(2,1)S(1)}, bf16[192,768]{1,0:T(8,128)(2,1)S(1)}, u32[]{:S(2)}, u32[]{:S(2)}) %collective-permute-start.15) | collective-permute-done | bytes 294944 | tf_op jit(solution)/shard_map/ppermute | solution.py:48
  90.5 4.7 %shard_map.221 = (bf16[512,384]{1,0:T(8,128)(2,1)S(1)}, f32[512,384]{1,0:T(8,128)S(1)}, bf16[512,384]{1,0:T(8,128)(2,1)S(1)}) custom-call(bf16[16,32,384]{2,1,0:T(8,128)(2,1)S(1)} %bitcast.67, bf16[3,32,384]{2,1,0:T(8,128)(2,1)S(1)} %copy-done.12, bf16[3,32,384]{2,1,0:T(8,128)(2,1)S(1)} %copy-done.10, bf16[22,3,384]{2,1,0:T(4,128)(2,1)S(1)} %copy-done.14, ...), custom_call_target="tpu_custom_call" | custom-call | tf_op jit(solution)/shard_map/pallas_call | solution.py:267
  111.1 6.0 %collective-permute-start.19 = (bf16[3,16,768]{2,1,0:T(8,128)(2,1)S(1)}, bf16[3,16,768]{2,1,0:T(8,128)(2,1)S(1)}, u32[]{:S(2)}, u32[]{:S(2)}) collective-permute-start(bf16[3,16,768]{2,1,0:T(8,128)(2,1)S(1)} %bitcast.83), channel_id=1, source_target_pairs={{8,0},{16,8},{24,16},{32,24},{40,32},{48,40},{56,48},{64,56},{72,6... | collective-permute-start | bytes 221192 | tf_op jit(solution)/shard_map/ppermute | solution.py:18
  119.2 4.0 %collective-permute-start.20 = (bf16[14,3,768]{2,1,0:T(4,128)(2,1)S(1)}, bf16[14,3,768]{2,1,0:T(4,128)(2,1)S(1)}, u32[]{:S(2)}, u32[]{:S(2)}) collective-permute-start(bf16[14,3,768]{2,1,0:T(4,128)(2,1)S(1)} %pad_maximum_fusion.2), channel_id=1, source_target_pairs={{0,1},{1,2},{2,3},{3,4},{4,5},{5,6},{6,7},{8,9},{9,10},{10,11},{11... | collective-permute-start | bytes 193544 | tf_op jit(solution)/shard_map/ppermute | solution.py:34
  125.2 4.4 %collective-permute-done.21.right = bf16[14,3,768]{2,1,0:T(4,128)(2,1)S(1)} collective-permute-done((bf16[14,3,768]{2,1,0:T(4,128)(2,1)S(1)}, bf16[14,3,768]{2,1,0:T(4,128)(2,1)S(1)}, u32[]{:S(2)}, u32[]{:S(2)}) %collective-permute-start.21) | collective-permute-done | bytes 64544 | tf_op jit(solution)/shard_map/ppermute | solution.py:35
  134.6 4.8 %fusion.11 = f32[128,768]{1,0:T(8,128)} fusion(bf16[1536,1536]{1,0:T(8,128)(2,1)} %all-gather.2.cloned.1.call-done, f32[128,1536]{1,0:T(8,128)} %convolution_add_fusion.1, bf16[128,768]{1,0:T(8,128)(2,1)} %bitcast.70, f32[768]{0:T(1024)} %param.42), kind=kOutput, calls=%fused_computation.17 | convolution fusion | flops 606240768 | bytes 6097920 | tf_op jit(solution)/shard_map/dot_general | solution.py:101
  139.4 3.6 %convolution_add_fusion = f32[128,1536]{1,0:T(8,128)} fusion(bf16[128,768]{1,0:T(8,128)(2,1)} %copy-done.19, bf16[1536,1536]{1,0:T(8,128)(2,1)} %collective-permute-done.22, f32[1536]{0:T(1024)S(1)} %copy-done.35), kind=kOutput, calls=%fused_computation.2 | convolution fusion | flops 302186496 | bytes 3348480 | tf_op jit(solution)/shard_map/dot_general | solution.py:78
  142.9 5.3 %fusion.150 = (f32[128]{0:T(128)}, f32[128]{0:T(128)}, f32[128,768]{1,0:T(8,128)}) fusion(f32[128]{0:T(128)} %add_rsqrt_fusion.2, f32[128]{0:T(128)} %copy-done.41, bf16[128,768]{1,0:T(8,128)(2,1)S(1)} %get-tuple-element.11, f32[768]{0:T(1024)} %param.36, f32[128,768]{1,0:T(8,128)} %fusion.11, bf16[1536,1536]{1,0:T(8,128)(2,1)} %collective-permute-done.22, ...), kind=kOutput, calls=%fused_computation.207 | convolution fusion | flops 607026944 | bytes 6692864 | tf_op jit(solution)/shard_map/dot_general | solution.py:101
  152.1 6.4 %collective-permute-start.24 = (bf16[3,16,768]{2,1,0:T(8,128)(2,1)S(1)}, bf16[3,16,768]{2,1,0:T(8,128)(2,1)S(1)}, u32[]{:S(2)}, u32[]{:S(2)}) collective-permute-start(bf16[3,16,768]{2,1,0:T(8,128)(2,1)S(1)} %bitcast.84), channel_id=1, source_target_pairs={{8,0},{16,8},{24,16},{32,24},{40,32},{48,40},{56,48},{64,56},{72,6... | collective-permute-start | bytes 221192 | tf_op jit(solution)/shard_map/ppermute | solution.py:18
  160.6 3.8 %collective-permute-start.25 = (bf16[14,3,768]{2,1,0:T(4,128)(2,1)S(1)}, bf16[14,3,768]{2,1,0:T(4,128)(2,1)S(1)}, u32[]{:S(2)}, u32[]{:S(2)}) collective-permute-start(bf16[14,3,768]{2,1,0:T(4,128)(2,1)S(1)} %pad_maximum_fusion.4), channel_id=1, source_target_pairs={{0,1},{1,2},{2,3},{3,4},{4,5},{5,6},{6,7},{8,9},{9,10},{10,11},{11... | collective-permute-start | bytes 193544 | tf_op jit(solution)/shard_map/ppermute | solution.py:34
  178.7 4.0 %fusion.30 = f32[512,384]{1,0:T(8,128)} fusion(f32[512,768]{1,0:T(8,128)} %convolution_add_fusion.2, bf16[768,768]{1,0:T(8,128)(2,1)} %collective-permute-done.17, f32[512,384]{1,0:T(8,128)} %fusion.71.upstream, f32[384]{0:T(512)S(1)} %copy-done.52), kind=kOutput, calls=%fused_computation.38 | convolution fusion | flops 608305152 | bytes 4326912 | tf_op jit(solution)/shard_map/dot_general | solution.py:101
  182.7 4.4 %fusion.149 = (f32[512]{0:T(512)S(1)}, f32[512]{0:T(512)S(1)}, f32[512,384]{1,0:T(8,128)}) fusion(f32[512]{0:T(512)S(1)} %copy-done.37, f32[512,384]{1,0:T(8,128)S(1)} %get-tuple-element.10, f32[512]{0:T(512)S(1)} %copy-done.29, f32[384]{0:T(512)S(1)} %copy-done.45, f32[512,384]{1,0:T(8,128)} %fusion.30, ...), kind=kOutput, calls=%fused_computation.206 | convolution fusion | flops 609680384 | bytes 5909504 | tf_op jit(solution)/shard_map/dot_general | solution.py:101
  188.7 3.7 %collective-permute-start.27 = (bf16[3,2,16,384]{3,2,1,0:T(8,128)(2,1)S(1)}, bf16[3,2,16,384]{3,2,1,0:T(8,128)(2,1)S(1)}, u32[]{:S(2)}, u32[]{:S(2)}) collective-permute-start(bf16[3,2,16,384]{3,2,1,0:T(8,128)(2,1)S(1)} %bitcast.88), channel_id=1, source_target_pairs={{0,8},{8,16},{16,24},{24,32},{32,40},{40,48},{48,56},{56,64},{64,7... | collective-permute-start | bytes 221192 | tf_op jit(solution)/shard_map/ppermute | solution.py:15
  192.5 4.6 %collective-permute-start.28 = (bf16[3,2,16,384]{3,2,1,0:T(8,128)(2,1)S(1)}, bf16[3,2,16,384]{3,2,1,0:T(8,128)(2,1)S(1)}, u32[]{:S(2)}, u32[]{:S(2)}) collective-permute-start(bf16[3,2,16,384]{3,2,1,0:T(8,128)(2,1)S(1)} %bitcast.85), channel_id=1, source_target_pairs={{8,0},{16,8},{24,16},{32,24},{40,32},{48,40},{56,48},{64,56},{72,6... | collective-permute-start | bytes 221192 | tf_op jit(solution)/shard_map/ppermute | solution.py:18
  199.2 4.3 %collective-permute-start.29 = (bf16[22,2,2,384]{3,2,1,0:T(2,128)(2,1)S(1)}, bf16[22,2,2,384]{3,2,1,0:T(2,128)(2,1)S(1)}, u32[]{:S(2)}, u32[]{:S(2)}) collective-permute-start(bf16[22,2,2,384]{3,2,1,0:T(2,128)(2,1)S(1)} %pad_maximum_fusion.8), channel_id=1, source_target_pairs={{0,1},{1,2},{2,3},{3,4},{4,5},{5,6},{6,7},{8,9},{9,10},{10,11},{11... | collective-permute-start | bytes 202760 | tf_op jit(solution)/shard_map/ppermute | solution.py:34
  210.0 3.5 %shard_map.224 = bf16[16,32,384]{2,1,0:T(8,128)(2,1)} custom-call(bf16[16,2,16,384]{3,2,1,0:T(8,128)(2,1)S(1)} %bitcast.63, bf16[3,2,16,384]{3,2,1,0:T(8,128)(2,1)S(1)} %collective-permute-done.27.top, bf16[3,2,16,384]{3,2,1,0:T(8,128)(2,1)S(1)} %collective-permute-done.28.bottom, bf16[22,2,2,384]{3,2,1,0:T(2,128)(2,1)S(1)} %collective-permute-done.29.left, ...), custom_call_target="tpu_custom_call" | custom-call | tf_op jit(solution)/shard_map/pallas_call | solution.py:267
  (259 shorter events, 95.5 us)
Async XLA Ops:
  7.2 96.0 %all-gather.2.cloned.1.call-start = ((), (), s32[]{:S(2)}) async-start(), calls=%async_computation | async-start | bytes 5013504 | tf_op jit(solution)/shard_map/all_gather | solution.py:345
  8.2 12.4 %collective-permute-start.4 = (bf16[1,30,768]{2,1,0:T(8,128)(2,1)S(1)}, bf16[1,30,768]{2,1,0:T(8,128)(2,1)S(1)}, u32[]{:S(2)}, u32[]{:S(2)}) collective-permute-start(bf16[1,30,768]{2,1,0:T(8,128)(2,1)S(1)} %get-tuple-element.17), channel_id=1, source_target_pairs={{1,0},{2,1},{3,2},{4,3},{5,4},{6,5},{7,6},{0,7},{9,8},{10,9},{11,1... | collective-permute-start | bytes 138248 | tf_op jit(solution)/shard_map/ppermute | solution.py:48
  14.1 18.6 %collective-permute-start.10 = (bf16[1,30,768]{2,1,0:T(8,128)(2,1)S(1)}, bf16[1,30,768]{2,1,0:T(8,128)(2,1)S(1)}, u32[]{:S(2)}, u32[]{:S(2)}) collective-permute-start(bf16[1,30,768]{2,1,0:T(8,128)(2,1)S(1)} %get-tuple-element.17), channel_id=1, source_target_pairs={{7,0},{0,1},{1,2},{2,3},{3,4},{4,5},{5,6},{6,7},{15,8},{8,9},{9,10... | collective-permute-start | bytes 138248 | tf_op jit(solution)/shard_map/ppermute | solution.py:48
  14.1 18.6 %collective-permute-start.9 = (bf16[1,30,768]{2,1,0:T(8,128)(2,1)S(1)}, bf16[1,30,768]{2,1,0:T(8,128)(2,1)S(1)}, u32[]{:S(2)}, u32[]{:S(2)}) collective-permute-start(bf16[1,30,768]{2,1,0:T(8,128)(2,1)S(1)} %get-tuple-element.17), channel_id=1, source_target_pairs={{6,0},{7,1},{0,2},{1,3},{2,4},{3,5},{4,6},{5,7},{14,8},{15,9},{8,1... | collective-permute-start | bytes 138248 | tf_op jit(solution)/shard_map/ppermute | solution.py:48
  14.1 18.6 %collective-permute-start.8 = (bf16[1,30,768]{2,1,0:T(8,128)(2,1)S(1)}, bf16[1,30,768]{2,1,0:T(8,128)(2,1)S(1)}, u32[]{:S(2)}, u32[]{:S(2)}) collective-permute-start(bf16[1,30,768]{2,1,0:T(8,128)(2,1)S(1)} %get-tuple-element.17), channel_id=1, source_target_pairs={{5,0},{6,1},{7,2},{0,3},{1,4},{2,5},{3,6},{4,7},{13,8},{14,9},{15,... | collective-permute-start | bytes 138248 | tf_op jit(solution)/shard_map/ppermute | solution.py:48
  18.5 14.2 %collective-permute-start.7 = (bf16[1,30,768]{2,1,0:T(8,128)(2,1)S(1)}, bf16[1,30,768]{2,1,0:T(8,128)(2,1)S(1)}, u32[]{:S(2)}, u32[]{:S(2)}) collective-permute-start(bf16[1,30,768]{2,1,0:T(8,128)(2,1)S(1)} %get-tuple-element.17), channel_id=1, source_target_pairs={{4,0},{5,1},{6,2},{7,3},{0,4},{1,5},{2,6},{3,7},{12,8},{13,9},{14,... | collective-permute-start | bytes 138248 | tf_op jit(solution)/shard_map/ppermute | solution.py:48
  35.1 27.8 %collective-permute-start.1 = (bf16[3,32,384]{2,1,0:T(8,128)(2,1)}, bf16[3,32,384]{2,1,0:T(8,128)(2,1)S(1)}, u32[]{:S(2)}, u32[]{:S(2)}) collective-permute-start(bf16[3,32,384]{2,1,0:T(8,128)(2,1)} %get-tuple-element.34), channel_id=1, source_target_pairs={{8,0},{16,8},{24,16},{32,24},{40,32},{48,40},{56,48},{64,56},{72,6... | collective-permute-start | bytes 221192 | tf_op jit(solution)/shard_map/ppermute | solution.py:18
  40.0 35.7 %collective-permute-start = (bf16[3,32,384]{2,1,0:T(8,128)(2,1)}, bf16[3,32,384]{2,1,0:T(8,128)(2,1)S(1)}, u32[]{:S(2)}, u32[]{:S(2)}) collective-permute-start(bf16[3,32,384]{2,1,0:T(8,128)(2,1)} %get-tuple-element.35), channel_id=1, source_target_pairs={{0,8},{8,16},{16,24},{24,32},{32,40},{40,48},{48,56},{56,64},{64,7... | collective-permute-start | bytes 221192 | tf_op jit(solution)/shard_map/ppermute | solution.py:15
  46.3 11.9 %collective-permute-start.13 = (bf16[48,768]{1,0:T(8,128)(2,1)S(1)}, bf16[48,768]{1,0:T(8,128)(2,1)S(1)}, u32[]{:S(2)}, u32[]{:S(2)}) collective-permute-start(bf16[48,768]{1,0:T(8,128)(2,1)S(1)} %reshape.138), channel_id=1, source_target_pairs={{24,0},{0,8},{8,16},{16,24},{56,32},{32,40},{40,48},{48,56},{88,64... | collective-permute-start | bytes 221192 | tf_op jit(solution)/shard_map/ppermute | solution.py:48
  47.0 10.6 %collective-permute-start.12 = (bf16[48,768]{1,0:T(8,128)(2,1)S(1)}, bf16[48,768]{1,0:T(8,128)(2,1)S(1)}, u32[]{:S(2)}, u32[]{:S(2)}) collective-permute-start(bf16[48,768]{1,0:T(8,128)(2,1)S(1)} %reshape.138), channel_id=1, source_target_pairs={{16,0},{24,8},{0,16},{8,24},{48,32},{56,40},{32,48},{40,56},{80,64... | collective-permute-start | bytes 221192 | tf_op jit(solution)/shard_map/ppermute | solution.py:48
  58.8 9.4 %collective-permute-start.14 = (bf16[192,768]{1,0:T(8,128)(2,1)S(1)}, bf16[192,768]{1,0:T(8,128)(2,1)S(1)}, u32[]{:S(2)}, u32[]{:S(2)}) collective-permute-start(bf16[192,768]{1,0:T(8,128)(2,1)S(1)} %get-tuple-element.62), channel_id=1, source_target_pairs={{32,0},{40,8},{48,16},{56,24},{64,32},{72,40},{80,48},{88,56},{96,... | collective-permute-start | bytes 884744 | tf_op jit(solution)/shard_map/ppermute | solution.py:48
  59.0 16.0 %collective-permute-start.16 = (bf16[192,768]{1,0:T(8,128)(2,1)S(1)}, bf16[192,768]{1,0:T(8,128)(2,1)S(1)}, u32[]{:S(2)}, u32[]{:S(2)}) collective-permute-start(bf16[192,768]{1,0:T(8,128)(2,1)S(1)} %get-tuple-element.62), channel_id=1, source_target_pairs={{96,0},{104,8},{112,16},{120,24},{0,32},{8,40},{16,48},{24,56},{32... | collective-permute-start | bytes 884744 | tf_op jit(solution)/shard_map/ppermute | solution.py:48
  61.0 13.3 %collective-permute-start.15 = (bf16[192,768]{1,0:T(8,128)(2,1)S(1)}, bf16[192,768]{1,0:T(8,128)(2,1)S(1)}, u32[]{:S(2)}, u32[]{:S(2)}) collective-permute-start(bf16[192,768]{1,0:T(8,128)(2,1)S(1)} %get-tuple-element.62), channel_id=1, source_target_pairs={{64,0},{72,8},{80,16},{88,24},{96,32},{104,40},{112,48},{120,56},{... | collective-permute-start | bytes 884744 | tf_op jit(solution)/shard_map/ppermute | solution.py:48
  75.8 24.5 %collective-permute-start.17 = (bf16[768,768]{1,0:T(8,128)(2,1)}, bf16[768,768]{1,0:T(8,128)(2,1)}, u32[]{:S(2)}, u32[]{:S(2)}) collective-permute-start(bf16[768,768]{1,0:T(8,128)(2,1)} %constant_dynamic-update-slice_fusion.12), channel_id=1, source_target_pairs={{0,128},{128,0},{1,129},{129,1},{2,130},{130,2},{3,131},{131,3},{4... | collective-permute-start | bytes 3538952 | tf_op jit(solution)/shard_map/ppermute | solution.py:316
  75.8 7.3 %collective-permute-start.2 = (bf16[22,3,384]{2,1,0:T(4,128)(2,1)S(1)}, bf16[22,3,384]{2,1,0:T(4,128)(2,1)S(1)}, u32[]{:S(2)}, u32[]{:S(2)}) collective-permute-start(bf16[22,3,384]{2,1,0:T(4,128)(2,1)S(1)} %pad_maximum_fusion.6), channel_id=1, source_target_pairs={{0,1},{1,2},{2,3},{3,4},{4,5},{5,6},{6,7},{8,9},{9,10},{10,11},{11... | collective-permute-start | bytes 152072 | tf_op jit(solution)/shard_map/ppermute | solution.py:34
  103.2 36.2 %collective-permute-start.22 = (bf16[1536,1536]{1,0:T(8,128)(2,1)}, bf16[1536,1536]{1,0:T(8,128)(2,1)}, u32[]{:S(2)}, u32[]{:S(2)}) collective-permute-start(bf16[1536,1536]{1,0:T(8,128)(2,1)} %all-gather.2.cloned.1.call-done), channel_id=1, source_target_pairs={{0,128},{128,0},{1,129},{129,1},{2,130},{130,2},{3,131},{131,3},{4... | collective-permute-start | bytes 14155784 | tf_op jit(solution)/shard_map/ppermute | solution.py:316
  108.8 8.8 %collective-permute-start.18 = (bf16[3,16,768]{2,1,0:T(8,128)(2,1)S(1)}, bf16[3,16,768]{2,1,0:T(8,128)(2,1)S(1)}, u32[]{:S(2)}, u32[]{:S(2)}) collective-permute-start(bf16[3,16,768]{2,1,0:T(8,128)(2,1)S(1)} %bitcast.86), channel_id=1, source_target_pairs={{0,8},{8,16},{16,24},{24,32},{32,40},{40,48},{48,56},{56,64},{64,7... | collective-permute-start | bytes 221192 | tf_op jit(solution)/shard_map/ppermute | solution.py:15
  111.1 8.0 %collective-permute-start.19 = (bf16[3,16,768]{2,1,0:T(8,128)(2,1)S(1)}, bf16[3,16,768]{2,1,0:T(8,128)(2,1)S(1)}, u32[]{:S(2)}, u32[]{:S(2)}) collective-permute-start(bf16[3,16,768]{2,1,0:T(8,128)(2,1)S(1)} %bitcast.83), channel_id=1, source_target_pairs={{8,0},{16,8},{24,16},{32,24},{40,32},{48,40},{56,48},{64,56},{72,6... | collective-permute-start | bytes 221192 | tf_op jit(solution)/shard_map/ppermute | solution.py:18
  150.1 8.7 %collective-permute-start.23 = (bf16[3,16,768]{2,1,0:T(8,128)(2,1)S(1)}, bf16[3,16,768]{2,1,0:T(8,128)(2,1)S(1)}, u32[]{:S(2)}, u32[]{:S(2)}) collective-permute-start(bf16[3,16,768]{2,1,0:T(8,128)(2,1)S(1)} %bitcast.87), channel_id=1, source_target_pairs={{0,8},{8,16},{16,24},{24,32},{32,40},{40,48},{48,56},{56,64},{64,7... | collective-permute-start | bytes 221192 | tf_op jit(solution)/shard_map/ppermute | solution.py:15
  152.1 8.4 %collective-permute-start.24 = (bf16[3,16,768]{2,1,0:T(8,128)(2,1)S(1)}, bf16[3,16,768]{2,1,0:T(8,128)(2,1)S(1)}, u32[]{:S(2)}, u32[]{:S(2)}) collective-permute-start(bf16[3,16,768]{2,1,0:T(8,128)(2,1)S(1)} %bitcast.84), channel_id=1, source_target_pairs={{8,0},{16,8},{24,16},{32,24},{40,32},{48,40},{56,48},{64,56},{72,6... | collective-permute-start | bytes 221192 | tf_op jit(solution)/shard_map/ppermute | solution.py:18
  160.6 8.5 %collective-permute-start.25 = (bf16[14,3,768]{2,1,0:T(4,128)(2,1)S(1)}, bf16[14,3,768]{2,1,0:T(4,128)(2,1)S(1)}, u32[]{:S(2)}, u32[]{:S(2)}) collective-permute-start(bf16[14,3,768]{2,1,0:T(4,128)(2,1)S(1)} %pad_maximum_fusion.4), channel_id=1, source_target_pairs={{0,1},{1,2},{2,3},{3,4},{4,5},{5,6},{6,7},{8,9},{9,10},{10,11},{11... | collective-permute-start | bytes 193544 | tf_op jit(solution)/shard_map/ppermute | solution.py:34
  188.7 8.7 %collective-permute-start.27 = (bf16[3,2,16,384]{3,2,1,0:T(8,128)(2,1)S(1)}, bf16[3,2,16,384]{3,2,1,0:T(8,128)(2,1)S(1)}, u32[]{:S(2)}, u32[]{:S(2)}) collective-permute-start(bf16[3,2,16,384]{3,2,1,0:T(8,128)(2,1)S(1)} %bitcast.88), channel_id=1, source_target_pairs={{0,8},{8,16},{16,24},{24,32},{32,40},{40,48},{48,56},{56,64},{64,7... | collective-permute-start | bytes 221192 | tf_op jit(solution)/shard_map/ppermute | solution.py:15
  192.5 6.6 %collective-permute-start.28 = (bf16[3,2,16,384]{3,2,1,0:T(8,128)(2,1)S(1)}, bf16[3,2,16,384]{3,2,1,0:T(8,128)(2,1)S(1)}, u32[]{:S(2)}, u32[]{:S(2)}) collective-permute-start(bf16[3,2,16,384]{3,2,1,0:T(8,128)(2,1)S(1)} %bitcast.85), channel_id=1, source_target_pairs={{8,0},{16,8},{24,16},{32,24},{40,32},{48,40},{56,48},{64,56},{72,6... | collective-permute-start | bytes 221192 | tf_op jit(solution)/shard_map/ppermute | solution.py:18
  199.2 8.8 %collective-permute-start.29 = (bf16[22,2,2,384]{3,2,1,0:T(2,128)(2,1)S(1)}, bf16[22,2,2,384]{3,2,1,0:T(2,128)(2,1)S(1)}, u32[]{:S(2)}, u32[]{:S(2)}) collective-permute-start(bf16[22,2,2,384]{3,2,1,0:T(2,128)(2,1)S(1)} %pad_maximum_fusion.8), channel_id=1, source_target_pairs={{0,1},{1,2},{2,3},{3,4},{4,5},{5,6},{6,7},{8,9},{9,10},{10,11},{11... | collective-permute-start | bytes 202760 | tf_op jit(solution)/shard_map/ppermute | solution.py:34
  (64 other events, 605.5 us)
Sparse Core Ops, SparseCore 0:
  34.6 61.8 all-gather.1
where the time goes:
time: 224 us; the launch traced here: 220 us
  starting transfers between devices  81.2 us (36%)
  matrix products  40.7 us (18%)
  waiting for transfers between devices  34.8 us (16%)
  local copies, waits for them, and re-layouts  21.6 us (10%)
  between operations  15.1 us (7%)
  other arithmetic  14.9 us (7%)
  Pallas kernels  12.2 us (5%)
    ppermute x13, starting transfers between devices, ring_collect(): found.append(lax.ppermute(piece, axis, pairs))  29.2 us
    ppermute x4, starting transfers between devices, exchange(): lax.ppermute(lax.slice_in_dim(block, 0, width, axis=dim), axis, backward)  21.9 us
    ppermute x13, waiting for transfers between devices, ring_collect(): found.append(lax.ppermute(piece, axis, pairs))  20 us
    dot_general x4, matrix products, dense_backward(): jnp.dot(d_pre, part[:, :width], preferred_element_type=jnp.float32)  18.4 us
    ppermute x4, starting transfers between devices, halo_of(): left = lax.ppermute(edge(extent - width, extent), 'col', forward)  14.4 us
    unnamed x124, local copies, waits for them, and re-layouts  12.6 us
    pallas_call x4, Pallas kernels, tile_call(): pl.pallas_call(kernel, out_shape=outputs, in_specs=[whole] * len(operands...  12.2 us
    dot_general x5, matrix products, contract_last(): lax.dot_general(left_side, right_side, (((1,), (1,)), ((), ())), preferre...  11.9 us
  transfers between devices with their start and end apart: 32, of which 16 were waited for; matrix products, arithmetic and copies ran while one was open for 18% of the time, Pallas kernels for 3%

commit v1 on v0

--- a/solution.py
+++ b/solution.py
@@ -38,26 +38,26 @@
 
 def ring_collect(piece, axis, inner, stride):
     count = lax.axis_size(axis)
-    found = [piece]
+    own_place = (lax.axis_index(axis) // stride) % inner
+    found = jnp.zeros((inner, *piece.shape), piece.dtype)
+    found = lax.dynamic_update_index_in_dim(found, piece, own_place, 0)
     for shift in range(1, inner):
         pairs = []
         for target in range(count):
             place = (target // stride) % inner
             source = target + ((place + shift) % inner - place) * stride
             pairs.append((source, target))
-        found.append(lax.ppermute(piece, axis, pairs))
-    return jnp.concatenate(found, axis=0)
-
-
-def gelu_exact(values):
-    return 0.5 * values * (1.0 + lax.erf(values * 0.7071067811865476))
-
-
-def gelu_slope(values):
-    return (
-        0.5 * (1.0 + lax.erf(values * 0.7071067811865476))
-        + values * jnp.exp(-0.5 * values * values) * 0.3989422804014327
-    )
+        arrived = lax.ppermute(piece, axis, pairs)
+        found = lax.dynamic_update_index_in_dim(found, arrived, (own_place + shift) % inner, 0)
+    return found
+
+
+def normal_cdf(values):
+    return 0.5 * (1.0 + lax.erf(values * 0.7071067811865476))
+
+
+def slope_from(values, cdf):
+    return cdf + values * jnp.exp(-0.5 * values * values) * 0.3989422804014327
 
 
 def norm_forward(values, norm_gain, norm_shift):
@@ -78,28 +78,6 @@
     return lax.dot_general(
         left_side, right_side, (((1,), (1,)), ((), ())), preferred_element_type=jnp.float32
     )
-
-
-def dense_forward(normed, weights, up_bias, down_bias):
-    width = normed.shape[1]
-    pre_acts = []
-    branch = down_bias
-    for part, part_bias in zip(weights, up_bias):
-        pre_act = contract_last(normed, part[:, :width]) + part_bias
-        hidden = gelu_exact(pre_act).astype(jnp.bfloat16)
-        branch = branch + jnp.dot(hidden, part[:, width:], preferred_element_type=jnp.float32)
-        pre_acts.append(pre_act)
-    return (branch, pre_acts)
-
-
-def dense_backward(d_branch, pre_acts, weights):
-    width = d_branch.shape[1]
-    total = 0.0
-    for part, pre_act in zip(weights, pre_acts):
-        d_hidden = contract_last(d_branch, part[:, width:])
-        d_pre = (d_hidden * gelu_slope(pre_act)).astype(jnp.bfloat16)
-        total = total + jnp.dot(d_pre, part[:, :width], preferred_element_type=jnp.float32)
-    return total
 
 
 lanes = 128
@@ -261,17 +239,191 @@
     lax.fori_loop(0, channels // lanes, step, 0)
 
 
-def tile_call(kernel, outputs, rows, width, channels, operands, extra=()):
-    whole = pl.BlockSpec(memory_space=pltpu.VMEM)
-    frame = pltpu.VMEM((channels // lanes, rows + 6, width + 16, lanes), jnp.float32)
+def dot(left_side, right_side):
+    return jnp.dot(left_side, right_side, preferred_element_type=jnp.float32)
+
+
+def row_blocks(total, size):
+    size = min(total, size)
+    return [slice(first, first + size) for first in range(0, total, size)]
+
+
+def mlp_one_half(normed, weights, bias, branch):
+    width = normed.shape[1]
+
+    @pl.when(pl.program_id(0) == 0)
+    def _():
+        branch[...] = jnp.zeros_like(branch)
+
+    for rows in row_blocks(normed.shape[0], 256):
+        pre_act = contract_last(normed[rows, :], weights[:, :width]) + bias[...]
+        hidden = (pre_act * normal_cdf(pre_act)).astype(jnp.bfloat16)
+        branch[rows, :] += dot(hidden, weights[:, width:])
+
+
+def mlp_one_finish(
+    normed, weights, bias, partial, residual, down_bias, scale, gain, shift, merge, merge_bias,
+    section, merged, branch, patches,
+):
+    mlp_one_half(normed, weights, bias, branch)
+    positions, width = normed.shape
+    quarter = patches.shape[0]
+    half_cols = patches.shape[2]
+
+    @pl.when(pl.program_id(0) == pl.num_programs(0) - 1)
+    def _():
+        step_rows = 4 * half_cols
+
+        def step(index, carry):
+            rows = pl.ds(pl.multiple_of(index * step_rows, step_rows), step_rows)
+            total = branch[rows, :] + partial[rows, :] + down_bias[...]
+            out = (residual[rows, :].astype(jnp.float32) + scale[...] * total).astype(jnp.bfloat16)
+            section[rows, :] = out
+            normal = norm_forward(out.astype(jnp.float32), gain[...], shift[...])[2]
+            normal = normal.astype(jnp.bfloat16)
+            for place in range(4):
+                patches[index, place] = normal[place * half_cols : (place + 1) * half_cols, :]
+            return carry
+
+        lax.fori_loop(0, quarter, step, 0)
+        total = merge_bias[...]
+        for place in range(4):
+            patch = patches[:, place].reshape(quarter * half_cols, width)
+            total = total + dot(patch, merge[place * width : (place + 1) * width, :])
+        merged[...] = total.astype(merged.dtype)
+
+
+def slope_one_kernel(normed, own, other, bias_own, bias_other, slope_own, slope_other):
+    width = normed.shape[1]
+    for rows in row_blocks(normed.shape[0], 256):
+        for weights, bias, slope in (
+            (own, bias_own, slope_own),
+            (other, bias_other, slope_other),
+        ):
+            pre_act = contract_last(normed[rows, :], weights[:, :width]) + bias[...]
+            slope[rows, :] = slope_from(pre_act, normal_cdf(pre_act)).astype(slope.dtype)
+
+
+def back_mlp_one(
+    d_merged, merge, section, gain_mid, scale, own, other, slope_own, slope_other, conv, gain,
+    d_conv, upstream, d_branch, d_normed,
+):
+    width = section.shape[1]
+    quarter = d_merged.shape[0]
+    half_cols = 16
+    groups = quarter // half_cols
+
+    @pl.when(pl.program_id(0) == 0)
+    def _():
+        d_normed[...] = jnp.zeros_like(d_normed)
+        for place in range(4):
+            d_normal = contract_last(d_merged[...], merge[place * width : (place + 1) * width, :])
+            for group in range(groups):
+                first = (4 * group + place) * half_cols
+                rows = slice(first, first + half_cols)
+                values = section[rows, :].astype(jnp.float32)
+                scaled, inv_std, _ = norm_forward(values, 1.0, 0.0)
+                flow = norm_backward(
+                    d_normal[group * half_cols : (group + 1) * half_cols],
+                    scaled,
+                    inv_std,
+                    gain_mid[...],
+                )
+                upstream[rows, :] = flow
+                d_branch[rows, :] = (flow * scale[...]).astype(d_branch.dtype)
+
+    for rows in row_blocks(section.shape[0], 256):
+        total = d_normed[rows, :]
+        for weights, slope in ((own, slope_own), (other, slope_other)):
+            d_hidden = contract_last(d_branch[rows, :], weights[:, width:])
+            d_pre = (d_hidden * slope[rows, :].astype(jnp.float32)).astype(jnp.bfloat16)
+            total = total + dot(d_pre, weights[:, :width])
+        d_normed[rows, :] = total
+
+    @pl.when(pl.program_id(0) == pl.num_programs(0) - 1)
+    def _():
+        norm_back_rows(conv, d_normed, gain, d_conv, 64)
+
+
+def norm_back_rows(conv, d_normed, gain, d_conv, chunk):
+    def step(index, carry):
+        rows = pl.ds(pl.multiple_of(index * chunk, chunk), chunk)
+        scaled, inv_std, _ = norm_forward(conv[rows, :].astype(jnp.float32), 1.0, 0.0)
+        flow = norm_backward(d_normed[rows, :], scaled, inv_std, gain[...])
+        d_conv[rows, :] = flow.astype(d_conv.dtype)
+        return carry
+
+    lax.fori_loop(0, conv.shape[0] // chunk, step, 0)
+
+
+def mlp_two_half(normed, grad, scale, weights, bias, branch, d_normed, d_branch):
+    width = normed.shape[1]
+
+    @pl.when(pl.program_id(0) == 0)
+    def _():
+        branch[...] = jnp.zeros_like(branch)
+        d_normed[...] = jnp.zeros_like(d_normed)
+        d_branch[...] = (grad[...].astype(jnp.float32) * scale[...]).astype(d_branch.dtype)
+
+    up = weights[:, :width]
+    down = weights[:, width:]
+    pre_act = contract_last(normed[...], up) + bias[...]
+    d_hidden = contract_last(d_branch[...], down)
+    cdf = normal_cdf(pre_act)
+    hidden = (pre_act * cdf).astype(jnp.bfloat16)
+    d_pre = (d_hidden * slope_from(pre_act, cdf)).astype(jnp.bfloat16)
+    branch[...] += dot(hidden, down)
+    d_normed[...] += dot(d_pre, up)
+
+
+def mlp_two_finish(
+    normed, grad, scale, weights, bias, partial, d_partial, merged, down_bias, conv, gain,
+    features, d_conv, branch, d_normed, d_branch,
+):
+    mlp_two_half(normed, grad, scale, weights, bias, branch, d_normed, d_branch)
+
+    @pl.when(pl.program_id(0) == pl.num_programs(0) - 1)
+    def _():
+        total = branch[...] + partial[...] + down_bias[...]
+        out = merged[...].astype(jnp.float32) + scale[...] * total
+        features[...] = out.astype(features.dtype)
+        d_normed[...] += d_partial[...]
+        norm_back_rows(conv, d_normed, gain, d_conv, 64)
+
+
+megabyte = 1024 * 1024
+
+
+def shape_of(dims, dtype):
+    return jax.ShapeDtypeStruct(dims, dtype)
+
+
+def block_call(kernel, outputs, operands, scratch, steps=1, split=(), limit=40):
+    def spec_of(array, key):
+        dims = list(array.shape)
+        axis = dict(split).get(key)
+        if axis is not None:
+            dims[axis] //= steps
+
+        def index_map(step):
+            return tuple(step if place == axis else 0 for place in range(len(dims)))
+
+        return pl.BlockSpec(tuple(dims), index_map)
+
     return pl.pallas_call(
         kernel,
+        grid=(steps,),
         out_shape=outputs,
-        in_specs=[whole] * len(operands),
-        out_specs=jax.tree.map(lambda _: whole, outputs),
-        scratch_shapes=[frame, *extra],
-        compiler_params=pltpu.CompilerParams(vmem_limit_bytes=32 * 1024 * 1024),
+        in_specs=[spec_of(array, index) for index, array in enumerate(operands)],
+        out_specs=[spec_of(array, "out%d" % index) for index, array in enumerate(outputs)],
+        scratch_shapes=scratch,
+        compiler_params=pltpu.CompilerParams(vmem_limit_bytes=limit * megabyte),
     )(*operands)
+
+
+def tile_call(kernel, outputs, rows, width, channels, operands, extra=()):
+    frame = pltpu.VMEM((channels // lanes, rows + 6, width + 16, lanes), jnp.float32)
+    return block_call(kernel, outputs, operands, [frame, *extra])
 
 
 def on_device(
@@ -311,29 +463,19 @@
     col_count = lax.axis_size("col")
     inner = 4 if row_count % 4 == 0 else row_count
     outer = row_count // inner
-
-    def both_halves(own):
-        return (own, lax.ppermute(own, "sec", swap))
-
-    def rolled(bias, roll_rows):
-        grid = bias.reshape(2, outer, inner, col_count, -1)
-        grid = jnp.concatenate([grid, grid], axis=3)
-        row_index = lax.axis_index("row")
-        start = (0, 0)
-        if roll_rows:
-            grid = jnp.concatenate([grid, grid], axis=1)
-            grid = jnp.concatenate([grid, grid], axis=2)
-            start = (row_index // inner, row_index % inner)
-        sizes = (1, outer, inner, col_count, grid.shape[4])
-        tail = (*start, lax.axis_index("col"), 0)
-        return tuple(
-            lax.dynamic_slice(grid, (half, *tail), sizes).reshape(-1) for half in (side, 1 - side)
+    bfloat = jnp.bfloat16
+
+    def bias_halves(bias):
+        halves = bias.reshape(2, 1, -1)
+        return (
+            jnp.where(side == 0, halves[0], halves[1]),
+            jnp.where(side == 0, halves[1], halves[0]),
         )
 
     share_two = up_two.shape[1]
     packed_one = jnp.concatenate([up_one.T, down_one.T], axis=1)
     packed = jnp.concatenate([up_two.T, down_two.T, packed_one], axis=0)
-    column = ring_collect(packed[None], "col", col_count, 1)
+    column = ring_collect(packed, "col", col_count, 1)
     part_one = column[:, 2 * share_two :].reshape(-1, 2 * width_one)
     part_two = jnp.concatenate(
         [
@@ -343,95 +485,162 @@
         axis=1,
     )
     own_two = lax.all_gather(part_two, "row", axis=0, tiled=True)
-    own_one = ring_collect(ring_collect(part_one, "row", inner, 1), "row", outer, inner)
-    pair_one = both_halves(own_one)
-    pair_two = both_halves(own_two)
-    bias_one = rolled(up_bias_one, True)
-    bias_two = rolled(up_bias_two, False)
+    own_one = ring_collect(part_one, "row", inner, 1).reshape(-1, 2 * width_one)
+    own_one = ring_collect(own_one, "row", outer, inner).reshape(-1, 2 * width_one)
+    bias_one = bias_halves(up_bias_one)
+    bias_two = bias_halves(up_bias_two)
 
     image_tile = images.reshape(tile_rows, tile_cols, width_one)
     normed_one, conv_one, images_par = tile_call(
         conv_one_kernel,
         (
-            jax.ShapeDtypeStruct((rows_one, width_one), jnp.bfloat16),
-            jax.ShapeDtypeStruct((rows_one, width_one), jnp.float32),
-            jax.ShapeDtypeStruct((rows_one, width_one), jnp.bfloat16),
+            shape_of((rows_one, width_one), bfloat),
+            shape_of((rows_one, width_one), jnp.float32),
+            shape_of((rows_one, width_one), bfloat),
         ),
         tile_rows,
         tile_cols,
         width_one,
         (image_tile, *halo_of(image_tile, 3), kernel_one, gain_one[None], shift_one[None]),
     )
-    scaled_one, inv_one, _ = norm_forward(conv_one, gain_one, shift_one)
-    branch_one, pre_one = dense_forward(normed_one, pair_one, bias_one, down_bias_one)
-    section_out = (
-        images_par.astype(jnp.float32) + scale_one * branch_one
-    ).astype(jnp.bfloat16)
-    scaled_mid, inv_mid, normed_mid = norm_forward(
-        section_out.astype(jnp.float32), gain_mid, shift_mid
-    )
-    patches = normed_mid.astype(jnp.bfloat16).reshape(
-        micro_count * half_rows, 4, half_cols, width_one
-    )
-    patches = jnp.concatenate(
-        [patches[:, place].reshape(rows_two, width_one) for place in range(4)], axis=1
-    )
-    merged = (
-        jnp.dot(patches, merge_weight, preferred_element_type=jnp.float32) + merge_bias
-    ).astype(jnp.bfloat16)
+    own_one, normed_one, images_par, bias_one, bias_two = lax.optimization_barrier(
+        (own_one, normed_one, images_par, bias_one, bias_two)
+    )
+    other_one = lax.ppermute(own_one, "sec", swap)
+    other_two = lax.ppermute(own_two, "sec", swap)
+    steps_one = max(1, own_one.shape[0] // 256)
+    steps_two = max(1, own_two.shape[0] // 256)
+
+    (partial_one,) = block_call(
+        mlp_one_half,
+        (shape_of((rows_one, width_one), jnp.float32),),
+        (normed_one, own_one, bias_one[0]),
+        [],
+        steps_one,
+        ((1, 0), (2, 1)),
+    )
+    section_out, merged = block_call(
+        mlp_one_finish,
+        (shape_of((rows_one, width_one), bfloat), shape_of((rows_two, width_two), bfloat)),
+        (
+            normed_one,
+            other_one,
+            bias_one[1],
+            partial_one,
+            images_par,
+            down_bias_one[None],
+            scale_one[None],
+            gain_mid[None],
+            shift_mid[None],
+            merge_weight,
+            merge_bias[None],
+        ),
+        [
+            pltpu.VMEM((rows_one, width_one), jnp.float32),
+            pltpu.VMEM((micro_count * half_rows, 4, half_cols, width_one), bfloat),
+        ],
+        steps_one,
+        ((1, 0), (2, 1)),
+    )
+    slope_own, slope_other = block_call(
+        slope_one_kernel,
+        (
+            shape_of((rows_one, own_one.shape[0]), bfloat),
+            shape_of((rows_one, own_one.shape[0]), bfloat),
+        ),
+        (normed_one, own_one, other_one, *bias_one),
+        [],
+        steps_one,
+        ((1, 0), (2, 0), (3, 1), (4, 1), ("out0", 1), ("out1", 1)),
+    )
+
     merged_tile = merged.reshape(half_rows, half_cols, width_two)
     normed_two, conv_two = tile_call(
         conv_two_kernel,
-        (
-            jax.ShapeDtypeStruct((rows_two, width_two), jnp.bfloat16),
-            jax.ShapeDtypeStruct((rows_two, width_two), jnp.bfloat16),
-        ),
+        (shape_of((rows_two, width_two), bfloat), shape_of((rows_two, width_two), bfloat)),
         half_rows,
         half_cols,
         width_two,
         (merged_tile, *halo_of(merged_tile, 3), kernel_two, gain_two[None], shift_two[None]),
     )
-    scaled_two, inv_two, _ = norm_forward(conv_two.astype(jnp.float32), gain_two, shift_two)
-    branch_two, pre_two = dense_forward(normed_two, pair_two, bias_two, down_bias_two)
-    features = (merged.astype(jnp.float32) + scale_two * branch_two).astype(jnp.bfloat16)
     grad_rows = grad_out.reshape(rows_two, width_two)
-    d_branch_two = (grad_rows.astype(jnp.float32) * scale_two).astype(jnp.bfloat16)
-    d_normed_two = dense_backward(d_branch_two, pre_two, pair_two)
-    d_conv_two = norm_backward(d_normed_two, scaled_two, inv_two, gain_two).astype(jnp.bfloat16)
+    two_wide = shape_of((rows_two, width_two), jnp.float32)
+    two_scratch = pltpu.VMEM((rows_two, width_two), jnp.float32)
+    two_branch = pltpu.VMEM((rows_two, width_two), bfloat)
+    partial_two, d_partial_two = block_call(
+        mlp_two_half,
+        (two_wide, two_wide),
+        (normed_two, grad_rows, scale_two[None], own_two, bias_two[0]),
+        [two_branch],
+        steps_two,
+        ((3, 0), (4, 1)),
+    )
+    features, d_conv_two = block_call(
+        mlp_two_finish,
+        (shape_of((rows_two, width_two), bfloat), shape_of((rows_two, width_two), bfloat)),
+        (
+            normed_two,
+            grad_rows,
+            scale_two[None],
+            other_two,
+            bias_two[1],
+            partial_two,
+            d_partial_two,
+            merged,
+            down_bias_two[None],
+            conv_two,
+            gain_two[None],
+        ),
+        [two_scratch, two_scratch, two_branch],
+        steps_two,
+        ((3, 0), (4, 1)),
+    )
     back_tile = d_conv_two.reshape(half_rows, half_cols, width_two)
-    d_merged = tile_call(
+    (d_merged,) = tile_call(
         back_two_kernel,
-        jax.ShapeDtypeStruct((rows_two, width_two), jnp.bfloat16),
+        (shape_of((rows_two, width_two), bfloat),),
         half_rows,
         half_cols,
         width_two,
         (back_tile, *halo_of(back_tile, 3), kernel_two, grad_rows),
     )
-    d_patches = contract_last(d_merged, merge_weight)
-    d_normed_mid = jnp.stack(
+    d_conv_one, upstream_one = block_call(
+        back_mlp_one,
+        (shape_of((rows_one, width_one), bfloat), shape_of((rows_one, width_one), jnp.float32)),
+        (
+            d_merged,
+            merge_weight,
+            section_out,
+            gain_mid[None],
+            scale_one[None],
+            own_one,
+            other_one,
+            slope_own,
+            slope_other,
+            conv_one,
+            gain_one[None],
+        ),
         [
-            d_patches[:, place * width_one : (place + 1) * width_one].reshape(
-                micro_count * half_rows, half_cols, width_one
-            )
-            for place in range(4)
+            pltpu.VMEM((rows_one, width_one), bfloat),
+            pltpu.VMEM((rows_one, width_one), jnp.float32),
         ],
-        axis=1,
-    ).reshape(rows_one, width_one)
-    upstream_one = norm_backward(d_normed_mid, scaled_mid, inv_mid, gain_mid)
-    d_branch_one = (upstream_one * scale_one).astype(jnp.bfloat16)
-    d_normed_one = dense_backward(d_branch_one, pre_one, pair_one)
-    d_conv_one = norm_backward(d_normed_one, scaled_one, inv_one, gain_one).astype(jnp.bfloat16)
+        steps_one,
+        ((5, 0), (6, 0), (7, 1), (8, 1)),
+    )
     d_conv_one = d_conv_one.reshape(tile_rows, 2, half_cols, width_one)
-    input_grad = tile_call(
+    (input_grad,) = tile_call(
         back_one_kernel,
-        jax.ShapeDtypeStruct((tile_rows, tile_cols, width_one), jnp.bfloat16),
+        (shape_of((tile_rows, tile_cols, width_one), bfloat),),
         tile_rows,
         tile_cols,
         width_one,
         (d_conv_one, *halo_of(d_conv_one, 2), kernel_one, upstream_one),
         (pltpu.VMEM((tile_rows, tile_cols, lanes), jnp.float32),),
-    ).reshape(images.shape)
-    return (features.reshape(micro_count, half_rows, half_cols, width_two), input_grad)
+    )
+    return (
+        features.reshape(micro_count, half_rows, half_cols, width_two),
+        input_grad.reshape(images.shape),
+    )
 
 
 def solution(mesh):

time: 224 us -> 229 us (1.022)
  waiting for transfers between devices: 34.8 us -> 87.4 us
  matrix products: 40.7 us -> 0 us
  Pallas kernels: 12.2 us -> 40.5 us
  local copies, waits for them, and re-layouts: 21.6 us -> 1.13 us
  other arithmetic: 14.9 us -> 2.13 us
    all_gather x1, waiting for transfers between devices: 0.01 us -> 50.3 us  [on_device(): own_two = lax.all_gather(part_two, 'row', axis=0, tiled=True)]
    dot_general x14 -> x0, matrix products: 40.7 us -> none  [the longest x4 18.4 us: dense_backward(): jnp.dot(d_pre, part[:, :width], preferred_element_type=jnp.float32)]
    pallas_call x4 -> x10, Pallas kernels: 12.2 us -> 40.5 us  [block_call(): pl.pallas_call(kernel, grid=(steps,), out_shape=outputs, in_specs=[spec_o...]
    unnamed x124 -> x38, local copies, waits for them, and re-layouts: 12.6 us -> 0.14 us
    ppermute x4, waiting for transfers between devices: 8.82 us -> 14.4 us  [halo_of(): right = lax.ppermute(edge(0, width), 'col', backward)]
    reduce_sum x7 -> x0, other arithmetic: 4.12 us -> none  [the longest x1 1.63 us: norm_backward(): mean_two = jnp.mean(weighted * scaled, axis=-1, keepdims=True)]
    ppermute x15, waiting for transfers between devices: 20 us -> 15.9 us  [the longest x13 15.9 us: ring_collect(): arrived = lax.ppermute(piece, axis, pairs)]
    ppermute x15, starting transfers between devices: 29.3 us -> 25.4 us  [the longest x13 25.3 us: ring_collect(): arrived = lax.ppermute(piece, axis, pairs)]
  transfers between devices with their start and end apart: 32 -> 32, of which waited for: 16 -> 16; matrix products, arithmetic and copies ran while one was open for 18% -> 1% of each run, Pallas kernels for 3% -> 9%
where the time goes in v1:
time: 229 us; the launch traced here: 227 us
  waiting for transfers between devices  87.4 us (38%)
  starting transfers between devices  80.1 us (35%)
  Pallas kernels  40.5 us (18%)
  between operations  15.2 us (7%)
    all_gather x1, waiting for transfers between devices, on_device(): own_two = lax.all_gather(part_two, 'row', axis=0, tiled=True)  50.3 us
    pallas_call x10, Pallas kernels, block_call(): pl.pallas_call(kernel, grid=(steps,), out_shape=outputs, in_specs=[spec_o...  40.5 us
    ppermute x13, starting transfers between devices, ring_collect(): arrived = lax.ppermute(piece, axis, pairs)  25.3 us
    ppermute x4, starting transfers between devices, exchange(): lax.ppermute(lax.slice_in_dim(block, 0, width, axis=dim), axis, backward)  21.6 us
    ppermute x4, starting transfers between devices, halo_of(): left = lax.ppermute(edge(extent - width, extent), 'col', forward)  16.9 us
    ppermute x13, waiting for transfers between devices, ring_collect(): arrived = lax.ppermute(piece, axis, pairs)  15.9 us
    ppermute x4, waiting for transfers between devices, halo_of(): right = lax.ppermute(edge(0, width), 'col', backward)  14.4 us
    ppermute x4, starting transfers between devices, exchange(): lax.ppermute(lax.slice_in_dim(block, block.shape[dim] - width, None, axis...  11.1 us
  transfers between devices with their start and end apart: 32, of which 16 were waited for; matrix products, arithmetic and copies ran while one was open for 1% of the time, Pallas kernels for 9%

profile of v1, /device:TPU:2, one launch (start us, length us, event | category | flops | bytes accessed | tf_op | source)
XLA Modules:
  0.0 226.5 jit_solution(13624626595939855298)
XLA Ops:
  8.1 5.9 %collective-permute-start = (bf16[30,768]{1,0:T(8,128)(2,1)S(1)}, bf16[30,768]{1,0:T(8,128)(2,1)S(1)}, u32[]{:S(2)}, u32[]{:S(2)}) collective-permute-start(bf16[30,768]{1,0:T(8,128)(2,1)S(1)} %get-tuple-element.47), channel_id=1, source_target_pairs={{1,0},{2,1},{3,2},{4,3},{5,4},{6,5},{7,6},{0,7},{9,8},{10,9},{11,1... | collective-permute-start | bytes 138248 | tf_op jit(solution)/shard_map/ppermute | solution.py:50
  15.9 5.0 %collective-permute-start.3 = (bf16[30,768]{1,0:T(8,128)(2,1)S(1)}, bf16[30,768]{1,0:T(8,128)(2,1)S(1)}, u32[]{:S(2)}, u32[]{:S(2)}) collective-permute-start(bf16[30,768]{1,0:T(8,128)(2,1)S(1)} %get-tuple-element.47), channel_id=1, source_target_pairs={{4,0},{5,1},{6,2},{7,3},{0,4},{1,5},{2,6},{3,7},{12,8},{13,9},{14,... | collective-permute-start | bytes 138248 | tf_op jit(solution)/shard_map/ppermute | solution.py:50
  25.5 3.7 %collective-permute-done.4 = bf16[30,768]{1,0:T(8,128)(2,1)S(1)} collective-permute-done((bf16[30,768]{1,0:T(8,128)(2,1)S(1)}, bf16[30,768]{1,0:T(8,128)(2,1)S(1)}, u32[]{:S(2)}, u32[]{:S(2)}) %collective-permute-start.4) | collective-permute-done | bytes 46112 | tf_op jit(solution)/shard_map/ppermute | solution.py:50
  31.8 3.5 %collective-permute-start.13 = (bf16[3,32,384]{2,1,0:T(8,128)(2,1)S(1)}, bf16[3,32,384]{2,1,0:T(8,128)(2,1)S(1)}, u32[]{:S(2)}, u32[]{:S(2)}) collective-permute-start(bf16[3,32,384]{2,1,0:T(8,128)(2,1)S(1)} %get-tuple-element.57), channel_id=1, source_target_pairs={{0,8},{8,16},{16,24},{24,32},{32,40},{40,48},{48,56},{56,64},{64,7... | collective-permute-start | bytes 221192 | tf_op jit(solution)/shard_map/ppermute | solution.py:15
  35.3 4.5 %collective-permute-start.14 = (bf16[3,32,384]{2,1,0:T(8,128)(2,1)S(1)}, bf16[3,32,384]{2,1,0:T(8,128)(2,1)S(1)}, u32[]{:S(2)}, u32[]{:S(2)}) collective-permute-start(bf16[3,32,384]{2,1,0:T(8,128)(2,1)S(1)} %get-tuple-element.56), channel_id=1, source_target_pairs={{8,0},{16,8},{24,16},{32,24},{40,32},{48,40},{56,48},{64,56},{72,6... | collective-permute-start | bytes 221192 | tf_op jit(solution)/shard_map/ppermute | solution.py:18
  39.8 50.3 %all-gather.2.cloned.1.call-done.weights = bf16[1536,1536]{1,0:T(8,128)(2,1)} async-done(((bf16[96,1536]{1,0:T(8,128)(2,1)}), bf16[1536,1536]{1,0:T(8,128)(2,1)}) %all-gather.2.cloned.1.call-update) | async-done | bytes 4718608 | tf_op jit(solution)/shard_map/all_gather | solution.py:487
  101.3 3.5 %collective-permute-start.15 = (bf16[22,3,384]{2,1,0:T(4,128)(2,1)S(1)}, bf16[22,3,384]{2,1,0:T(4,128)(2,1)S(1)}, u32[]{:S(2)}, u32[]{:S(2)}) collective-permute-start(bf16[22,3,384]{2,1,0:T(4,128)(2,1)S(1)} %pad_maximum_fusion.5), channel_id=1, source_target_pairs={{0,1},{1,2},{2,3},{3,4},{4,5},{5,6},{6,7},{8,9},{9,10},{10,11},{11... | collective-permute-start | bytes 152072 | tf_op jit(solution)/shard_map/ppermute | solution.py:34
  111.0 4.6 %shard_map.221 = (bf16[512,384]{1,0:T(8,128)(2,1)S(1)}, f32[512,384]{1,0:T(8,128)S(1)}, bf16[512,384]{1,0:T(8,128)(2,1)S(1)}) custom-call(bf16[16,32,384]{2,1,0:T(8,128)(2,1)S(1)} %bitcast.64, bf16[3,32,384]{2,1,0:T(8,128)(2,1)S(1)} %collective-permute-done.13.top, bf16[3,32,384]{2,1,0:T(8,128)(2,1)S(1)} %collective-permute-done.14.bottom, ...), custom_call_target="tpu_custom_call" | custom-call | tf_op jit(solution)/shard_map/pallas_call | solution.py:413
  115.8 5.2 %collective-permute-done.12 = bf16[192,768]{1,0:T(8,128)(2,1)S(1)} collective-permute-done((bf16[192,768]{1,0:T(8,128)(2,1)S(1)}, bf16[192,768]{1,0:T(8,128)(2,1)S(1)}, u32[]{:S(2)}, u32[]{:S(2)}) %collective-permute-start.12) | collective-permute-done | bytes 294944 | tf_op jit(solution)/shard_map/ppermute | solution.py:50
  123.9 4.8 %shard_map.223 = (bf16[512,384]{1,0:T(8,128)(2,1)S(1)}, bf16[128,768]{1,0:T(8,128)(2,1)S(1)}) custom-call(bf16[512,384]{1,0:T(8,128)(2,1)S(1)} %get-tuple-element.26.normed, bf16[768,768]{1,0:T(8,128)(2,1)S(1)} %collective-permute-done.17.weights.other, f32[1,768]{1,0:T(1,128)S(1)} %select_n.197.bias.bias_other, f32[512,384]{1,0:T(8,128)S(1)} %shard_map.222.partial, ...), custom_call_target="tpu_custom_call" | custom-call | tf_op jit(solution)/shard_map/pallas_call | solution.py:413
  130.8 6.0 %collective-permute-start.19 = (bf16[3,16,768]{2,1,0:T(8,128)(2,1)S(1)}, bf16[3,16,768]{2,1,0:T(8,128)(2,1)S(1)}, u32[]{:S(2)}, u32[]{:S(2)}) collective-permute-start(bf16[3,16,768]{2,1,0:T(8,128)(2,1)S(1)} %bitcast.77), channel_id=1, source_target_pairs={{8,0},{16,8},{24,16},{32,24},{40,32},{48,40},{56,48},{64,56},{72,6... | collective-permute-start | bytes 221192 | tf_op jit(solution)/shard_map/ppermute | solution.py:18
  138.9 4.3 %collective-permute-start.20 = (bf16[14,3,768]{2,1,0:T(4,128)(2,1)S(1)}, bf16[14,3,768]{2,1,0:T(4,128)(2,1)S(1)}, u32[]{:S(2)}, u32[]{:S(2)}) collective-permute-start(bf16[14,3,768]{2,1,0:T(4,128)(2,1)S(1)} %pad_maximum_fusion.1), channel_id=1, source_target_pairs={{0,1},{1,2},{2,3},{3,4},{4,5},{5,6},{6,7},{8,9},{9,10},{10,11},{11... | collective-permute-start | bytes 193544 | tf_op jit(solution)/shard_map/ppermute | solution.py:34
  145.3 4.4 %collective-permute-done.21.right = bf16[14,3,768]{2,1,0:T(4,128)(2,1)S(1)} collective-permute-done((bf16[14,3,768]{2,1,0:T(4,128)(2,1)S(1)}, bf16[14,3,768]{2,1,0:T(4,128)(2,1)S(1)}, u32[]{:S(2)}, u32[]{:S(2)}) %collective-permute-start.21) | collective-permute-done | bytes 64544 | tf_op jit(solution)/shard_map/ppermute | solution.py:35
  152.0 3.9 %shard_map.225 = (f32[128,768]{1,0:T(8,128)S(1)}, f32[128,768]{1,0:T(8,128)S(1)}) custom-call(bf16[128,768]{1,0:T(8,128)(2,1)S(1)} %get-tuple-element.32.normed, bf16[128,768]{1,0:T(8,128)(2,1)S(1)} %bitcast.60, f32[1,768]{1,0:T(1,128)S(1)} %broadcast_in_dim.126.scale, bf16[1536,1536]{1,0:T(8,128)(2,1)S(1)} %copy-done.1, f32[1,1536]{1,0:T(1,128)S(1)} %select_n.200.bias), custom_call_target="tpu_custom_call" | custom-call | tf_op jit(solution)/shard_map/pallas_call | solution.py:413
  155.9 7.5 %shard_map.226 = (bf16[128,768]{1,0:T(8,128)(2,1)}, bf16[128,768]{1,0:T(8,128)(2,1)S(1)}) custom-call(bf16[128,768]{1,0:T(8,128)(2,1)S(1)} %get-tuple-element.32.normed, bf16[128,768]{1,0:T(8,128)(2,1)S(1)} %bitcast.61, f32[1,768]{1,0:T(1,128)S(1)} %broadcast_in_dim.126.scale, bf16[1536,1536]{1,0:T(8,128)(2,1)} %collective-permute-done.22.weights, ...), custom_call_target="tpu_custom_call" | custom-call | tf_op jit(solution)/shard_map/pallas_call | solution.py:413
  165.4 6.4 %collective-permute-start.24 = (bf16[3,16,768]{2,1,0:T(8,128)(2,1)S(1)}, bf16[3,16,768]{2,1,0:T(8,128)(2,1)S(1)}, u32[]{:S(2)}, u32[]{:S(2)}) collective-permute-start(bf16[3,16,768]{2,1,0:T(8,128)(2,1)S(1)} %bitcast.78), channel_id=1, source_target_pairs={{8,0},{16,8},{24,16},{32,24},{40,32},{48,40},{56,48},{64,56},{72,6... | collective-permute-start | bytes 221192 | tf_op jit(solution)/shard_map/ppermute | solution.py:18
  173.9 4.0 %collective-permute-start.25 = (bf16[14,3,768]{2,1,0:T(4,128)(2,1)S(1)}, bf16[14,3,768]{2,1,0:T(4,128)(2,1)S(1)}, u32[]{:S(2)}, u32[]{:S(2)}) collective-permute-start(bf16[14,3,768]{2,1,0:T(4,128)(2,1)S(1)} %pad_maximum_fusion.3), channel_id=1, source_target_pairs={{0,1},{1,2},{2,3},{3,4},{4,5},{5,6},{6,7},{8,9},{9,10},{10,11},{11... | collective-permute-start | bytes 193544 | tf_op jit(solution)/shard_map/ppermute | solution.py:34
  181.5 3.7 %collective-permute-done.26.right = bf16[14,3,768]{2,1,0:T(4,128)(2,1)S(1)} collective-permute-done((bf16[14,3,768]{2,1,0:T(4,128)(2,1)S(1)}, bf16[14,3,768]{2,1,0:T(4,128)(2,1)S(1)}, u32[]{:S(2)}, u32[]{:S(2)}) %collective-permute-start.26) | collective-permute-done | bytes 64544 | tf_op jit(solution)/shard_map/ppermute | solution.py:35
  187.0 7.3 %shard_map.229 = (bf16[512,384]{1,0:T(8,128)(2,1)S(1)}, f32[512,384]{1,0:T(8,128)S(1)}) custom-call(bf16[128,768]{1,0:T(8,128)(2,1)S(1)} %shard_map.227.d_merged, bf16[1536,768]{1,0:T(8,128)(2,1)S(1)} %copy-done, bf16[512,384]{1,0:T(8,128)(2,1)S(1)} %get-tuple-element.40.section, f32[1,384]{1,0:T(1,128)S(1)} %broadcast_in_dim.121.gain.gain_mid, ...), custom_call_target="tpu_custom_call" | custom-call | tf_op jit(solution)/shard_map/pallas_call | solution.py:413
  194.3 3.6 %collective-permute-start.27 = (bf16[3,2,16,384]{3,2,1,0:T(8,128)(2,1)S(1)}, bf16[3,2,16,384]{3,2,1,0:T(8,128)(2,1)S(1)}, u32[]{:S(2)}, u32[]{:S(2)}) collective-permute-start(bf16[3,2,16,384]{3,2,1,0:T(8,128)(2,1)S(1)} %bitcast.76), channel_id=1, source_target_pairs={{0,8},{8,16},{16,24},{24,32},{32,40},{40,48},{48,56},{56,64},{64,7... | collective-permute-start | bytes 221192 | tf_op jit(solution)/shard_map/ppermute | solution.py:15
  197.9 4.7 %collective-permute-start.28 = (bf16[3,2,16,384]{3,2,1,0:T(8,128)(2,1)S(1)}, bf16[3,2,16,384]{3,2,1,0:T(8,128)(2,1)S(1)}, u32[]{:S(2)}, u32[]{:S(2)}) collective-permute-start(bf16[3,2,16,384]{3,2,1,0:T(8,128)(2,1)S(1)} %bitcast.79), channel_id=1, source_target_pairs={{8,0},{16,8},{24,16},{32,24},{40,32},{48,40},{56,48},{64,56},{72,6... | collective-permute-start | bytes 221192 | tf_op jit(solution)/shard_map/ppermute | solution.py:18
  204.7 5.1 %collective-permute-start.29 = (bf16[22,2,2,384]{3,2,1,0:T(2,128)(2,1)S(1)}, bf16[22,2,2,384]{3,2,1,0:T(2,128)(2,1)S(1)}, u32[]{:S(2)}, u32[]{:S(2)}) collective-permute-start(bf16[22,2,2,384]{3,2,1,0:T(2,128)(2,1)S(1)} %pad_maximum_fusion.7), channel_id=1, source_target_pairs={{0,1},{1,2},{2,3},{3,4},{4,5},{5,6},{6,7},{8,9},{9,10},{10,11},{11... | collective-permute-start | bytes 202760 | tf_op jit(solution)/shard_map/ppermute | solution.py:34
  211.8 4.4 %collective-permute-done.30.right = bf16[22,2,2,384]{3,2,1,0:T(2,128)(2,1)S(1)} collective-permute-done((bf16[22,2,2,384]{3,2,1,0:T(2,128)(2,1)S(1)}, bf16[22,2,2,384]{3,2,1,0:T(2,128)(2,1)S(1)}, u32[]{:S(2)}, u32[]{:S(2)}) %collective-permute-start.30) | collective-permute-done | bytes 67616 | tf_op jit(solution)/shard_map/ppermute | solution.py:35
  216.2 3.5 %shard_map.230 = bf16[16,32,384]{2,1,0:T(8,128)(2,1)} custom-call(bf16[16,2,16,384]{3,2,1,0:T(8,128)(2,1)S(1)} %bitcast.66, bf16[3,2,16,384]{3,2,1,0:T(8,128)(2,1)S(1)} %collective-permute-done.27.top, bf16[3,2,16,384]{3,2,1,0:T(8,128)(2,1)S(1)} %collective-permute-done.28.bottom, bf16[22,2,2,384]{3,2,1,0:T(2,128)(2,1)S(1)} %collective-permute-done.29.left, ...), custom_call_target="tpu_custom_call" | custom-call | tf_op jit(solution)/shard_map/pallas_call | solution.py:413
  (156 shorter events, 51.6 us)
Async XLA Ops:
  7.2 82.9 %all-gather.2.cloned.1.call-start = ((), (), s32[]{:S(2)}) async-start(), calls=%async_computation | async-start | bytes 5013504 | tf_op jit(solution)/shard_map/all_gather | solution.py:487
  8.1 12.9 %collective-permute-start = (bf16[30,768]{1,0:T(8,128)(2,1)S(1)}, bf16[30,768]{1,0:T(8,128)(2,1)S(1)}, u32[]{:S(2)}, u32[]{:S(2)}) collective-permute-start(bf16[30,768]{1,0:T(8,128)(2,1)S(1)} %get-tuple-element.47), channel_id=1, source_target_pairs={{1,0},{2,1},{3,2},{4,3},{5,4},{6,5},{7,6},{0,7},{9,8},{10,9},{11,1... | collective-permute-start | bytes 138248 | tf_op jit(solution)/shard_map/ppermute | solution.py:50
  14.0 9.4 %collective-permute-start.1 = (bf16[30,768]{1,0:T(8,128)(2,1)S(1)}, bf16[30,768]{1,0:T(8,128)(2,1)S(1)}, u32[]{:S(2)}, u32[]{:S(2)}) collective-permute-start(bf16[30,768]{1,0:T(8,128)(2,1)S(1)} %get-tuple-element.47), channel_id=1, source_target_pairs={{2,0},{3,1},{4,2},{5,3},{6,4},{7,5},{0,6},{1,7},{10,8},{11,9},{12,... | collective-permute-start | bytes 138248 | tf_op jit(solution)/shard_map/ppermute | solution.py:50
  15.5 10.0 %collective-permute-start.2 = (bf16[30,768]{1,0:T(8,128)(2,1)S(1)}, bf16[30,768]{1,0:T(8,128)(2,1)S(1)}, u32[]{:S(2)}, u32[]{:S(2)}) collective-permute-start(bf16[30,768]{1,0:T(8,128)(2,1)S(1)} %get-tuple-element.47), channel_id=1, source_target_pairs={{3,0},{4,1},{5,2},{6,3},{7,4},{0,5},{1,6},{2,7},{11,8},{12,9},{13,... | collective-permute-start | bytes 138248 | tf_op jit(solution)/shard_map/ppermute | solution.py:50
  15.9 9.5 %collective-permute-start.3 = (bf16[30,768]{1,0:T(8,128)(2,1)S(1)}, bf16[30,768]{1,0:T(8,128)(2,1)S(1)}, u32[]{:S(2)}, u32[]{:S(2)}) collective-permute-start(bf16[30,768]{1,0:T(8,128)(2,1)S(1)} %get-tuple-element.47), channel_id=1, source_target_pairs={{4,0},{5,1},{6,2},{7,3},{0,4},{1,5},{2,6},{3,7},{12,8},{13,9},{14,... | collective-permute-start | bytes 138248 | tf_op jit(solution)/shard_map/ppermute | solution.py:50
  21.0 8.2 %collective-permute-start.4 = (bf16[30,768]{1,0:T(8,128)(2,1)S(1)}, bf16[30,768]{1,0:T(8,128)(2,1)S(1)}, u32[]{:S(2)}, u32[]{:S(2)}) collective-permute-start(bf16[30,768]{1,0:T(8,128)(2,1)S(1)} %get-tuple-element.47), channel_id=1, source_target_pairs={{5,0},{6,1},{7,2},{0,3},{1,4},{2,5},{3,6},{4,7},{13,8},{14,9},{15,... | collective-permute-start | bytes 138248 | tf_op jit(solution)/shard_map/ppermute | solution.py:50
  21.0 9.8 %collective-permute-start.5 = (bf16[30,768]{1,0:T(8,128)(2,1)S(1)}, bf16[30,768]{1,0:T(8,128)(2,1)S(1)}, u32[]{:S(2)}, u32[]{:S(2)}) collective-permute-start(bf16[30,768]{1,0:T(8,128)(2,1)S(1)} %get-tuple-element.47), channel_id=1, source_target_pairs={{6,0},{7,1},{0,2},{1,3},{2,4},{3,5},{4,6},{5,7},{14,8},{15,9},{8,1... | collective-permute-start | bytes 138248 | tf_op jit(solution)/shard_map/ppermute | solution.py:50
  23.4 7.3 %collective-permute-start.6 = (bf16[30,768]{1,0:T(8,128)(2,1)S(1)}, bf16[30,768]{1,0:T(8,128)(2,1)S(1)}, u32[]{:S(2)}, u32[]{:S(2)}) collective-permute-start(bf16[30,768]{1,0:T(8,128)(2,1)S(1)} %get-tuple-element.47), channel_id=1, source_target_pairs={{7,0},{0,1},{1,2},{2,3},{3,4},{4,5},{5,6},{6,7},{15,8},{8,9},{9,10... | collective-permute-start | bytes 138248 | tf_op jit(solution)/shard_map/ppermute | solution.py:50
  31.8 62.1 %collective-permute-start.13 = (bf16[3,32,384]{2,1,0:T(8,128)(2,1)S(1)}, bf16[3,32,384]{2,1,0:T(8,128)(2,1)S(1)}, u32[]{:S(2)}, u32[]{:S(2)}) collective-permute-start(bf16[3,32,384]{2,1,0:T(8,128)(2,1)S(1)} %get-tuple-element.57), channel_id=1, source_target_pairs={{0,8},{8,16},{16,24},{24,32},{32,40},{40,48},{48,56},{56,64},{64,7... | collective-permute-start | bytes 221192 | tf_op jit(solution)/shard_map/ppermute | solution.py:15
  35.3 57.6 %collective-permute-start.14 = (bf16[3,32,384]{2,1,0:T(8,128)(2,1)S(1)}, bf16[3,32,384]{2,1,0:T(8,128)(2,1)S(1)}, u32[]{:S(2)}, u32[]{:S(2)}) collective-permute-start(bf16[3,32,384]{2,1,0:T(8,128)(2,1)S(1)} %get-tuple-element.56), channel_id=1, source_target_pairs={{8,0},{16,8},{24,16},{32,24},{40,32},{48,40},{56,48},{64,56},{72,6... | collective-permute-start | bytes 221192 | tf_op jit(solution)/shard_map/ppermute | solution.py:18
  90.1 65.8 %collective-permute-start.22 = (bf16[1536,1536]{1,0:T(8,128)(2,1)}, bf16[1536,1536]{1,0:T(8,128)(2,1)}, u32[]{:S(2)}, u32[]{:S(2)}) collective-permute-start(bf16[1536,1536]{1,0:T(8,128)(2,1)} %all-gather.2.cloned.1.call-done.weights), channel_id=1, source_target_pairs={{0,128},{128,0},{1,129},{129,1},{2,130},{130,2},{3,131},{131,3},{4... | collective-permute-start | bytes 14155784 | tf_op jit(solution)/shard_map/ppermute | solution.py:510
  92.0 6.5 %collective-permute-start.8 = (bf16[48,768]{1,0:T(8,128)(2,1)S(1)}, bf16[48,768]{1,0:T(8,128)(2,1)S(1)}, u32[]{:S(2)}, u32[]{:S(2)}) collective-permute-start(bf16[48,768]{1,0:T(8,128)(2,1)S(1)} %reshape.64), channel_id=1, source_target_pairs={{16,0},{24,8},{0,16},{8,24},{48,32},{56,40},{32,48},{40,56},{80,64... | collective-permute-start | bytes 221192 | tf_op jit(solution)/shard_map/ppermute | solution.py:50
  99.4 16.3 %collective-permute-start.10 = (bf16[192,768]{1,0:T(8,128)(2,1)S(1)}, bf16[192,768]{1,0:T(8,128)(2,1)S(1)}, u32[]{:S(2)}, u32[]{:S(2)}) collective-permute-start(bf16[192,768]{1,0:T(8,128)(2,1)S(1)} %bitcast.69), channel_id=1, source_target_pairs={{32,0},{40,8},{48,16},{56,24},{64,32},{72,40},{80,48},{88,56},{96,... | collective-permute-start | bytes 884744 | tf_op jit(solution)/shard_map/ppermute | solution.py:50
  106.1 9.6 %collective-permute-start.11 = (bf16[192,768]{1,0:T(8,128)(2,1)S(1)}, bf16[192,768]{1,0:T(8,128)(2,1)S(1)}, u32[]{:S(2)}, u32[]{:S(2)}) collective-permute-start(bf16[192,768]{1,0:T(8,128)(2,1)S(1)} %bitcast.70), channel_id=1, source_target_pairs={{64,0},{72,8},{80,16},{88,24},{96,32},{104,40},{112,48},{120,56},{... | collective-permute-start | bytes 884744 | tf_op jit(solution)/shard_map/ppermute | solution.py:50
  107.3 13.7 %collective-permute-start.12 = (bf16[192,768]{1,0:T(8,128)(2,1)S(1)}, bf16[192,768]{1,0:T(8,128)(2,1)S(1)}, u32[]{:S(2)}, u32[]{:S(2)}) collective-permute-start(bf16[192,768]{1,0:T(8,128)(2,1)S(1)} %bitcast.72), channel_id=1, source_target_pairs={{96,0},{104,8},{112,16},{120,24},{0,32},{8,40},{16,48},{24,56},{32... | collective-permute-start | bytes 884744 | tf_op jit(solution)/shard_map/ppermute | solution.py:50
  128.7 10.1 %collective-permute-start.18 = (bf16[3,16,768]{2,1,0:T(8,128)(2,1)S(1)}, bf16[3,16,768]{2,1,0:T(8,128)(2,1)S(1)}, u32[]{:S(2)}, u32[]{:S(2)}) collective-permute-start(bf16[3,16,768]{2,1,0:T(8,128)(2,1)S(1)} %bitcast.74), channel_id=1, source_target_pairs={{0,8},{8,16},{16,24},{24,32},{32,40},{40,48},{48,56},{56,64},{64,7... | collective-permute-start | bytes 221192 | tf_op jit(solution)/shard_map/ppermute | solution.py:15
  130.8 8.0 %collective-permute-start.19 = (bf16[3,16,768]{2,1,0:T(8,128)(2,1)S(1)}, bf16[3,16,768]{2,1,0:T(8,128)(2,1)S(1)}, u32[]{:S(2)}, u32[]{:S(2)}) collective-permute-start(bf16[3,16,768]{2,1,0:T(8,128)(2,1)S(1)} %bitcast.77), channel_id=1, source_target_pairs={{8,0},{16,8},{24,16},{32,24},{40,32},{48,40},{56,48},{64,56},{72,6... | collective-permute-start | bytes 221192 | tf_op jit(solution)/shard_map/ppermute | solution.py:18
  163.4 10.3 %collective-permute-start.23 = (bf16[3,16,768]{2,1,0:T(8,128)(2,1)S(1)}, bf16[3,16,768]{2,1,0:T(8,128)(2,1)S(1)}, u32[]{:S(2)}, u32[]{:S(2)}) collective-permute-start(bf16[3,16,768]{2,1,0:T(8,128)(2,1)S(1)} %bitcast.75), channel_id=1, source_target_pairs={{0,8},{8,16},{16,24},{24,32},{32,40},{40,48},{48,56},{56,64},{64,7... | collective-permute-start | bytes 221192 | tf_op jit(solution)/shard_map/ppermute | solution.py:15
  165.4 8.4 %collective-permute-start.24 = (bf16[3,16,768]{2,1,0:T(8,128)(2,1)S(1)}, bf16[3,16,768]{2,1,0:T(8,128)(2,1)S(1)}, u32[]{:S(2)}, u32[]{:S(2)}) collective-permute-start(bf16[3,16,768]{2,1,0:T(8,128)(2,1)S(1)} %bitcast.78), channel_id=1, source_target_pairs={{8,0},{16,8},{24,16},{32,24},{40,32},{48,40},{56,48},{64,56},{72,6... | collective-permute-start | bytes 221192 | tf_op jit(solution)/shard_map/ppermute | solution.py:18
  173.9 7.7 %collective-permute-start.25 = (bf16[14,3,768]{2,1,0:T(4,128)(2,1)S(1)}, bf16[14,3,768]{2,1,0:T(4,128)(2,1)S(1)}, u32[]{:S(2)}, u32[]{:S(2)}) collective-permute-start(bf16[14,3,768]{2,1,0:T(4,128)(2,1)S(1)} %pad_maximum_fusion.3), channel_id=1, source_target_pairs={{0,1},{1,2},{2,3},{3,4},{4,5},{5,6},{6,7},{8,9},{9,10},{10,11},{11... | collective-permute-start | bytes 193544 | tf_op jit(solution)/shard_map/ppermute | solution.py:34
  178.0 7.3 %collective-permute-start.26 = (bf16[14,3,768]{2,1,0:T(4,128)(2,1)S(1)}, bf16[14,3,768]{2,1,0:T(4,128)(2,1)S(1)}, u32[]{:S(2)}, u32[]{:S(2)}) collective-permute-start(bf16[14,3,768]{2,1,0:T(4,128)(2,1)S(1)} %pad_maximum_fusion.4), channel_id=1, source_target_pairs={{1,0},{2,1},{3,2},{4,3},{5,4},{6,5},{7,6},{9,8},{10,9},{11,10},{12... | collective-permute-start | bytes 193544 | tf_op jit(solution)/shard_map/ppermute | solution.py:35
  194.3 10.3 %collective-permute-start.27 = (bf16[3,2,16,384]{3,2,1,0:T(8,128)(2,1)S(1)}, bf16[3,2,16,384]{3,2,1,0:T(8,128)(2,1)S(1)}, u32[]{:S(2)}, u32[]{:S(2)}) collective-permute-start(bf16[3,2,16,384]{3,2,1,0:T(8,128)(2,1)S(1)} %bitcast.76), channel_id=1, source_target_pairs={{0,8},{8,16},{16,24},{24,32},{32,40},{40,48},{48,56},{56,64},{64,7... | collective-permute-start | bytes 221192 | tf_op jit(solution)/shard_map/ppermute | solution.py:15
  197.9 6.6 %collective-permute-start.28 = (bf16[3,2,16,384]{3,2,1,0:T(8,128)(2,1)S(1)}, bf16[3,2,16,384]{3,2,1,0:T(8,128)(2,1)S(1)}, u32[]{:S(2)}, u32[]{:S(2)}) collective-permute-start(bf16[3,2,16,384]{3,2,1,0:T(8,128)(2,1)S(1)} %bitcast.79), channel_id=1, source_target_pairs={{8,0},{16,8},{24,16},{32,24},{40,32},{48,40},{56,48},{64,56},{72,6... | collective-permute-start | bytes 221192 | tf_op jit(solution)/shard_map/ppermute | solution.py:18
  204.7 7.0 %collective-permute-start.29 = (bf16[22,2,2,384]{3,2,1,0:T(2,128)(2,1)S(1)}, bf16[22,2,2,384]{3,2,1,0:T(2,128)(2,1)S(1)}, u32[]{:S(2)}, u32[]{:S(2)}) collective-permute-start(bf16[22,2,2,384]{3,2,1,0:T(2,128)(2,1)S(1)} %pad_maximum_fusion.7), channel_id=1, source_target_pairs={{0,1},{1,2},{2,3},{3,4},{4,5},{5,6},{6,7},{8,9},{9,10},{10,11},{11... | collective-permute-start | bytes 202760 | tf_op jit(solution)/shard_map/ppermute | solution.py:34
  (27 other events, 481.3 us)
Sparse Core Ops, SparseCore 0:
  31.9 58.1 all-gather.1

commit v2 on v1

--- a/solution.py
+++ b/solution.py
@@ -248,17 +248,28 @@
     return [slice(first, first + size) for first in range(0, total, size)]
 
 
+def over_hidden(weights, step):
+    total = weights.shape[0]
+    block = min(total, 256)
+
+    def run(index, carry):
+        step(pl.ds(pl.multiple_of(index * block, block), block))
+        return carry
+
+    lax.fori_loop(0, total // block, run, 0)
+
+
 def mlp_one_half(normed, weights, bias, branch):
     width = normed.shape[1]
-
-    @pl.when(pl.program_id(0) == 0)
-    def _():
-        branch[...] = jnp.zeros_like(branch)
-
-    for rows in row_blocks(normed.shape[0], 256):
-        pre_act = contract_last(normed[rows, :], weights[:, :width]) + bias[...]
-        hidden = (pre_act * normal_cdf(pre_act)).astype(jnp.bfloat16)
-        branch[rows, :] += dot(hidden, weights[:, width:])
+    branch[...] = jnp.zeros_like(branch)
+
+    def step(units):
+        for rows in row_blocks(normed.shape[0], 256):
+            pre_act = contract_last(normed[rows, :], weights[units, :width]) + bias[:, units]
+            hidden = (pre_act * normal_cdf(pre_act)).astype(jnp.bfloat16)
+            branch[rows, :] += dot(hidden, weights[units, width:])
+
+    over_hidden(weights, step)
 
 
 def mlp_one_finish(
@@ -269,39 +280,40 @@
     positions, width = normed.shape
     quarter = patches.shape[0]
     half_cols = patches.shape[2]
-
-    @pl.when(pl.program_id(0) == pl.num_programs(0) - 1)
-    def _():
-        step_rows = 4 * half_cols
-
-        def step(index, carry):
-            rows = pl.ds(pl.multiple_of(index * step_rows, step_rows), step_rows)
-            total = branch[rows, :] + partial[rows, :] + down_bias[...]
-            out = (residual[rows, :].astype(jnp.float32) + scale[...] * total).astype(jnp.bfloat16)
-            section[rows, :] = out
-            normal = norm_forward(out.astype(jnp.float32), gain[...], shift[...])[2]
-            normal = normal.astype(jnp.bfloat16)
-            for place in range(4):
-                patches[index, place] = normal[place * half_cols : (place + 1) * half_cols, :]
-            return carry
-
-        lax.fori_loop(0, quarter, step, 0)
-        total = merge_bias[...]
+    step_rows = 4 * half_cols
+
+    def step(index, carry):
+        rows = pl.ds(pl.multiple_of(index * step_rows, step_rows), step_rows)
+        total = branch[rows, :] + partial[rows, :] + down_bias[...]
+        out = (residual[rows, :].astype(jnp.float32) + scale[...] * total).astype(jnp.bfloat16)
+        section[rows, :] = out
+        normal = norm_forward(out.astype(jnp.float32), gain[...], shift[...])[2]
+        normal = normal.astype(jnp.bfloat16)
         for place in range(4):
-            patch = patches[:, place].reshape(quarter * half_cols, width)
-            total = total + dot(patch, merge[place * width : (place + 1) * width, :])
-        merged[...] = total.astype(merged.dtype)
+            patches[index, place] = normal[place * half_cols : (place + 1) * half_cols, :]
+        return carry
+
+    lax.fori_loop(0, quarter, step, 0)
+    total = merge_bias[...]
+    for place in range(4):
+        patch = patches[:, place].reshape(quarter * half_cols, width)
+        total = total + dot(patch, merge[place * width : (place + 1) * width, :])
+    merged[...] = total.astype(merged.dtype)
 
 
 def slope_one_kernel(normed, own, other, bias_own, bias_other, slope_own, slope_other):
     width = normed.shape[1]
-    for rows in row_blocks(normed.shape[0], 256):
-        for weights, bias, slope in (
-            (own, bias_own, slope_own),
-            (other, bias_other, slope_other),
-        ):
-            pre_act = contract_last(normed[rows, :], weights[:, :width]) + bias[...]
-            slope[rows, :] = slope_from(pre_act, normal_cdf(pre_act)).astype(slope.dtype)
+
+    def step(units):
+        for rows in row_blocks(normed.shape[0], 256):
+            for weights, bias, slope in (
+                (own, bias_own, slope_own),
+                (other, bias_other, slope_other),
+            ):
+                pre_act = contract_last(normed[rows, :], weights[units, :width]) + bias[:, units]
+                slope[rows, units] = slope_from(pre_act, normal_cdf(pre_act)).astype(slope.dtype)
+
+    over_hidden(own, step)
 
 
 def back_mlp_one(
@@ -310,39 +322,36 @@
 ):
     width = section.shape[1]
     quarter = d_merged.shape[0]
-    half_cols = 16
-    groups = quarter // half_cols
-
-    @pl.when(pl.program_id(0) == 0)
-    def _():
-        d_normed[...] = jnp.zeros_like(d_normed)
-        for place in range(4):
-            d_normal = contract_last(d_merged[...], merge[place * width : (place + 1) * width, :])
-            for group in range(groups):
-                first = (4 * group + place) * half_cols
-                rows = slice(first, first + half_cols)
-                values = section[rows, :].astype(jnp.float32)
-                scaled, inv_std, _ = norm_forward(values, 1.0, 0.0)
-                flow = norm_backward(
-                    d_normal[group * half_cols : (group + 1) * half_cols],
-                    scaled,
-                    inv_std,
-                    gain_mid[...],
-                )
-                upstream[rows, :] = flow
-                d_branch[rows, :] = (flow * scale[...]).astype(d_branch.dtype)
-
-    for rows in row_blocks(section.shape[0], 256):
-        total = d_normed[rows, :]
-        for weights, slope in ((own, slope_own), (other, slope_other)):
-            d_hidden = contract_last(d_branch[rows, :], weights[:, width:])
-            d_pre = (d_hidden * slope[rows, :].astype(jnp.float32)).astype(jnp.bfloat16)
-            total = total + dot(d_pre, weights[:, :width])
-        d_normed[rows, :] = total
-
-    @pl.when(pl.program_id(0) == pl.num_programs(0) - 1)
-    def _():
-        norm_back_rows(conv, d_normed, gain, d_conv, 64)
+    groups = section.shape[0] // 64
+    half_cols = quarter // groups
+    for place in range(4):
+        d_normal = contract_last(d_merged[...], merge[place * width : (place + 1) * width, :])
+        for group in range(groups):
+            first = (4 * group + place) * half_cols
+            rows = slice(first, first + half_cols)
+            values = section[rows, :].astype(jnp.float32)
+            scaled, inv_std, _ = norm_forward(values, 1.0, 0.0)
+            flow = norm_backward(
+                d_normal[group * half_cols : (group + 1) * half_cols],
+                scaled,
+                inv_std,
+                gain_mid[...],
+            )
+            upstream[rows, :] = flow
+            d_branch[rows, :] = (flow * scale[...]).astype(d_branch.dtype)
+    d_normed[...] = jnp.zeros_like(d_normed)
+
+    def step(units):
+        for rows in row_blocks(section.shape[0], 256):
+            total = d_normed[rows, :]
+            for weights, slope in ((own, slope_own), (other, slope_other)):
+                d_hidden = contract_last(d_branch[rows, :], weights[units, width:])
+                d_pre = (d_hidden * slope[rows, units].astype(jnp.float32)).astype(jnp.bfloat16)
+                total = total + dot(d_pre, weights[units, :width])
+            d_normed[rows, :] = total
+
+    over_hidden(own, step)
+    norm_back_rows(conv, d_normed, gain, d_conv, 64)
 
 
 def norm_back_rows(conv, d_normed, gain, d_conv, chunk):
@@ -358,22 +367,20 @@
 
 def mlp_two_half(normed, grad, scale, weights, bias, branch, d_normed, d_branch):
     width = normed.shape[1]
-
-    @pl.when(pl.program_id(0) == 0)
-    def _():
-        branch[...] = jnp.zeros_like(branch)
-        d_normed[...] = jnp.zeros_like(d_normed)
-        d_branch[...] = (grad[...].astype(jnp.float32) * scale[...]).astype(d_branch.dtype)
-
-    up = weights[:, :width]
-    down = weights[:, width:]
-    pre_act = contract_last(normed[...], up) + bias[...]
-    d_hidden = contract_last(d_branch[...], down)
-    cdf = normal_cdf(pre_act)
-    hidden = (pre_act * cdf).astype(jnp.bfloat16)
-    d_pre = (d_hidden * slope_from(pre_act, cdf)).astype(jnp.bfloat16)
-    branch[...] += dot(hidden, down)
-    d_normed[...] += dot(d_pre, up)
+    branch[...] = jnp.zeros_like(branch)
+    d_normed[...] = jnp.zeros_like(d_normed)
+    d_branch[...] = (grad[...].astype(jnp.float32) * scale[...]).astype(d_branch.dtype)
+
+    def step(units):
+        pre_act = contract_last(normed[...], weights[units, :width]) + bias[:, units]
+        d_hidden = contract_last(d_branch[...], weights[units, width:])
+        cdf = normal_cdf(pre_act)
+        hidden = (pre_act * cdf).astype(jnp.bfloat16)
+        d_pre = (d_hidden * slope_from(pre_act, cdf)).astype(jnp.bfloat16)
+        branch[...] += dot(hidden, weights[units, width:])
+        d_normed[...] += dot(d_pre, weights[units, :width])
+
+    over_hidden(weights, step)
 
 
 def mlp_two_finish(
@@ -381,14 +388,11 @@
     features, d_conv, branch, d_normed, d_branch,
 ):
     mlp_two_half(normed, grad, scale, weights, bias, branch, d_normed, d_branch)
-
-    @pl.when(pl.program_id(0) == pl.num_programs(0) - 1)
-    def _():
-        total = branch[...] + partial[...] + down_bias[...]
-        out = merged[...].astype(jnp.float32) + scale[...] * total
-        features[...] = out.astype(features.dtype)
-        d_normed[...] += d_partial[...]
-        norm_back_rows(conv, d_normed, gain, d_conv, 64)
+    total = branch[...] + partial[...] + down_bias[...]
+    out = merged[...].astype(jnp.float32) + scale[...] * total
+    features[...] = out.astype(features.dtype)
+    d_normed[...] += d_partial[...]
+    norm_back_rows(conv, d_normed, gain, d_conv, 64)
 
 
 megabyte = 1024 * 1024
@@ -398,24 +402,13 @@
     return jax.ShapeDtypeStruct(dims, dtype)
 
 
-def block_call(kernel, outputs, operands, scratch, steps=1, split=(), limit=40):
-    def spec_of(array, key):
-        dims = list(array.shape)
-        axis = dict(split).get(key)
-        if axis is not None:
-            dims[axis] //= steps
-
-        def index_map(step):
-            return tuple(step if place == axis else 0 for place in range(len(dims)))
-
-        return pl.BlockSpec(tuple(dims), index_map)
-
+def block_call(kernel, outputs, operands, scratch, limit=48):
+    whole = pl.BlockSpec(memory_space=pltpu.VMEM)
     return pl.pallas_call(
         kernel,
-        grid=(steps,),
         out_shape=outputs,
-        in_specs=[spec_of(array, index) for index, array in enumerate(operands)],
-        out_specs=[spec_of(array, "out%d" % index) for index, array in enumerate(outputs)],
+        in_specs=[whole] * len(operands),
+        out_specs=[whole] * len(outputs),
         scratch_shapes=scratch,
         compiler_params=pltpu.CompilerParams(vmem_limit_bytes=limit * megabyte),
     )(*operands)
@@ -507,17 +500,12 @@
         (own_one, normed_one, images_par, bias_one, bias_two)
     )
     other_one = lax.ppermute(own_one, "sec", swap)
-    other_two = lax.ppermute(own_two, "sec", swap)
-    steps_one = max(1, own_one.shape[0] // 256)
-    steps_two = max(1, own_two.shape[0] // 256)
 
     (partial_one,) = block_call(
         mlp_one_half,
         (shape_of((rows_one, width_one), jnp.float32),),
         (normed_one, own_one, bias_one[0]),
         [],
-        steps_one,
-        ((1, 0), (2, 1)),
     )
     section_out, merged = block_call(
         mlp_one_finish,
@@ -539,8 +527,6 @@
             pltpu.VMEM((rows_one, width_one), jnp.float32),
             pltpu.VMEM((micro_count * half_rows, 4, half_cols, width_one), bfloat),
         ],
-        steps_one,
-        ((1, 0), (2, 1)),
     )
     slope_own, slope_other = block_call(
         slope_one_kernel,
@@ -550,8 +536,6 @@
         ),
         (normed_one, own_one, other_one, *bias_one),
         [],
-        steps_one,
-        ((1, 0), (2, 0), (3, 1), (4, 1), ("out0", 1), ("out1", 1)),
     )
 
     merged_tile = merged.reshape(half_rows, half_cols, width_two)
@@ -563,6 +547,8 @@
         width_two,
         (merged_tile, *halo_of(merged_tile, 3), kernel_two, gain_two[None], shift_two[None]),
     )
+    own_two, normed_two = lax.optimization_barrier((own_two, normed_two))
+    other_two = lax.ppermute(own_two, "sec", swap)
     grad_rows = grad_out.reshape(rows_two, width_two)
     two_wide = shape_of((rows_two, width_two), jnp.float32)
     two_scratch = pltpu.VMEM((rows_two, width_two), jnp.float32)
@@ -572,8 +558,6 @@
         (two_wide, two_wide),
         (normed_two, grad_rows, scale_two[None], own_two, bias_two[0]),
         [two_branch],
-        steps_two,
-        ((3, 0), (4, 1)),
     )
     features, d_conv_two = block_call(
         mlp_two_finish,
@@ -592,8 +576,6 @@
             gain_two[None],
         ),
         [two_scratch, two_scratch, two_branch],
-        steps_two,
-        ((3, 0), (4, 1)),
     )
     back_tile = d_conv_two.reshape(half_rows, half_cols, width_two)
     (d_merged,) = tile_call(
@@ -624,8 +606,6 @@
             pltpu.VMEM((rows_one, width_one), bfloat),
             pltpu.VMEM((rows_one, width_one), jnp.float32),
         ],
-        steps_one,
-        ((5, 0), (6, 0), (7, 1), (8, 1)),
     )
     d_conv_one = d_conv_one.reshape(tile_rows, 2, half_cols, width_one)
     (input_grad,) = tile_call(

time: 229 us -> 184 us (0.80)
  waiting for transfers between devices: 87.4 us -> 36.5 us
  local copies, waits for them, and re-layouts: 1.13 us -> 7.69 us
    all_gather x1, waiting for transfers between devices: 50.3 us -> 0.01 us  [on_device(): own_two = lax.all_gather(part_two, 'row', axis=0, tiled=True)]
    unnamed x38 -> x52, local copies, waits for them, and re-layouts: 0.14 us -> 5.33 us
    ppermute x4, waiting for transfers between devices: 14.4 us -> 12.1 us  [halo_of(): right = lax.ppermute(edge(0, width), 'col', backward)]
  transfers between devices with their start and end apart: 32 -> 32, of which waited for: 16 -> 18; matrix products, arithmetic and copies ran while one was open for 1% -> 1% of each run, Pallas kernels for 9% -> 11%
where the time goes in v2:
time: 184 us; the launch traced here: 182 us
  starting transfers between devices  78.6 us (43%)
  Pallas kernels  41.7 us (23%)
  waiting for transfers between devices  36.5 us (20%)
  between operations  15.2 us (8%)
  local copies, waits for them, and re-layouts  7.69 us (4%)
  other arithmetic  2.15 us (1%)
    pallas_call x10, Pallas kernels, block_call(): pl.pallas_call(kernel, out_shape=outputs, in_specs=[whole] * len(operands...  41.7 us
    ppermute x13, starting transfers between devices, ring_collect(): arrived = lax.ppermute(piece, axis, pairs)  24.8 us
    ppermute x4, starting transfers between devices, exchange(): lax.ppermute(lax.slice_in_dim(block, 0, width, axis=dim), axis, backward)  20.6 us
    ppermute x4, starting transfers between devices, halo_of(): left = lax.ppermute(edge(extent - width, extent), 'col', forward)  15.6 us
    ppermute x13, waiting for transfers between devices, ring_collect(): arrived = lax.ppermute(piece, axis, pairs)  14.9 us
    ppermute x4, starting transfers between devices, exchange(): lax.ppermute(lax.slice_in_dim(block, block.shape[dim] - width, None, axis...  12.2 us
    ppermute x4, waiting for transfers between devices, halo_of(): right = lax.ppermute(edge(0, width), 'col', backward)  12.1 us
    ppermute x4, waiting for transfers between devices, exchange(): lax.ppermute(lax.slice_in_dim(block, 0, width, axis=dim), axis, backward)  7.62 us
  transfers between devices with their start and end apart: 32, of which 18 were waited for; matrix products, arithmetic and copies ran while one was open for 1% of the time, Pallas kernels for 11%

profile of v2, /device:TPU:2, one launch (start us, length us, event | category | flops | bytes accessed | tf_op | source)
XLA Modules:
  0.0 181.9 jit_solution(5911864207253520459)
XLA Ops:
  8.1 5.9 %collective-permute-start = (bf16[30,768]{1,0:T(8,128)(2,1)S(1)}, bf16[30,768]{1,0:T(8,128)(2,1)S(1)}, u32[]{:S(2)}, u32[]{:S(2)}) collective-permute-start(bf16[30,768]{1,0:T(8,128)(2,1)S(1)} %get-tuple-element.51), channel_id=1, source_target_pairs={{1,0},{2,1},{3,2},{4,3},{5,4},{6,5},{7,6},{0,7},{9,8},{10,9},{11,1... | collective-permute-start | bytes 138248 | tf_op jit(solution)/shard_map/ppermute | solution.py:50
  15.9 5.0 %collective-permute-start.3 = (bf16[30,768]{1,0:T(8,128)(2,1)S(1)}, bf16[30,768]{1,0:T(8,128)(2,1)S(1)}, u32[]{:S(2)}, u32[]{:S(2)}) collective-permute-start(bf16[30,768]{1,0:T(8,128)(2,1)S(1)} %get-tuple-element.51), channel_id=1, source_target_pairs={{4,0},{5,1},{6,2},{7,3},{0,4},{1,5},{2,6},{3,7},{12,8},{13,9},{14,... | collective-permute-start | bytes 138248 | tf_op jit(solution)/shard_map/ppermute | solution.py:50
  25.5 3.7 %collective-permute-done.4 = bf16[30,768]{1,0:T(8,128)(2,1)S(1)} collective-permute-done((bf16[30,768]{1,0:T(8,128)(2,1)S(1)}, bf16[30,768]{1,0:T(8,128)(2,1)S(1)}, u32[]{:S(2)}, u32[]{:S(2)}) %collective-permute-start.4) | collective-permute-done | bytes 46112 | tf_op jit(solution)/shard_map/ppermute | solution.py:50
  31.8 3.5 %collective-permute-start.13 = (bf16[3,32,384]{2,1,0:T(8,128)(2,1)S(1)}, bf16[3,32,384]{2,1,0:T(8,128)(2,1)S(1)}, u32[]{:S(2)}, u32[]{:S(2)}) collective-permute-start(bf16[3,32,384]{2,1,0:T(8,128)(2,1)S(1)} %get-tuple-element.59), channel_id=1, source_target_pairs={{0,8},{8,16},{16,24},{24,32},{32,40},{40,48},{48,56},{56,64},{64,7... | collective-permute-start | bytes 221192 | tf_op jit(solution)/shard_map/ppermute | solution.py:15
  35.3 4.5 %collective-permute-start.14 = (bf16[3,32,384]{2,1,0:T(8,128)(2,1)S(1)}, bf16[3,32,384]{2,1,0:T(8,128)(2,1)S(1)}, u32[]{:S(2)}, u32[]{:S(2)}) collective-permute-start(bf16[3,32,384]{2,1,0:T(8,128)(2,1)S(1)} %get-tuple-element.58), channel_id=1, source_target_pairs={{8,0},{16,8},{24,16},{32,24},{40,32},{48,40},{56,48},{64,56},{72,6... | collective-permute-start | bytes 221192 | tf_op jit(solution)/shard_map/ppermute | solution.py:18
  57.2 4.7 %shard_map.221 = (bf16[512,384]{1,0:T(8,128)(2,1)S(1)}, f32[512,384]{1,0:T(8,128)S(1)}, bf16[512,384]{1,0:T(8,128)(2,1)S(1)}) custom-call(bf16[16,32,384]{2,1,0:T(8,128)(2,1)S(1)} %bitcast.64, bf16[3,32,384]{2,1,0:T(8,128)(2,1)S(1)} %collective-permute-done.13.top, bf16[3,32,384]{2,1,0:T(8,128)(2,1)S(1)} %collective-permute-done.14.bottom, ...), custom_call_target="tpu_custom_call" | custom-call | tf_op jit(solution)/shard_map/pallas_call | solution.py:407
  66.8 2.6 %shard_map.222.partial = f32[512,384]{1,0:T(8,128)S(1)} custom-call(bf16[512,384]{1,0:T(8,128)(2,1)S(1)} %get-tuple-element.28.normed, bf16[768,768]{1,0:T(8,128)(2,1)S(1)} %bitcast.55, f32[1,768]{1,0:T(1,128)S(1)} %select_n.195.bias.bias_own), custom_call_target="tpu_custom_call" | custom-call | tf_op jit(solution)/shard_map/pallas_call | solution.py:407
  69.5 4.7 %shard_map.223 = (bf16[512,384]{1,0:T(8,128)(2,1)S(1)}, bf16[128,768]{1,0:T(8,128)(2,1)S(1)}) custom-call(bf16[512,384]{1,0:T(8,128)(2,1)S(1)} %get-tuple-element.28.normed, bf16[768,768]{1,0:T(8,128)(2,1)S(1)} %collective-permute-done.17.weights.other, f32[1,768]{1,0:T(1,128)S(1)} %select_n.197.bias.bias_other, f32[512,384]{1,0:T(8,128)S(1)} %shard_map.222.partial, ...), custom_call_target="tpu_custom_call" | custom-call | tf_op jit(solution)/shard_map/pallas_call | solution.py:407
  74.3 3.0 %collective-permute-start.18 = (bf16[3,16,768]{2,1,0:T(8,128)(2,1)S(1)}, bf16[3,16,768]{2,1,0:T(8,128)(2,1)S(1)}, u32[]{:S(2)}, u32[]{:S(2)}) collective-permute-start(bf16[3,16,768]{2,1,0:T(8,128)(2,1)S(1)} %bitcast.74), channel_id=1, source_target_pairs={{0,8},{8,16},{16,24},{24,32},{32,40},{40,48},{48,56},{56,64},{64,7... | collective-permute-start | bytes 221192 | tf_op jit(solution)/shard_map/ppermute | solution.py:15
  77.3 5.1 %collective-permute-start.19 = (bf16[3,16,768]{2,1,0:T(8,128)(2,1)S(1)}, bf16[3,16,768]{2,1,0:T(8,128)(2,1)S(1)}, u32[]{:S(2)}, u32[]{:S(2)}) collective-permute-start(bf16[3,16,768]{2,1,0:T(8,128)(2,1)S(1)} %bitcast.77), channel_id=1, source_target_pairs={{8,0},{16,8},{24,16},{32,24},{40,32},{48,40},{56,48},{64,56},{72,6... | collective-permute-start | bytes 221192 | tf_op jit(solution)/shard_map/ppermute | solution.py:18
  82.5 3.8 %collective-permute-done.19.bottom = bf16[3,16,768]{2,1,0:T(8,128)(2,1)S(1)} collective-permute-done((bf16[3,16,768]{2,1,0:T(8,128)(2,1)S(1)}, bf16[3,16,768]{2,1,0:T(8,128)(2,1)S(1)}, u32[]{:S(2)}, u32[]{:S(2)}) %collective-permute-start.19) | collective-permute-done | bytes 73760 | tf_op jit(solution)/shard_map/ppermute | solution.py:18
  86.5 4.7 %collective-permute-start.20 = (bf16[14,3,768]{2,1,0:T(4,128)(2,1)S(1)}, bf16[14,3,768]{2,1,0:T(4,128)(2,1)S(1)}, u32[]{:S(2)}, u32[]{:S(2)}) collective-permute-start(bf16[14,3,768]{2,1,0:T(4,128)(2,1)S(1)} %pad_maximum_fusion.1), channel_id=1, source_target_pairs={{0,1},{1,2},{2,3},{3,4},{4,5},{5,6},{6,7},{8,9},{9,10},{10,11},{11... | collective-permute-start | bytes 193544 | tf_op jit(solution)/shard_map/ppermute | solution.py:34
  93.2 4.4 %collective-permute-done.21.right = bf16[14,3,768]{2,1,0:T(4,128)(2,1)S(1)} collective-permute-done((bf16[14,3,768]{2,1,0:T(4,128)(2,1)S(1)}, bf16[14,3,768]{2,1,0:T(4,128)(2,1)S(1)}, u32[]{:S(2)}, u32[]{:S(2)}) %collective-permute-start.21) | collective-permute-done | bytes 64544 | tf_op jit(solution)/shard_map/ppermute | solution.py:35
  104.3 3.8 %shard_map.225 = (f32[128,768]{1,0:T(8,128)S(1)}, f32[128,768]{1,0:T(8,128)S(1)}) custom-call(bf16[128,768]{1,0:T(8,128)(2,1)S(1)} %get-tuple-element.35.normed, bf16[128,768]{1,0:T(8,128)(2,1)S(1)} %bitcast.60, f32[1,768]{1,0:T(1,128)S(1)} %broadcast_in_dim.126.scale, bf16[1536,1536]{1,0:T(8,128)(2,1)S(1)} %copy-done.2, f32[1,1536]{1,0:T(1,128)S(1)} %select_n.200.bias), custom_call_target="tpu_custom_call" | custom-call | tf_op jit(solution)/shard_map/pallas_call | solution.py:407
  110.9 7.2 %shard_map.226 = (bf16[128,768]{1,0:T(8,128)(2,1)}, bf16[128,768]{1,0:T(8,128)(2,1)S(1)}) custom-call(bf16[128,768]{1,0:T(8,128)(2,1)S(1)} %get-tuple-element.35.normed, bf16[128,768]{1,0:T(8,128)(2,1)S(1)} %bitcast.61, f32[1,768]{1,0:T(1,128)S(1)} %broadcast_in_dim.126.scale, bf16[1536,1536]{1,0:T(8,128)(2,1)} %copy-done.14, f32[1,1536]{1,0:T(1,128)S(1)} %select_n.202.bias, ...), custom_call_target="tpu_custom_call" | custom-call | tf_op jit(solution)/shard_map/pallas_call | solution.py:407
  120.2 6.4 %collective-permute-start.24 = (bf16[3,16,768]{2,1,0:T(8,128)(2,1)S(1)}, bf16[3,16,768]{2,1,0:T(8,128)(2,1)S(1)}, u32[]{:S(2)}, u32[]{:S(2)}) collective-permute-start(bf16[3,16,768]{2,1,0:T(8,128)(2,1)S(1)} %bitcast.78), channel_id=1, source_target_pairs={{8,0},{16,8},{24,16},{32,24},{40,32},{48,40},{56,48},{64,56},{72,6... | collective-permute-start | bytes 221192 | tf_op jit(solution)/shard_map/ppermute | solution.py:18
  128.7 3.6 %collective-permute-start.25 = (bf16[14,3,768]{2,1,0:T(4,128)(2,1)S(1)}, bf16[14,3,768]{2,1,0:T(4,128)(2,1)S(1)}, u32[]{:S(2)}, u32[]{:S(2)}) collective-permute-start(bf16[14,3,768]{2,1,0:T(4,128)(2,1)S(1)} %pad_maximum_fusion.3), channel_id=1, source_target_pairs={{0,1},{1,2},{2,3},{3,4},{4,5},{5,6},{6,7},{8,9},{9,10},{10,11},{11... | collective-permute-start | bytes 193544 | tf_op jit(solution)/shard_map/ppermute | solution.py:34
  135.8 3.0 %collective-permute-done.26.right = bf16[14,3,768]{2,1,0:T(4,128)(2,1)S(1)} collective-permute-done((bf16[14,3,768]{2,1,0:T(4,128)(2,1)S(1)}, bf16[14,3,768]{2,1,0:T(4,128)(2,1)S(1)}, u32[]{:S(2)}, u32[]{:S(2)}) %collective-permute-start.26) | collective-permute-done | bytes 64544 | tf_op jit(solution)/shard_map/ppermute | solution.py:35
  140.5 9.1 %shard_map.229 = (bf16[512,384]{1,0:T(8,128)(2,1)S(1)}, f32[512,384]{1,0:T(8,128)S(1)}) custom-call(bf16[128,768]{1,0:T(8,128)(2,1)S(1)} %shard_map.227.d_merged, bf16[1536,768]{1,0:T(8,128)(2,1)} %merge.3, bf16[512,384]{1,0:T(8,128)(2,1)S(1)} %copy-done.9, f32[1,384]{1,0:T(1,128)S(1)} %broadcast_in_dim.121.gain.gain_mid, ...), custom_call_target="tpu_custom_call" | custom-call | tf_op jit(solution)/shard_map/pallas_call | solution.py:407
  149.7 3.7 %collective-permute-start.27 = (bf16[3,2,16,384]{3,2,1,0:T(8,128)(2,1)S(1)}, bf16[3,2,16,384]{3,2,1,0:T(8,128)(2,1)S(1)}, u32[]{:S(2)}, u32[]{:S(2)}) collective-permute-start(bf16[3,2,16,384]{3,2,1,0:T(8,128)(2,1)S(1)} %bitcast.76), channel_id=1, source_target_pairs={{0,8},{8,16},{16,24},{24,32},{32,40},{40,48},{48,56},{56,64},{64,7... | collective-permute-start | bytes 221192 | tf_op jit(solution)/shard_map/ppermute | solution.py:15
  153.3 4.6 %collective-permute-start.28 = (bf16[3,2,16,384]{3,2,1,0:T(8,128)(2,1)S(1)}, bf16[3,2,16,384]{3,2,1,0:T(8,128)(2,1)S(1)}, u32[]{:S(2)}, u32[]{:S(2)}) collective-permute-start(bf16[3,2,16,384]{3,2,1,0:T(8,128)(2,1)S(1)} %bitcast.79), channel_id=1, source_target_pairs={{8,0},{16,8},{24,16},{32,24},{40,32},{48,40},{56,48},{64,56},{72,6... | collective-permute-start | bytes 221192 | tf_op jit(solution)/shard_map/ppermute | solution.py:18
  160.1 5.1 %collective-permute-start.29 = (bf16[22,2,2,384]{3,2,1,0:T(2,128)(2,1)S(1)}, bf16[22,2,2,384]{3,2,1,0:T(2,128)(2,1)S(1)}, u32[]{:S(2)}, u32[]{:S(2)}) collective-permute-start(bf16[22,2,2,384]{3,2,1,0:T(2,128)(2,1)S(1)} %pad_maximum_fusion.7), channel_id=1, source_target_pairs={{0,1},{1,2},{2,3},{3,4},{4,5},{5,6},{6,7},{8,9},{9,10},{10,11},{11... | collective-permute-start | bytes 202760 | tf_op jit(solution)/shard_map/ppermute | solution.py:34
  167.1 4.4 %collective-permute-done.30.right = bf16[22,2,2,384]{3,2,1,0:T(2,128)(2,1)S(1)} collective-permute-done((bf16[22,2,2,384]{3,2,1,0:T(2,128)(2,1)S(1)}, bf16[22,2,2,384]{3,2,1,0:T(2,128)(2,1)S(1)}, u32[]{:S(2)}, u32[]{:S(2)}) %collective-permute-start.30) | collective-permute-done | bytes 67616 | tf_op jit(solution)/shard_map/ppermute | solution.py:35
  171.5 3.5 %shard_map.230 = bf16[16,32,384]{2,1,0:T(8,128)(2,1)} custom-call(bf16[16,2,16,384]{3,2,1,0:T(8,128)(2,1)S(1)} %bitcast.66, bf16[3,2,16,384]{3,2,1,0:T(8,128)(2,1)S(1)} %collective-permute-done.27.top, bf16[3,2,16,384]{3,2,1,0:T(8,128)(2,1)S(1)} %collective-permute-done.28.bottom, bf16[22,2,2,384]{3,2,1,0:T(2,128)(2,1)S(1)} %collective-permute-done.29.left, ...), custom_call_target="tpu_custom_call" | custom-call | tf_op jit(solution)/shard_map/pallas_call | solution.py:407
  (170 shorter events, 56.7 us)
Async XLA Ops:
  7.2 93.4 %all-gather.2.cloned.1.call-start = ((), (), s32[]{:S(2)}) async-start(), calls=%async_computation | async-start | bytes 5013504 | tf_op jit(solution)/shard_map/all_gather | solution.py:480
  8.1 12.9 %collective-permute-start = (bf16[30,768]{1,0:T(8,128)(2,1)S(1)}, bf16[30,768]{1,0:T(8,128)(2,1)S(1)}, u32[]{:S(2)}, u32[]{:S(2)}) collective-permute-start(bf16[30,768]{1,0:T(8,128)(2,1)S(1)} %get-tuple-element.51), channel_id=1, source_target_pairs={{1,0},{2,1},{3,2},{4,3},{5,4},{6,5},{7,6},{0,7},{9,8},{10,9},{11,1... | collective-permute-start | bytes 138248 | tf_op jit(solution)/shard_map/ppermute | solution.py:50
  14.0 9.4 %collective-permute-start.1 = (bf16[30,768]{1,0:T(8,128)(2,1)S(1)}, bf16[30,768]{1,0:T(8,128)(2,1)S(1)}, u32[]{:S(2)}, u32[]{:S(2)}) collective-permute-start(bf16[30,768]{1,0:T(8,128)(2,1)S(1)} %get-tuple-element.51), channel_id=1, source_target_pairs={{2,0},{3,1},{4,2},{5,3},{6,4},{7,5},{0,6},{1,7},{10,8},{11,9},{12,... | collective-permute-start | bytes 138248 | tf_op jit(solution)/shard_map/ppermute | solution.py:50
  15.5 10.0 %collective-permute-start.2 = (bf16[30,768]{1,0:T(8,128)(2,1)S(1)}, bf16[30,768]{1,0:T(8,128)(2,1)S(1)}, u32[]{:S(2)}, u32[]{:S(2)}) collective-permute-start(bf16[30,768]{1,0:T(8,128)(2,1)S(1)} %get-tuple-element.51), channel_id=1, source_target_pairs={{3,0},{4,1},{5,2},{6,3},{7,4},{0,5},{1,6},{2,7},{11,8},{12,9},{13,... | collective-permute-start | bytes 138248 | tf_op jit(solution)/shard_map/ppermute | solution.py:50
  15.9 9.5 %collective-permute-start.3 = (bf16[30,768]{1,0:T(8,128)(2,1)S(1)}, bf16[30,768]{1,0:T(8,128)(2,1)S(1)}, u32[]{:S(2)}, u32[]{:S(2)}) collective-permute-start(bf16[30,768]{1,0:T(8,128)(2,1)S(1)} %get-tuple-element.51), channel_id=1, source_target_pairs={{4,0},{5,1},{6,2},{7,3},{0,4},{1,5},{2,6},{3,7},{12,8},{13,9},{14,... | collective-permute-start | bytes 138248 | tf_op jit(solution)/shard_map/ppermute | solution.py:50
  21.0 8.2 %collective-permute-start.4 = (bf16[30,768]{1,0:T(8,128)(2,1)S(1)}, bf16[30,768]{1,0:T(8,128)(2,1)S(1)}, u32[]{:S(2)}, u32[]{:S(2)}) collective-permute-start(bf16[30,768]{1,0:T(8,128)(2,1)S(1)} %get-tuple-element.51), channel_id=1, source_target_pairs={{5,0},{6,1},{7,2},{0,3},{1,4},{2,5},{3,6},{4,7},{13,8},{14,9},{15,... | collective-permute-start | bytes 138248 | tf_op jit(solution)/shard_map/ppermute | solution.py:50
  21.0 9.8 %collective-permute-start.5 = (bf16[30,768]{1,0:T(8,128)(2,1)S(1)}, bf16[30,768]{1,0:T(8,128)(2,1)S(1)}, u32[]{:S(2)}, u32[]{:S(2)}) collective-permute-start(bf16[30,768]{1,0:T(8,128)(2,1)S(1)} %get-tuple-element.51), channel_id=1, source_target_pairs={{6,0},{7,1},{0,2},{1,3},{2,4},{3,5},{4,6},{5,7},{14,8},{15,9},{8,1... | collective-permute-start | bytes 138248 | tf_op jit(solution)/shard_map/ppermute | solution.py:50
  23.4 7.3 %collective-permute-start.6 = (bf16[30,768]{1,0:T(8,128)(2,1)S(1)}, bf16[30,768]{1,0:T(8,128)(2,1)S(1)}, u32[]{:S(2)}, u32[]{:S(2)}) collective-permute-start(bf16[30,768]{1,0:T(8,128)(2,1)S(1)} %get-tuple-element.51), channel_id=1, source_target_pairs={{7,0},{0,1},{1,2},{2,3},{3,4},{4,5},{5,6},{6,7},{15,8},{8,9},{9,10... | collective-permute-start | bytes 138248 | tf_op jit(solution)/shard_map/ppermute | solution.py:50
  31.8 11.1 %collective-permute-start.13 = (bf16[3,32,384]{2,1,0:T(8,128)(2,1)S(1)}, bf16[3,32,384]{2,1,0:T(8,128)(2,1)S(1)}, u32[]{:S(2)}, u32[]{:S(2)}) collective-permute-start(bf16[3,32,384]{2,1,0:T(8,128)(2,1)S(1)} %get-tuple-element.59), channel_id=1, source_target_pairs={{0,8},{8,16},{16,24},{24,32},{32,40},{40,48},{48,56},{56,64},{64,7... | collective-permute-start | bytes 221192 | tf_op jit(solution)/shard_map/ppermute | solution.py:15
  35.3 7.6 %collective-permute-start.14 = (bf16[3,32,384]{2,1,0:T(8,128)(2,1)S(1)}, bf16[3,32,384]{2,1,0:T(8,128)(2,1)S(1)}, u32[]{:S(2)}, u32[]{:S(2)}) collective-permute-start(bf16[3,32,384]{2,1,0:T(8,128)(2,1)S(1)} %get-tuple-element.58), channel_id=1, source_target_pairs={{8,0},{16,8},{24,16},{32,24},{40,32},{48,40},{56,48},{64,56},{72,6... | collective-permute-start | bytes 221192 | tf_op jit(solution)/shard_map/ppermute | solution.py:18
  48.1 13.8 %collective-permute-start.10 = (bf16[192,768]{1,0:T(8,128)(2,1)S(1)}, bf16[192,768]{1,0:T(8,128)(2,1)S(1)}, u32[]{:S(2)}, u32[]{:S(2)}) collective-permute-start(bf16[192,768]{1,0:T(8,128)(2,1)S(1)} %bitcast.69), channel_id=1, source_target_pairs={{32,0},{40,8},{48,16},{56,24},{64,32},{72,40},{80,48},{88,56},{96,... | collective-permute-start | bytes 884744 | tf_op jit(solution)/shard_map/ppermute | solution.py:50
  48.7 8.1 %collective-permute-start.15 = (bf16[22,3,384]{2,1,0:T(4,128)(2,1)S(1)}, bf16[22,3,384]{2,1,0:T(4,128)(2,1)S(1)}, u32[]{:S(2)}, u32[]{:S(2)}) collective-permute-start(bf16[22,3,384]{2,1,0:T(4,128)(2,1)S(1)} %pad_maximum_fusion.5), channel_id=1, source_target_pairs={{0,1},{1,2},{2,3},{3,4},{4,5},{5,6},{6,7},{8,9},{9,10},{10,11},{11... | collective-permute-start | bytes 152072 | tf_op jit(solution)/shard_map/ppermute | solution.py:34
  52.3 12.0 %collective-permute-start.11 = (bf16[192,768]{1,0:T(8,128)(2,1)S(1)}, bf16[192,768]{1,0:T(8,128)(2,1)S(1)}, u32[]{:S(2)}, u32[]{:S(2)}) collective-permute-start(bf16[192,768]{1,0:T(8,128)(2,1)S(1)} %bitcast.70), channel_id=1, source_target_pairs={{64,0},{72,8},{80,16},{88,24},{96,32},{104,40},{112,48},{120,56},{... | collective-permute-start | bytes 884744 | tf_op jit(solution)/shard_map/ppermute | solution.py:50
  54.8 11.7 %collective-permute-start.12 = (bf16[192,768]{1,0:T(8,128)(2,1)S(1)}, bf16[192,768]{1,0:T(8,128)(2,1)S(1)}, u32[]{:S(2)}, u32[]{:S(2)}) collective-permute-start(bf16[192,768]{1,0:T(8,128)(2,1)S(1)} %bitcast.71), channel_id=1, source_target_pairs={{96,0},{104,8},{112,16},{120,24},{0,32},{8,40},{16,48},{24,56},{32... | collective-permute-start | bytes 884744 | tf_op jit(solution)/shard_map/ppermute | solution.py:50
  74.3 12.0 %collective-permute-start.18 = (bf16[3,16,768]{2,1,0:T(8,128)(2,1)S(1)}, bf16[3,16,768]{2,1,0:T(8,128)(2,1)S(1)}, u32[]{:S(2)}, u32[]{:S(2)}) collective-permute-start(bf16[3,16,768]{2,1,0:T(8,128)(2,1)S(1)} %bitcast.74), channel_id=1, source_target_pairs={{0,8},{8,16},{16,24},{24,32},{32,40},{40,48},{48,56},{56,64},{64,7... | collective-permute-start | bytes 221192 | tf_op jit(solution)/shard_map/ppermute | solution.py:15
  77.3 9.0 %collective-permute-start.19 = (bf16[3,16,768]{2,1,0:T(8,128)(2,1)S(1)}, bf16[3,16,768]{2,1,0:T(8,128)(2,1)S(1)}, u32[]{:S(2)}, u32[]{:S(2)}) collective-permute-start(bf16[3,16,768]{2,1,0:T(8,128)(2,1)S(1)} %bitcast.77), channel_id=1, source_target_pairs={{8,0},{16,8},{24,16},{32,24},{40,32},{48,40},{56,48},{64,56},{72,6... | collective-permute-start | bytes 221192 | tf_op jit(solution)/shard_map/ppermute | solution.py:18
  86.5 6.8 %collective-permute-start.20 = (bf16[14,3,768]{2,1,0:T(4,128)(2,1)S(1)}, bf16[14,3,768]{2,1,0:T(4,128)(2,1)S(1)}, u32[]{:S(2)}, u32[]{:S(2)}) collective-permute-start(bf16[14,3,768]{2,1,0:T(4,128)(2,1)S(1)} %pad_maximum_fusion.1), channel_id=1, source_target_pairs={{0,1},{1,2},{2,3},{3,4},{4,5},{5,6},{6,7},{8,9},{9,10},{10,11},{11... | collective-permute-start | bytes 193544 | tf_op jit(solution)/shard_map/ppermute | solution.py:34
  100.6 8.1 %collective-permute-start.22 = (bf16[1536,1536]{1,0:T(8,128)(2,1)}, bf16[1536,1536]{1,0:T(8,128)(2,1)S(1)}, u32[]{:S(2)}, u32[]{:S(2)}) collective-permute-start(bf16[1536,1536]{1,0:T(8,128)(2,1)} %all-gather.2.cloned.1.call-done.weights), channel_id=1, source_target_pairs={{0,128},{128,0},{1,129},{129,1},{2,130},{130,2},{3,131},{131,3},{4... | collective-permute-start | bytes 14155784 | tf_op jit(solution)/shard_map/ppermute | solution.py:551
  118.1 10.4 %collective-permute-start.23 = (bf16[3,16,768]{2,1,0:T(8,128)(2,1)S(1)}, bf16[3,16,768]{2,1,0:T(8,128)(2,1)S(1)}, u32[]{:S(2)}, u32[]{:S(2)}) collective-permute-start(bf16[3,16,768]{2,1,0:T(8,128)(2,1)S(1)} %bitcast.75), channel_id=1, source_target_pairs={{0,8},{8,16},{16,24},{24,32},{32,40},{40,48},{48,56},{56,64},{64,7... | collective-permute-start | bytes 221192 | tf_op jit(solution)/shard_map/ppermute | solution.py:15
  120.2 8.4 %collective-permute-start.24 = (bf16[3,16,768]{2,1,0:T(8,128)(2,1)S(1)}, bf16[3,16,768]{2,1,0:T(8,128)(2,1)S(1)}, u32[]{:S(2)}, u32[]{:S(2)}) collective-permute-start(bf16[3,16,768]{2,1,0:T(8,128)(2,1)S(1)} %bitcast.78), channel_id=1, source_target_pairs={{8,0},{16,8},{24,16},{32,24},{40,32},{48,40},{56,48},{64,56},{72,6... | collective-permute-start | bytes 221192 | tf_op jit(solution)/shard_map/ppermute | solution.py:18
  128.7 7.1 %collective-permute-start.25 = (bf16[14,3,768]{2,1,0:T(4,128)(2,1)S(1)}, bf16[14,3,768]{2,1,0:T(4,128)(2,1)S(1)}, u32[]{:S(2)}, u32[]{:S(2)}) collective-permute-start(bf16[14,3,768]{2,1,0:T(4,128)(2,1)S(1)} %pad_maximum_fusion.3), channel_id=1, source_target_pairs={{0,1},{1,2},{2,3},{3,4},{4,5},{5,6},{6,7},{8,9},{9,10},{10,11},{11... | collective-permute-start | bytes 193544 | tf_op jit(solution)/shard_map/ppermute | solution.py:34
  149.7 10.3 %collective-permute-start.27 = (bf16[3,2,16,384]{3,2,1,0:T(8,128)(2,1)S(1)}, bf16[3,2,16,384]{3,2,1,0:T(8,128)(2,1)S(1)}, u32[]{:S(2)}, u32[]{:S(2)}) collective-permute-start(bf16[3,2,16,384]{3,2,1,0:T(8,128)(2,1)S(1)} %bitcast.76), channel_id=1, source_target_pairs={{0,8},{8,16},{16,24},{24,32},{32,40},{40,48},{48,56},{56,64},{64,7... | collective-permute-start | bytes 221192 | tf_op jit(solution)/shard_map/ppermute | solution.py:15
  153.3 6.6 %collective-permute-start.28 = (bf16[3,2,16,384]{3,2,1,0:T(8,128)(2,1)S(1)}, bf16[3,2,16,384]{3,2,1,0:T(8,128)(2,1)S(1)}, u32[]{:S(2)}, u32[]{:S(2)}) collective-permute-start(bf16[3,2,16,384]{3,2,1,0:T(8,128)(2,1)S(1)} %bitcast.79), channel_id=1, source_target_pairs={{8,0},{16,8},{24,16},{32,24},{40,32},{48,40},{56,48},{64,56},{72,6... | collective-permute-start | bytes 221192 | tf_op jit(solution)/shard_map/ppermute | solution.py:18
  160.1 7.0 %collective-permute-start.29 = (bf16[22,2,2,384]{3,2,1,0:T(2,128)(2,1)S(1)}, bf16[22,2,2,384]{3,2,1,0:T(2,128)(2,1)S(1)}, u32[]{:S(2)}, u32[]{:S(2)}) collective-permute-start(bf16[22,2,2,384]{3,2,1,0:T(2,128)(2,1)S(1)} %pad_maximum_fusion.7), channel_id=1, source_target_pairs={{0,1},{1,2},{2,3},{3,4},{4,5},{5,6},{6,7},{8,9},{9,10},{10,11},{11... | collective-permute-start | bytes 202760 | tf_op jit(solution)/shard_map/ppermute | solution.py:34
  (34 other events, 391.3 us)
Sparse Core Ops, SparseCore 0:
  31.9 65.6 all-gather.1

commit v3 on v2

--- a/solution.py
+++ b/solution.py
@@ -202,7 +202,9 @@
     lax.fori_loop(0, channels // lanes, step, 0)
 
 
-def conv_two_kernel(tile_ref, top, bottom, left, right, taps, gain, shift, normed, conv, frame):
+def conv_two_kernel(
+    tile_ref, top, bottom, left, right, taps, gain, shift, grad, scale, mine, conv, frame
+):
     rows, width, channels = tile_ref.shape
     fill_rows(frame, top, 0, width)
     fill_rows(frame, tile_ref, 3, width)
@@ -217,7 +219,9 @@
         return carry
 
     lax.fori_loop(0, channels // lanes, step, 0)
-    norm_rows(conv, normed, gain, shift, 64)
+    norm_rows(conv, mine, gain, shift, 32)
+    count = rows * width
+    mine[count:, :] = (grad[...].astype(jnp.float32) * scale[...]).astype(mine.dtype)
 
 
 def back_two_kernel(tile_ref, top, bottom, left, right, taps, grad, out, frame):
@@ -248,22 +252,28 @@
     return [slice(first, first + size) for first in range(0, total, size)]
 
 
-def over_hidden(weights, step):
+hidden_block = 256
+
+
+def over_hidden(weights, step, together=1):
     total = weights.shape[0]
-    block = min(total, 256)
+    block = min(total, hidden_block)
+    together = min(together, total // block)
 
     def run(index, carry):
-        step(pl.ds(pl.multiple_of(index * block, block), block))
-        return carry
-
-    lax.fori_loop(0, total // block, run, 0)
+        for part in range(together):
+            place = index * together + part
+            step(place, pl.ds(pl.multiple_of(place * block, block), block))
+        return carry
+
+    lax.fori_loop(0, total // block // together, run, 0)
 
 
 def mlp_one_half(normed, weights, bias, branch):
     width = normed.shape[1]
     branch[...] = jnp.zeros_like(branch)
 
-    def step(units):
+    def step(place, units):
         for rows in row_blocks(normed.shape[0], 256):
             pre_act = contract_last(normed[rows, :], weights[units, :width]) + bias[:, units]
             hidden = (pre_act * normal_cdf(pre_act)).astype(jnp.bfloat16)
@@ -304,14 +314,16 @@
 def slope_one_kernel(normed, own, other, bias_own, bias_other, slope_own, slope_other):
     width = normed.shape[1]
 
-    def step(units):
+    def step(place, units):
         for rows in row_blocks(normed.shape[0], 256):
             for weights, bias, slope in (
                 (own, bias_own, slope_own),
                 (other, bias_other, slope_other),
             ):
                 pre_act = contract_last(normed[rows, :], weights[units, :width]) + bias[:, units]
-                slope[rows, units] = slope_from(pre_act, normal_cdf(pre_act)).astype(slope.dtype)
+                slope[place, rows, :] = slope_from(pre_act, normal_cdf(pre_act)).astype(
+                    slope.dtype
+                )
 
     over_hidden(own, step)
 
@@ -328,25 +340,27 @@
         d_normal = contract_last(d_merged[...], merge[place * width : (place + 1) * width, :])
         for group in range(groups):
             first = (4 * group + place) * half_cols
-            rows = slice(first, first + half_cols)
-            values = section[rows, :].astype(jnp.float32)
-            scaled, inv_std, _ = norm_forward(values, 1.0, 0.0)
-            flow = norm_backward(
-                d_normal[group * half_cols : (group + 1) * half_cols],
-                scaled,
-                inv_std,
-                gain_mid[...],
-            )
-            upstream[rows, :] = flow
-            d_branch[rows, :] = (flow * scale[...]).astype(d_branch.dtype)
+            d_normed[first : first + half_cols, :] = d_normal[
+                group * half_cols : (group + 1) * half_cols
+            ]
+
+    def norm_step(index, carry):
+        rows = pl.ds(pl.multiple_of(index * 64, 64), 64)
+        scaled, inv_std, _ = norm_forward(section[rows, :].astype(jnp.float32), 1.0, 0.0)
+        flow = norm_backward(d_normed[rows, :], scaled, inv_std, gain_mid[...])
+        upstream[rows, :] = flow
+        d_branch[rows, :] = (flow * scale[...]).astype(d_branch.dtype)
+        return carry
+
+    lax.fori_loop(0, groups, norm_step, 0)
     d_normed[...] = jnp.zeros_like(d_normed)
 
-    def step(units):
+    def step(place, units):
         for rows in row_blocks(section.shape[0], 256):
             total = d_normed[rows, :]
             for weights, slope in ((own, slope_own), (other, slope_other)):
                 d_hidden = contract_last(d_branch[rows, :], weights[units, width:])
-                d_pre = (d_hidden * slope[rows, units].astype(jnp.float32)).astype(jnp.bfloat16)
+                d_pre = (d_hidden * slope[place, rows, :].astype(jnp.float32)).astype(jnp.bfloat16)
                 total = total + dot(d_pre, weights[units, :width])
             d_normed[rows, :] = total
 
@@ -365,34 +379,46 @@
     lax.fori_loop(0, conv.shape[0] // chunk, step, 0)
 
 
-def mlp_two_half(normed, grad, scale, weights, bias, branch, d_normed, d_branch):
-    width = normed.shape[1]
-    branch[...] = jnp.zeros_like(branch)
-    d_normed[...] = jnp.zeros_like(d_normed)
-    d_branch[...] = (grad[...].astype(jnp.float32) * scale[...]).astype(d_branch.dtype)
-
-    def step(units):
-        pre_act = contract_last(normed[...], weights[units, :width]) + bias[:, units]
-        d_hidden = contract_last(d_branch[...], weights[units, width:])
+def mlp_two_kernel(mine, theirs, weights, bias, keep, send, stacked, d_stacked):
+    count = mine.shape[0] // 2
+    width = mine.shape[1]
+    for first, source in ((0, mine), (count, theirs)):
+        stacked[first : first + count, :] = source[:count, :]
+        d_stacked[first : first + count, :] = source[count:, :]
+    keep[...] = jnp.zeros_like(keep)
+    send[...] = jnp.zeros_like(send)
+
+    def step(place, units):
+        pre_act = contract_last(stacked[...], weights[units, :width]) + bias[:, units]
+        d_hidden = contract_last(d_stacked[...], weights[units, width:])
         cdf = normal_cdf(pre_act)
         hidden = (pre_act * cdf).astype(jnp.bfloat16)
         d_pre = (d_hidden * slope_from(pre_act, cdf)).astype(jnp.bfloat16)
-        branch[...] += dot(hidden, weights[units, width:])
-        d_normed[...] += dot(d_pre, weights[units, :width])
-
-    over_hidden(weights, step)
-
-
-def mlp_two_finish(
-    normed, grad, scale, weights, bias, partial, d_partial, merged, down_bias, conv, gain,
-    features, d_conv, branch, d_normed, d_branch,
-):
-    mlp_two_half(normed, grad, scale, weights, bias, branch, d_normed, d_branch)
-    total = branch[...] + partial[...] + down_bias[...]
-    out = merged[...].astype(jnp.float32) + scale[...] * total
-    features[...] = out.astype(features.dtype)
-    d_normed[...] += d_partial[...]
-    norm_back_rows(conv, d_normed, gain, d_conv, 64)
+        branch = dot(hidden, weights[units, width:])
+        d_normed = dot(d_pre, weights[units, :width])
+        keep[:count, :] += branch[:count]
+        send[:count, :] += branch[count:]
+        keep[count:, :] += d_normed[:count]
+        send[count:, :] += d_normed[count:]
+
+    over_hidden(weights, step, 2)
+
+
+def two_finish_kernel(keep, back, merged, scale, down_bias, conv, gain, features, d_conv):
+    count = merged.shape[0]
+
+    def step(index, carry):
+        rows = pl.ds(pl.multiple_of(index * 32, 32), 32)
+        low = pl.ds(pl.multiple_of(count + index * 32, 32), 32)
+        total = keep[rows, :] + back[rows, :] + down_bias[...]
+        out = merged[rows, :].astype(jnp.float32) + scale[...] * total
+        features[rows, :] = out.astype(features.dtype)
+        scaled, inv_std, _ = norm_forward(conv[rows, :].astype(jnp.float32), 1.0, 0.0)
+        flow = norm_backward(keep[low, :] + back[low, :], scaled, inv_std, gain[...])
+        d_conv[rows, :] = flow.astype(d_conv.dtype)
+        return carry
+
+    lax.fori_loop(0, count // 32, step, 0)
 
 
 megabyte = 1024 * 1024
@@ -496,9 +522,20 @@
         width_one,
         (image_tile, *halo_of(image_tile, 3), kernel_one, gain_one[None], shift_one[None]),
     )
-    own_one, normed_one, images_par, bias_one, bias_two = lax.optimization_barrier(
-        (own_one, normed_one, images_par, bias_one, bias_two)
-    )
+    flat = tuple(
+        vector[None]
+        for vector in (
+            down_bias_one, scale_one, gain_mid, shift_mid, merge_bias, gain_two, shift_two,
+            scale_two, down_bias_two, gain_one,
+        )
+    )
+    own_one, normed_one, images_par, bias_one, bias_two, flat = lax.optimization_barrier(
+        (own_one, normed_one, images_par, bias_one, bias_two, flat)
+    )
+    (
+        flat_down_one, flat_scale_one, flat_gain_mid, flat_shift_mid, flat_merge_bias,
+        flat_gain_two, flat_shift_two, flat_scale_two, flat_down_two, flat_gain_one,
+    ) = flat
     other_one = lax.ppermute(own_one, "sec", swap)
 
     (partial_one,) = block_call(
@@ -516,66 +553,60 @@
             bias_one[1],
             partial_one,
             images_par,
-            down_bias_one[None],
-            scale_one[None],
-            gain_mid[None],
-            shift_mid[None],
+            flat_down_one,
+            flat_scale_one,
+            flat_gain_mid,
+            flat_shift_mid,
             merge_weight,
-            merge_bias[None],
+            flat_merge_bias,
         ),
         [
             pltpu.VMEM((rows_one, width_one), jnp.float32),
             pltpu.VMEM((micro_count * half_rows, 4, half_cols, width_one), bfloat),
         ],
     )
+    block = min(own_one.shape[0], hidden_block)
+    slope_dims = (own_one.shape[0] // block, rows_one, block)
     slope_own, slope_other = block_call(
         slope_one_kernel,
-        (
-            shape_of((rows_one, own_one.shape[0]), bfloat),
-            shape_of((rows_one, own_one.shape[0]), bfloat),
-        ),
+        (shape_of(slope_dims, bfloat), shape_of(slope_dims, bfloat)),
         (normed_one, own_one, other_one, *bias_one),
         [],
     )
 
     merged_tile = merged.reshape(half_rows, half_cols, width_two)
-    normed_two, conv_two = tile_call(
+    grad_rows = grad_out.reshape(rows_two, width_two)
+    mine, conv_two = tile_call(
         conv_two_kernel,
-        (shape_of((rows_two, width_two), bfloat), shape_of((rows_two, width_two), bfloat)),
+        (shape_of((2 * rows_two, width_two), bfloat), shape_of((rows_two, width_two), bfloat)),
         half_rows,
         half_cols,
         width_two,
-        (merged_tile, *halo_of(merged_tile, 3), kernel_two, gain_two[None], shift_two[None]),
-    )
-    own_two, normed_two = lax.optimization_barrier((own_two, normed_two))
-    other_two = lax.ppermute(own_two, "sec", swap)
-    grad_rows = grad_out.reshape(rows_two, width_two)
-    two_wide = shape_of((rows_two, width_two), jnp.float32)
-    two_scratch = pltpu.VMEM((rows_two, width_two), jnp.float32)
-    two_branch = pltpu.VMEM((rows_two, width_two), bfloat)
-    partial_two, d_partial_two = block_call(
-        mlp_two_half,
-        (two_wide, two_wide),
-        (normed_two, grad_rows, scale_two[None], own_two, bias_two[0]),
-        [two_branch],
-    )
+        (
+            merged_tile,
+            *halo_of(merged_tile, 3),
+            kernel_two,
+            flat_gain_two,
+            flat_shift_two,
+            grad_rows,
+            flat_scale_two,
+        ),
+    )
+    mine, own_two = lax.optimization_barrier((mine, own_two))
+    theirs = lax.ppermute(mine, "sec", swap)
+    both_dims = (2 * rows_two, width_two)
+    keep, send = block_call(
+        mlp_two_kernel,
+        (shape_of(both_dims, jnp.float32), shape_of(both_dims, jnp.float32)),
+        (mine, theirs, own_two, bias_two[0]),
+        [pltpu.VMEM(both_dims, bfloat), pltpu.VMEM(both_dims, bfloat)],
+    )
+    back = lax.ppermute(send, "sec", swap)
     features, d_conv_two = block_call(
-        mlp_two_finish,
+        two_finish_kernel,
         (shape_of((rows_two, width_two), bfloat), shape_of((rows_two, width_two), bfloat)),
-        (
-            normed_two,
-            grad_rows,
-            scale_two[None],
-            other_two,
-            bias_two[1],
-            partial_two,
-            d_partial_two,
-            merged,
-            down_bias_two[None],
-            conv_two,
-            gain_two[None],
-        ),
-        [two_scratch, two_scratch, two_branch],
+        (keep, back, merged, flat_scale_two, flat_down_two, conv_two, flat_gain_two),
+        [],
     )
     back_tile = d_conv_two.reshape(half_rows, half_cols, width_two)
     (d_merged,) = tile_call(
@@ -593,14 +624,14 @@
             d_merged,
             merge_weight,
             section_out,
-            gain_mid[None],
-            scale_one[None],
+            flat_gain_mid,
+            flat_scale_one,
             own_one,
             other_one,
             slope_own,
             slope_other,
             conv_one,
-            gain_one[None],
+            flat_gain_one,
         ),
         [
             pltpu.VMEM((rows_one, width_one), bfloat),

time: 184 us -> 188 us (1.022)
  waiting for transfers between devices: 36.5 us -> 42.9 us
  local copies, waits for them, and re-layouts: 7.69 us -> 4.32 us
    ppermute x4, waiting for transfers between devices: 0.01 us -> 3.92 us  [exchange(): lax.ppermute(lax.slice_in_dim(block, block.shape[dim] - width, None, axis...]
    ppermute x1 -> x2, waiting for transfers between devices: 0.58 us -> 4.08 us  [the longest x1 2.15 us: on_device(): back = lax.ppermute(send, 'sec', swap)]
    ppermute x4, waiting for transfers between devices: 7.62 us -> 4.52 us  [exchange(): lax.ppermute(lax.slice_in_dim(block, 0, width, axis=dim), axis, backward)]
    ppermute x4, waiting for transfers between devices: 12.1 us -> 14.6 us  [halo_of(): right = lax.ppermute(edge(0, width), 'col', backward)]
    unnamed x52 -> x54, local copies, waits for them, and re-layouts: 5.33 us -> 3.32 us
  transfers between devices with their start and end apart: 32 -> 33, of which waited for: 18 -> 20; matrix products, arithmetic and copies ran while one was open for 1% -> 1% of each run, Pallas kernels for 11% -> 9%
where the time goes in v3:
time: 188 us; the launch traced here: 185 us
  starting transfers between devices  79.5 us (42%)
  waiting for transfers between devices  42.9 us (23%)
  Pallas kernels  41.1 us (22%)
  between operations  15.3 us (8%)
  local copies, waits for them, and re-layouts  4.32 us (2%)
  other arithmetic  2.16 us (1%)
    pallas_call x10, Pallas kernels, block_call(): pl.pallas_call(kernel, out_shape=outputs, in_specs=[whole] * len(operands...  41.1 us
    ppermute x13, starting transfers between devices, ring_collect(): arrived = lax.ppermute(piece, axis, pairs)  25.7 us
    ppermute x4, starting transfers between devices, exchange(): lax.ppermute(lax.slice_in_dim(block, 0, width, axis=dim), axis, backward)  21.9 us
    ppermute x4, starting transfers between devices, halo_of(): left = lax.ppermute(edge(extent - width, extent), 'col', forward)  15.5 us
    ppermute x4, waiting for transfers between devices, halo_of(): right = lax.ppermute(edge(0, width), 'col', backward)  14.6 us
    ppermute x13, waiting for transfers between devices, ring_collect(): arrived = lax.ppermute(piece, axis, pairs)  14.4 us
    ppermute x4, starting transfers between devices, exchange(): lax.ppermute(lax.slice_in_dim(block, block.shape[dim] - width, None, axis...  10.9 us
    ppermute x4, starting transfers between devices, halo_of(): right = lax.ppermute(edge(0, width), 'col', backward)  5.17 us
  transfers between devices with their start and end apart: 33, of which 20 were waited for; matrix products, arithmetic and copies ran while one was open for 1% of the time, Pallas kernels for 9%

profile of v3, /device:TPU:2, one launch (start us, length us, event | category | flops | bytes accessed | tf_op | source)
XLA Modules:
  0.0 185.3 jit_solution(6007234272225626447)
XLA Ops:
  8.1 5.9 %collective-permute-start = (bf16[30,768]{1,0:T(8,128)(2,1)S(1)}, bf16[30,768]{1,0:T(8,128)(2,1)S(1)}, u32[]{:S(2)}, u32[]{:S(2)}) collective-permute-start(bf16[30,768]{1,0:T(8,128)(2,1)S(1)} %get-tuple-element.69), channel_id=1, source_target_pairs={{1,0},{2,1},{3,2},{4,3},{5,4},{6,5},{7,6},{0,7},{9,8},{10,9},{11,1... | collective-permute-start | bytes 138248 | tf_op jit(solution)/shard_map/ppermute | solution.py:50
  14.0 3.4 %collective-permute-start.4 = (bf16[30,768]{1,0:T(8,128)(2,1)S(1)}, bf16[30,768]{1,0:T(8,128)(2,1)S(1)}, u32[]{:S(2)}, u32[]{:S(2)}) collective-permute-start(bf16[30,768]{1,0:T(8,128)(2,1)S(1)} %get-tuple-element.69), channel_id=1, source_target_pairs={{5,0},{6,1},{7,2},{0,3},{1,4},{2,5},{3,6},{4,7},{13,8},{14,9},{15,... | collective-permute-start | bytes 138248 | tf_op jit(solution)/shard_map/ppermute | solution.py:50
  18.3 4.6 %collective-permute-start.2 = (bf16[30,768]{1,0:T(8,128)(2,1)S(1)}, bf16[30,768]{1,0:T(8,128)(2,1)S(1)}, u32[]{:S(2)}, u32[]{:S(2)}) collective-permute-start(bf16[30,768]{1,0:T(8,128)(2,1)S(1)} %get-tuple-element.69), channel_id=1, source_target_pairs={{3,0},{4,1},{5,2},{6,3},{7,4},{0,5},{1,6},{2,7},{11,8},{12,9},{13,... | collective-permute-start | bytes 138248 | tf_op jit(solution)/shard_map/ppermute | solution.py:50
  24.6 4.7 %collective-permute-done.1 = bf16[30,768]{1,0:T(8,128)(2,1)S(1)} collective-permute-done((bf16[30,768]{1,0:T(8,128)(2,1)S(1)}, bf16[30,768]{1,0:T(8,128)(2,1)S(1)}, u32[]{:S(2)}, u32[]{:S(2)}) %collective-permute-start.1) | collective-permute-done | bytes 46112 | tf_op jit(solution)/shard_map/ppermute | solution.py:50
  29.4 5.2 %collective-permute-done.6 = bf16[30,768]{1,0:T(8,128)(2,1)S(1)} collective-permute-done((bf16[30,768]{1,0:T(8,128)(2,1)S(1)}, bf16[30,768]{1,0:T(8,128)(2,1)S(1)}, u32[]{:S(2)}, u32[]{:S(2)}) %collective-permute-start.6) | collective-permute-done | bytes 46112 | tf_op jit(solution)/shard_map/ppermute | solution.py:50
  35.7 4.9 %collective-permute-start.14 = (bf16[3,32,384]{2,1,0:T(8,128)(2,1)S(1)}, bf16[3,32,384]{2,1,0:T(8,128)(2,1)S(1)}, u32[]{:S(2)}, u32[]{:S(2)}) collective-permute-start(bf16[3,32,384]{2,1,0:T(8,128)(2,1)S(1)} %get-tuple-element.78), channel_id=1, source_target_pairs={{8,0},{16,8},{24,16},{32,24},{40,32},{48,40},{56,48},{64,56},{72,6... | collective-permute-start | bytes 221192 | tf_op jit(solution)/shard_map/ppermute | solution.py:18
  43.9 5.0 %collective-permute-start.8 = (bf16[48,768]{1,0:T(8,128)(2,1)S(1)}, bf16[48,768]{1,0:T(8,128)(2,1)S(1)}, u32[]{:S(2)}, u32[]{:S(2)}) collective-permute-start(bf16[48,768]{1,0:T(8,128)(2,1)S(1)} %reshape.63), channel_id=1, source_target_pairs={{16,0},{24,8},{0,16},{8,24},{48,32},{56,40},{32,48},{40,56},{80,64... | collective-permute-start | bytes 221192 | tf_op jit(solution)/shard_map/ppermute | solution.py:50
  49.5 3.7 %collective-permute-done.7 = bf16[48,768]{1,0:T(8,128)(2,1)S(1)} collective-permute-done((bf16[48,768]{1,0:T(8,128)(2,1)S(1)}, bf16[48,768]{1,0:T(8,128)(2,1)S(1)}, u32[]{:S(2)}, u32[]{:S(2)}) %collective-permute-start.7) | collective-permute-done | bytes 73760 | tf_op jit(solution)/shard_map/ppermute | solution.py:50
  63.2 4.7 %shard_map.221 = (bf16[512,384]{1,0:T(8,128)(2,1)S(1)}, f32[512,384]{1,0:T(8,128)S(1)}, bf16[512,384]{1,0:T(8,128)(2,1)S(1)}) custom-call(bf16[16,32,384]{2,1,0:T(8,128)(2,1)S(1)} %bitcast.61, bf16[3,32,384]{2,1,0:T(8,128)(2,1)S(1)} %collective-permute-done.13.top, bf16[3,32,384]{2,1,0:T(8,128)(2,1)S(1)} %collective-permute-done.14.bottom, ...), custom_call_target="tpu_custom_call" | custom-call | tf_op jit(solution)/shard_map/pallas_call | solution.py:433
  71.7 4.7 %shard_map.223 = (bf16[512,384]{1,0:T(8,128)(2,1)S(1)}, bf16[128,768]{1,0:T(8,128)(2,1)S(1)}) custom-call(bf16[512,384]{1,0:T(8,128)(2,1)S(1)} %get-tuple-element.37.normed, bf16[768,768]{1,0:T(8,128)(2,1)S(1)} %collective-permute-done.17.weights.other, f32[1,768]{1,0:T(1,128)S(1)} %select_n.192.bias.bias_other, f32[512,384]{1,0:T(8,128)S(1)} %shard_map.222.partial, ...), custom_call_target="tpu_custom_call" | custom-call | tf_op jit(solution)/shard_map/pallas_call | solution.py:433
  77.2 2.9 %collective-permute-start.18 = (bf16[3,16,768]{2,1,0:T(8,128)(2,1)S(1)}, bf16[3,16,768]{2,1,0:T(8,128)(2,1)S(1)}, u32[]{:S(2)}, u32[]{:S(2)}) collective-permute-start(bf16[3,16,768]{2,1,0:T(8,128)(2,1)S(1)} %bitcast.76), channel_id=1, source_target_pairs={{0,8},{8,16},{16,24},{24,32},{32,40},{40,48},{48,56},{56,64},{64,7... | collective-permute-start | bytes 221192 | tf_op jit(solution)/shard_map/ppermute | solution.py:15
  80.1 6.3 %collective-permute-start.19 = (bf16[3,16,768]{2,1,0:T(8,128)(2,1)S(1)}, bf16[3,16,768]{2,1,0:T(8,128)(2,1)S(1)}, u32[]{:S(2)}, u32[]{:S(2)}) collective-permute-start(bf16[3,16,768]{2,1,0:T(8,128)(2,1)S(1)} %bitcast.73), channel_id=1, source_target_pairs={{8,0},{16,8},{24,16},{32,24},{40,32},{48,40},{56,48},{64,56},{72,6... | collective-permute-start | bytes 221192 | tf_op jit(solution)/shard_map/ppermute | solution.py:18
  90.5 3.8 %collective-permute-start.20 = (bf16[14,3,768]{2,1,0:T(4,128)(2,1)S(1)}, bf16[14,3,768]{2,1,0:T(4,128)(2,1)S(1)}, u32[]{:S(2)}, u32[]{:S(2)}) collective-permute-start(bf16[14,3,768]{2,1,0:T(4,128)(2,1)S(1)} %pad_maximum_fusion.1), channel_id=1, source_target_pairs={{0,1},{1,2},{2,3},{3,4},{4,5},{5,6},{6,7},{8,9},{9,10},{10,11},{11... | collective-permute-start | bytes 193544 | tf_op jit(solution)/shard_map/ppermute | solution.py:34
  96.4 4.4 %collective-permute-done.21.right = bf16[14,3,768]{2,1,0:T(4,128)(2,1)S(1)} collective-permute-done((bf16[14,3,768]{2,1,0:T(4,128)(2,1)S(1)}, bf16[14,3,768]{2,1,0:T(4,128)(2,1)S(1)}, u32[]{:S(2)}, u32[]{:S(2)}) %collective-permute-start.21) | collective-permute-done | bytes 64544 | tf_op jit(solution)/shard_map/ppermute | solution.py:35
  107.9 6.4 %shard_map.225 = (f32[256,768]{1,0:T(8,128)S(1)}, f32[256,768]{1,0:T(8,128)S(1)}) custom-call(bf16[256,768]{1,0:T(8,128)(2,1)S(1)} %copy-done.10, bf16[256,768]{1,0:T(8,128)(2,1)S(1)} %collective-permute-done.22.theirs, bf16[1536,1536]{1,0:T(8,128)(2,1)} %all-gather.2.cloned.1.call-done.weights, f32[1,1536]{1,0:T(1,128)S(1)} %select_n.195.bias), custom_call_target="tpu_custom_call" | custom-call | tf_op jit(solution)/shard_map/pallas_call | solution.py:433
  120.3 6.5 %collective-permute-start.25 = (bf16[3,16,768]{2,1,0:T(8,128)(2,1)S(1)}, bf16[3,16,768]{2,1,0:T(8,128)(2,1)S(1)}, u32[]{:S(2)}, u32[]{:S(2)}) collective-permute-start(bf16[3,16,768]{2,1,0:T(8,128)(2,1)S(1)} %bitcast.74), channel_id=1, source_target_pairs={{8,0},{16,8},{24,16},{32,24},{40,32},{48,40},{56,48},{64,56},{72,6... | collective-permute-start | bytes 221192 | tf_op jit(solution)/shard_map/ppermute | solution.py:18
  128.9 3.8 %collective-permute-start.26 = (bf16[14,3,768]{2,1,0:T(4,128)(2,1)S(1)}, bf16[14,3,768]{2,1,0:T(4,128)(2,1)S(1)}, u32[]{:S(2)}, u32[]{:S(2)}) collective-permute-start(bf16[14,3,768]{2,1,0:T(4,128)(2,1)S(1)} %pad_maximum_fusion.3), channel_id=1, source_target_pairs={{0,1},{1,2},{2,3},{3,4},{4,5},{5,6},{6,7},{8,9},{9,10},{10,11},{11... | collective-permute-start | bytes 193544 | tf_op jit(solution)/shard_map/ppermute | solution.py:34
  136.2 3.9 %collective-permute-done.27.right = bf16[14,3,768]{2,1,0:T(4,128)(2,1)S(1)} collective-permute-done((bf16[14,3,768]{2,1,0:T(4,128)(2,1)S(1)}, bf16[14,3,768]{2,1,0:T(4,128)(2,1)S(1)}, u32[]{:S(2)}, u32[]{:S(2)}) %collective-permute-start.27) | collective-permute-done | bytes 64544 | tf_op jit(solution)/shard_map/ppermute | solution.py:35
  141.8 11.1 %shard_map.229 = (bf16[512,384]{1,0:T(8,128)(2,1)S(1)}, f32[512,384]{1,0:T(8,128)S(1)}) custom-call(bf16[128,768]{1,0:T(8,128)(2,1)S(1)} %shard_map.227.d_merged, bf16[1536,768]{1,0:T(8,128)(2,1)} %merge.3, bf16[512,384]{1,0:T(8,128)(2,1)S(1)} %copy-done.8, f32[1,384]{1,0:T(1,128)S(1)} %broadcast_in_dim.117.gain.gain_mid, ...), custom_call_target="tpu_custom_call" | custom-call | tf_op jit(solution)/shard_map/pallas_call | solution.py:433
  152.9 4.2 %collective-permute-start.28 = (bf16[3,2,16,384]{3,2,1,0:T(8,128)(2,1)S(1)}, bf16[3,2,16,384]{3,2,1,0:T(8,128)(2,1)S(1)}, u32[]{:S(2)}, u32[]{:S(2)}) collective-permute-start(bf16[3,2,16,384]{3,2,1,0:T(8,128)(2,1)S(1)} %bitcast.78), channel_id=1, source_target_pairs={{0,8},{8,16},{16,24},{24,32},{32,40},{40,48},{48,56},{56,64},{64,7... | collective-permute-start | bytes 221192 | tf_op jit(solution)/shard_map/ppermute | solution.py:15
  157.1 4.2 %collective-permute-start.29 = (bf16[3,2,16,384]{3,2,1,0:T(8,128)(2,1)S(1)}, bf16[3,2,16,384]{3,2,1,0:T(8,128)(2,1)S(1)}, u32[]{:S(2)}, u32[]{:S(2)}) collective-permute-start(bf16[3,2,16,384]{3,2,1,0:T(8,128)(2,1)S(1)} %bitcast.75), channel_id=1, source_target_pairs={{8,0},{16,8},{24,16},{32,24},{40,32},{48,40},{56,48},{64,56},{72,6... | collective-permute-start | bytes 221192 | tf_op jit(solution)/shard_map/ppermute | solution.py:18
  163.5 5.1 %collective-permute-start.30 = (bf16[22,2,2,384]{3,2,1,0:T(2,128)(2,1)S(1)}, bf16[22,2,2,384]{3,2,1,0:T(2,128)(2,1)S(1)}, u32[]{:S(2)}, u32[]{:S(2)}) collective-permute-start(bf16[22,2,2,384]{3,2,1,0:T(2,128)(2,1)S(1)} %pad_maximum_fusion.7), channel_id=1, source_target_pairs={{0,1},{1,2},{2,3},{3,4},{4,5},{5,6},{6,7},{8,9},{9,10},{10,11},{11... | collective-permute-start | bytes 202760 | tf_op jit(solution)/shard_map/ppermute | solution.py:34
  170.6 4.4 %collective-permute-done.31.right = bf16[22,2,2,384]{3,2,1,0:T(2,128)(2,1)S(1)} collective-permute-done((bf16[22,2,2,384]{3,2,1,0:T(2,128)(2,1)S(1)}, bf16[22,2,2,384]{3,2,1,0:T(2,128)(2,1)S(1)}, u32[]{:S(2)}, u32[]{:S(2)}) %collective-permute-start.31) | collective-permute-done | bytes 67616 | tf_op jit(solution)/shard_map/ppermute | solution.py:35
  175.0 3.5 %shard_map.230 = bf16[16,32,384]{2,1,0:T(8,128)(2,1)} custom-call(bf16[16,2,16,384]{3,2,1,0:T(8,128)(2,1)S(1)} %bitcast.63, bf16[3,2,16,384]{3,2,1,0:T(8,128)(2,1)S(1)} %collective-permute-done.28.top, bf16[3,2,16,384]{3,2,1,0:T(8,128)(2,1)S(1)} %collective-permute-done.29.bottom, bf16[22,2,2,384]{3,2,1,0:T(2,128)(2,1)S(1)} %collective-permute-done.30.left, ...), custom_call_target="tpu_custom_call" | custom-call | tf_op jit(solution)/shard_map/pallas_call | solution.py:433
  (173 shorter events, 53.0 us)
Async XLA Ops:
  7.2 97.8 %all-gather.2.cloned.1.call-start = ((), (), s32[]{:S(2)}) async-start(), calls=%async_computation | async-start | bytes 5013504 | tf_op jit(solution)/shard_map/all_gather | solution.py:506
  8.1 14.8 %collective-permute-start = (bf16[30,768]{1,0:T(8,128)(2,1)S(1)}, bf16[30,768]{1,0:T(8,128)(2,1)S(1)}, u32[]{:S(2)}, u32[]{:S(2)}) collective-permute-start(bf16[30,768]{1,0:T(8,128)(2,1)S(1)} %get-tuple-element.69), channel_id=1, source_target_pairs={{1,0},{2,1},{3,2},{4,3},{5,4},{6,5},{7,6},{0,7},{9,8},{10,9},{11,1... | collective-permute-start | bytes 138248 | tf_op jit(solution)/shard_map/ppermute | solution.py:50
  14.0 15.4 %collective-permute-start.5 = (bf16[30,768]{1,0:T(8,128)(2,1)S(1)}, bf16[30,768]{1,0:T(8,128)(2,1)S(1)}, u32[]{:S(2)}, u32[]{:S(2)}) collective-permute-start(bf16[30,768]{1,0:T(8,128)(2,1)S(1)} %get-tuple-element.69), channel_id=1, source_target_pairs={{6,0},{7,1},{0,2},{1,3},{2,4},{3,5},{4,6},{5,7},{14,8},{15,9},{8,1... | collective-permute-start | bytes 138248 | tf_op jit(solution)/shard_map/ppermute | solution.py:50
  14.0 15.3 %collective-permute-start.4 = (bf16[30,768]{1,0:T(8,128)(2,1)S(1)}, bf16[30,768]{1,0:T(8,128)(2,1)S(1)}, u32[]{:S(2)}, u32[]{:S(2)}) collective-permute-start(bf16[30,768]{1,0:T(8,128)(2,1)S(1)} %get-tuple-element.69), channel_id=1, source_target_pairs={{5,0},{6,1},{7,2},{0,3},{1,4},{2,5},{3,6},{4,7},{13,8},{14,9},{15,... | collective-permute-start | bytes 138248 | tf_op jit(solution)/shard_map/ppermute | solution.py:50
  17.4 12.0 %collective-permute-start.3 = (bf16[30,768]{1,0:T(8,128)(2,1)S(1)}, bf16[30,768]{1,0:T(8,128)(2,1)S(1)}, u32[]{:S(2)}, u32[]{:S(2)}) collective-permute-start(bf16[30,768]{1,0:T(8,128)(2,1)S(1)} %get-tuple-element.69), channel_id=1, source_target_pairs={{4,0},{5,1},{6,2},{7,3},{0,4},{1,5},{2,6},{3,7},{12,8},{13,9},{14,... | collective-permute-start | bytes 138248 | tf_op jit(solution)/shard_map/ppermute | solution.py:50
  18.3 11.0 %collective-permute-start.2 = (bf16[30,768]{1,0:T(8,128)(2,1)S(1)}, bf16[30,768]{1,0:T(8,128)(2,1)S(1)}, u32[]{:S(2)}, u32[]{:S(2)}) collective-permute-start(bf16[30,768]{1,0:T(8,128)(2,1)S(1)} %get-tuple-element.69), channel_id=1, source_target_pairs={{3,0},{4,1},{5,2},{6,3},{7,4},{0,5},{1,6},{2,7},{11,8},{12,9},{13,... | collective-permute-start | bytes 138248 | tf_op jit(solution)/shard_map/ppermute | solution.py:50
  22.9 6.4 %collective-permute-start.1 = (bf16[30,768]{1,0:T(8,128)(2,1)S(1)}, bf16[30,768]{1,0:T(8,128)(2,1)S(1)}, u32[]{:S(2)}, u32[]{:S(2)}) collective-permute-start(bf16[30,768]{1,0:T(8,128)(2,1)S(1)} %get-tuple-element.69), channel_id=1, source_target_pairs={{2,0},{3,1},{4,2},{5,3},{6,4},{7,5},{0,6},{1,7},{10,8},{11,9},{12,... | collective-permute-start | bytes 138248 | tf_op jit(solution)/shard_map/ppermute | solution.py:50
  35.7 13.2 %collective-permute-start.14 = (bf16[3,32,384]{2,1,0:T(8,128)(2,1)S(1)}, bf16[3,32,384]{2,1,0:T(8,128)(2,1)S(1)}, u32[]{:S(2)}, u32[]{:S(2)}) collective-permute-start(bf16[3,32,384]{2,1,0:T(8,128)(2,1)S(1)} %get-tuple-element.78), channel_id=1, source_target_pairs={{8,0},{16,8},{24,16},{32,24},{40,32},{48,40},{56,48},{64,56},{72,6... | collective-permute-start | bytes 221192 | tf_op jit(solution)/shard_map/ppermute | solution.py:18
  40.6 8.9 %collective-permute-start.13 = (bf16[3,32,384]{2,1,0:T(8,128)(2,1)S(1)}, bf16[3,32,384]{2,1,0:T(8,128)(2,1)S(1)}, u32[]{:S(2)}, u32[]{:S(2)}) collective-permute-start(bf16[3,32,384]{2,1,0:T(8,128)(2,1)S(1)} %get-tuple-element.79), channel_id=1, source_target_pairs={{0,8},{8,16},{16,24},{24,32},{32,40},{40,48},{48,56},{56,64},{64,7... | collective-permute-start | bytes 221192 | tf_op jit(solution)/shard_map/ppermute | solution.py:15
  43.2 10.1 %collective-permute-start.9 = (bf16[48,768]{1,0:T(8,128)(2,1)S(1)}, bf16[48,768]{1,0:T(8,128)(2,1)S(1)}, u32[]{:S(2)}, u32[]{:S(2)}) collective-permute-start(bf16[48,768]{1,0:T(8,128)(2,1)S(1)} %reshape.63), channel_id=1, source_target_pairs={{24,0},{0,8},{8,16},{16,24},{56,32},{32,40},{40,48},{48,56},{88,64... | collective-permute-start | bytes 221192 | tf_op jit(solution)/shard_map/ppermute | solution.py:50
  43.9 9.4 %collective-permute-start.8 = (bf16[48,768]{1,0:T(8,128)(2,1)S(1)}, bf16[48,768]{1,0:T(8,128)(2,1)S(1)}, u32[]{:S(2)}, u32[]{:S(2)}) collective-permute-start(bf16[48,768]{1,0:T(8,128)(2,1)S(1)} %reshape.63), channel_id=1, source_target_pairs={{16,0},{24,8},{0,16},{8,24},{48,32},{56,40},{32,48},{40,56},{80,64... | collective-permute-start | bytes 221192 | tf_op jit(solution)/shard_map/ppermute | solution.py:50
  53.4 14.5 %collective-permute-start.10 = (bf16[192,768]{1,0:T(8,128)(2,1)S(1)}, bf16[192,768]{1,0:T(8,128)(2,1)S(1)}, u32[]{:S(2)}, u32[]{:S(2)}) collective-permute-start(bf16[192,768]{1,0:T(8,128)(2,1)S(1)} %bitcast.68), channel_id=1, source_target_pairs={{32,0},{40,8},{48,16},{56,24},{64,32},{72,40},{80,48},{88,56},{96,... | collective-permute-start | bytes 884744 | tf_op jit(solution)/shard_map/ppermute | solution.py:50
  54.0 7.2 %collective-permute-start.15 = (bf16[22,3,384]{2,1,0:T(4,128)(2,1)S(1)}, bf16[22,3,384]{2,1,0:T(4,128)(2,1)S(1)}, u32[]{:S(2)}, u32[]{:S(2)}) collective-permute-start(bf16[22,3,384]{2,1,0:T(4,128)(2,1)S(1)} %pad_maximum_fusion.5), channel_id=1, source_target_pairs={{0,1},{1,2},{2,3},{3,4},{4,5},{5,6},{6,7},{8,9},{9,10},{10,11},{11... | collective-permute-start | bytes 152072 | tf_op jit(solution)/shard_map/ppermute | solution.py:34
  58.2 10.5 %collective-permute-start.12 = (bf16[192,768]{1,0:T(8,128)(2,1)S(1)}, bf16[192,768]{1,0:T(8,128)(2,1)S(1)}, u32[]{:S(2)}, u32[]{:S(2)}) collective-permute-start(bf16[192,768]{1,0:T(8,128)(2,1)S(1)} %bitcast.69), channel_id=1, source_target_pairs={{96,0},{104,8},{112,16},{120,24},{0,32},{8,40},{16,48},{24,56},{32... | collective-permute-start | bytes 884744 | tf_op jit(solution)/shard_map/ppermute | solution.py:50
  59.8 8.8 %collective-permute-start.11 = (bf16[192,768]{1,0:T(8,128)(2,1)S(1)}, bf16[192,768]{1,0:T(8,128)(2,1)S(1)}, u32[]{:S(2)}, u32[]{:S(2)}) collective-permute-start(bf16[192,768]{1,0:T(8,128)(2,1)S(1)} %bitcast.70), channel_id=1, source_target_pairs={{64,0},{72,8},{80,16},{88,24},{96,32},{104,40},{112,48},{120,56},{... | collective-permute-start | bytes 884744 | tf_op jit(solution)/shard_map/ppermute | solution.py:50
  77.2 11.8 %collective-permute-start.18 = (bf16[3,16,768]{2,1,0:T(8,128)(2,1)S(1)}, bf16[3,16,768]{2,1,0:T(8,128)(2,1)S(1)}, u32[]{:S(2)}, u32[]{:S(2)}) collective-permute-start(bf16[3,16,768]{2,1,0:T(8,128)(2,1)S(1)} %bitcast.76), channel_id=1, source_target_pairs={{0,8},{8,16},{16,24},{24,32},{32,40},{40,48},{48,56},{56,64},{64,7... | collective-permute-start | bytes 221192 | tf_op jit(solution)/shard_map/ppermute | solution.py:15
  80.1 10.2 %collective-permute-start.19 = (bf16[3,16,768]{2,1,0:T(8,128)(2,1)S(1)}, bf16[3,16,768]{2,1,0:T(8,128)(2,1)S(1)}, u32[]{:S(2)}, u32[]{:S(2)}) collective-permute-start(bf16[3,16,768]{2,1,0:T(8,128)(2,1)S(1)} %bitcast.73), channel_id=1, source_target_pairs={{8,0},{16,8},{24,16},{32,24},{40,32},{48,40},{56,48},{64,56},{72,6... | collective-permute-start | bytes 221192 | tf_op jit(solution)/shard_map/ppermute | solution.py:18
  94.4 6.4 %collective-permute-start.21 = (bf16[14,3,768]{2,1,0:T(4,128)(2,1)S(1)}, bf16[14,3,768]{2,1,0:T(4,128)(2,1)S(1)}, u32[]{:S(2)}, u32[]{:S(2)}) collective-permute-start(bf16[14,3,768]{2,1,0:T(4,128)(2,1)S(1)} %pad_maximum_fusion.2), channel_id=1, source_target_pairs={{1,0},{2,1},{3,2},{4,3},{5,4},{6,5},{7,6},{9,8},{10,9},{11,10},{12... | collective-permute-start | bytes 193544 | tf_op jit(solution)/shard_map/ppermute | solution.py:35
  118.3 9.1 %collective-permute-start.24 = (bf16[3,16,768]{2,1,0:T(8,128)(2,1)S(1)}, bf16[3,16,768]{2,1,0:T(8,128)(2,1)S(1)}, u32[]{:S(2)}, u32[]{:S(2)}) collective-permute-start(bf16[3,16,768]{2,1,0:T(8,128)(2,1)S(1)} %bitcast.77), channel_id=1, source_target_pairs={{0,8},{8,16},{16,24},{24,32},{32,40},{40,48},{48,56},{56,64},{64,7... | collective-permute-start | bytes 221192 | tf_op jit(solution)/shard_map/ppermute | solution.py:15
  120.3 8.5 %collective-permute-start.25 = (bf16[3,16,768]{2,1,0:T(8,128)(2,1)S(1)}, bf16[3,16,768]{2,1,0:T(8,128)(2,1)S(1)}, u32[]{:S(2)}, u32[]{:S(2)}) collective-permute-start(bf16[3,16,768]{2,1,0:T(8,128)(2,1)S(1)} %bitcast.74), channel_id=1, source_target_pairs={{8,0},{16,8},{24,16},{32,24},{40,32},{48,40},{56,48},{64,56},{72,6... | collective-permute-start | bytes 221192 | tf_op jit(solution)/shard_map/ppermute | solution.py:18
  128.9 7.3 %collective-permute-start.26 = (bf16[14,3,768]{2,1,0:T(4,128)(2,1)S(1)}, bf16[14,3,768]{2,1,0:T(4,128)(2,1)S(1)}, u32[]{:S(2)}, u32[]{:S(2)}) collective-permute-start(bf16[14,3,768]{2,1,0:T(4,128)(2,1)S(1)} %pad_maximum_fusion.3), channel_id=1, source_target_pairs={{0,1},{1,2},{2,3},{3,4},{4,5},{5,6},{6,7},{8,9},{9,10},{10,11},{11... | collective-permute-start | bytes 193544 | tf_op jit(solution)/shard_map/ppermute | solution.py:34
  132.7 7.3 %collective-permute-start.27 = (bf16[14,3,768]{2,1,0:T(4,128)(2,1)S(1)}, bf16[14,3,768]{2,1,0:T(4,128)(2,1)S(1)}, u32[]{:S(2)}, u32[]{:S(2)}) collective-permute-start(bf16[14,3,768]{2,1,0:T(4,128)(2,1)S(1)} %pad_maximum_fusion.4), channel_id=1, source_target_pairs={{1,0},{2,1},{3,2},{4,3},{5,4},{6,5},{7,6},{9,8},{10,9},{11,10},{12... | collective-permute-start | bytes 193544 | tf_op jit(solution)/shard_map/ppermute | solution.py:35
  152.9 8.7 %collective-permute-start.28 = (bf16[3,2,16,384]{3,2,1,0:T(8,128)(2,1)S(1)}, bf16[3,2,16,384]{3,2,1,0:T(8,128)(2,1)S(1)}, u32[]{:S(2)}, u32[]{:S(2)}) collective-permute-start(bf16[3,2,16,384]{3,2,1,0:T(8,128)(2,1)S(1)} %bitcast.78), channel_id=1, source_target_pairs={{0,8},{8,16},{16,24},{24,32},{32,40},{40,48},{48,56},{56,64},{64,7... | collective-permute-start | bytes 221192 | tf_op jit(solution)/shard_map/ppermute | solution.py:15
  163.5 7.0 %collective-permute-start.30 = (bf16[22,2,2,384]{3,2,1,0:T(2,128)(2,1)S(1)}, bf16[22,2,2,384]{3,2,1,0:T(2,128)(2,1)S(1)}, u32[]{:S(2)}, u32[]{:S(2)}) collective-permute-start(bf16[22,2,2,384]{3,2,1,0:T(2,128)(2,1)S(1)} %pad_maximum_fusion.7), channel_id=1, source_target_pairs={{0,1},{1,2},{2,3},{3,4},{4,5},{5,6},{6,7},{8,9},{9,10},{10,11},{11... | collective-permute-start | bytes 202760 | tf_op jit(solution)/shard_map/ppermute | solution.py:34
  (36 other events, 308.0 us)
Sparse Core Ops, SparseCore 0:
  35.8 61.8 all-gather.1

commit v4 on v3

--- a/solution.py
+++ b/solution.py
@@ -146,13 +146,10 @@
     gain = gain_ref[...]
     shift = shift_ref[...]
 
-    def step(index, carry):
-        span = pl.ds(pl.multiple_of(index * chunk, chunk), chunk)
+    for first in range(0, values_ref.shape[0], chunk):
+        span = slice(first, first + chunk)
         values = values_ref[span, :].astype(jnp.float32)
         normed_ref[span, :] = norm_forward(values, gain, shift)[2].astype(normed_ref.dtype)
-        return carry
-
-    lax.fori_loop(0, values_ref.shape[0] // chunk, step, 0)
 
 
 def conv_one_kernel(
@@ -177,7 +174,7 @@
         return carry
 
     lax.fori_loop(0, channels // lanes, step, 0)
-    norm_rows(conv, normed, gain, shift, 64)
+    norm_rows(conv, normed, gain, shift, 32)
 
 
 def back_one_kernel(tile_ref, top, bottom, left, right, taps, upstream, out, frame, total):
@@ -292,8 +289,8 @@
     half_cols = patches.shape[2]
     step_rows = 4 * half_cols
 
-    def step(index, carry):
-        rows = pl.ds(pl.multiple_of(index * step_rows, step_rows), step_rows)
+    for index in range(quarter):
+        rows = slice(index * step_rows, (index + 1) * step_rows)
         total = branch[rows, :] + partial[rows, :] + down_bias[...]
         out = (residual[rows, :].astype(jnp.float32) + scale[...] * total).astype(jnp.bfloat16)
         section[rows, :] = out
@@ -301,9 +298,7 @@
         normal = normal.astype(jnp.bfloat16)
         for place in range(4):
             patches[index, place] = normal[place * half_cols : (place + 1) * half_cols, :]
-        return carry
-
-    lax.fori_loop(0, quarter, step, 0)
+
     total = merge_bias[...]
     for place in range(4):
         patch = patches[:, place].reshape(quarter * half_cols, width)
@@ -340,19 +335,16 @@
         d_normal = contract_last(d_merged[...], merge[place * width : (place + 1) * width, :])
         for group in range(groups):
             first = (4 * group + place) * half_cols
-            d_normed[first : first + half_cols, :] = d_normal[
-                group * half_cols : (group + 1) * half_cols
-            ]
-
-    def norm_step(index, carry):
-        rows = pl.ds(pl.multiple_of(index * 64, 64), 64)
-        scaled, inv_std, _ = norm_forward(section[rows, :].astype(jnp.float32), 1.0, 0.0)
-        flow = norm_backward(d_normed[rows, :], scaled, inv_std, gain_mid[...])
-        upstream[rows, :] = flow
-        d_branch[rows, :] = (flow * scale[...]).astype(d_branch.dtype)
-        return carry
-
-    lax.fori_loop(0, groups, norm_step, 0)
+            rows = slice(first, first + half_cols)
+            scaled, inv_std, _ = norm_forward(section[rows, :].astype(jnp.float32), 1.0, 0.0)
+            flow = norm_backward(
+                d_normal[group * half_cols : (group + 1) * half_cols],
+                scaled,
+                inv_std,
+                gain_mid[...],
+            )
+            upstream[rows, :] = flow
+            d_branch[rows, :] = (flow * scale[...]).astype(d_branch.dtype)
     d_normed[...] = jnp.zeros_like(d_normed)
 
     def step(place, units):
@@ -365,18 +357,15 @@
             d_normed[rows, :] = total
 
     over_hidden(own, step)
-    norm_back_rows(conv, d_normed, gain, d_conv, 64)
+    norm_back_rows(conv, d_normed, gain, d_conv, 32)
 
 
 def norm_back_rows(conv, d_normed, gain, d_conv, chunk):
-    def step(index, carry):
-        rows = pl.ds(pl.multiple_of(index * chunk, chunk), chunk)
+    for first in range(0, conv.shape[0], chunk):
+        rows = slice(first, first + chunk)
         scaled, inv_std, _ = norm_forward(conv[rows, :].astype(jnp.float32), 1.0, 0.0)
         flow = norm_backward(d_normed[rows, :], scaled, inv_std, gain[...])
         d_conv[rows, :] = flow.astype(d_conv.dtype)
-        return carry
-
-    lax.fori_loop(0, conv.shape[0] // chunk, step, 0)
 
 
 def mlp_two_kernel(mine, theirs, weights, bias, keep, send, stacked, d_stacked):
@@ -407,18 +396,15 @@
 def two_finish_kernel(keep, back, merged, scale, down_bias, conv, gain, features, d_conv):
     count = merged.shape[0]
 
-    def step(index, carry):
-        rows = pl.ds(pl.multiple_of(index * 32, 32), 32)
-        low = pl.ds(pl.multiple_of(count + index * 32, 32), 32)
+    for first in range(0, count, 32):
+        rows = slice(first, first + 32)
+        low = slice(count + first, count + first + 32)
         total = keep[rows, :] + back[rows, :] + down_bias[...]
         out = merged[rows, :].astype(jnp.float32) + scale[...] * total
         features[rows, :] = out.astype(features.dtype)
         scaled, inv_std, _ = norm_forward(conv[rows, :].astype(jnp.float32), 1.0, 0.0)
         flow = norm_backward(keep[low, :] + back[low, :], scaled, inv_std, gain[...])
         d_conv[rows, :] = flow.astype(d_conv.dtype)
-        return carry
-
-    lax.fori_loop(0, count // 32, step, 0)
 
 
 megabyte = 1024 * 1024

time: 188 us -> 182 us (0.968)
  Pallas kernels: 41.1 us -> 34 us
    pallas_call x10, Pallas kernels: 41.1 us -> 34 us  [block_call(): pl.pallas_call(kernel, out_shape=outputs, in_specs=[whole] * len(operands...]
  transfers between devices with their start and end apart: 33 -> 33, of which waited for: 20 -> 20; matrix products, arithmetic and copies ran while one was open for 1% -> 1% of each run, Pallas kernels for 9% -> 8%
where the time goes in v4:
time: 182 us; the launch traced here: 179 us
  starting transfers between devices  79.5 us (44%)
  waiting for transfers between devices  44.1 us (24%)
  Pallas kernels  34 us (19%)
  between operations  15.3 us (8%)
  local copies, waits for them, and re-layouts  4.32 us (2%)
  other arithmetic  2.16 us (1%)
    pallas_call x10, Pallas kernels, block_call(): pl.pallas_call(kernel, out_shape=outputs, in_specs=[whole] * len(operands...  34 us
    ppermute x13, starting transfers between devices, ring_collect(): arrived = lax.ppermute(piece, axis, pairs)  25.7 us
    ppermute x4, starting transfers between devices, exchange(): lax.ppermute(lax.slice_in_dim(block, 0, width, axis=dim), axis, backward)  21.8 us
    ppermute x4, starting transfers between devices, halo_of(): left = lax.ppermute(edge(extent - width, extent), 'col', forward)  15.6 us
    ppermute x13, waiting for transfers between devices, ring_collect(): arrived = lax.ppermute(piece, axis, pairs)  15.5 us
    ppermute x4, waiting for transfers between devices, halo_of(): right = lax.ppermute(edge(0, width), 'col', backward)  14.6 us
    ppermute x4, starting transfers between devices, exchange(): lax.ppermute(lax.slice_in_dim(block, block.shape[dim] - width, None, axis...  10.9 us
    ppermute x4, starting transfers between devices, halo_of(): right = lax.ppermute(edge(0, width), 'col', backward)  5.17 us
  transfers between devices with their start and end apart: 33, of which 20 were waited for; matrix products, arithmetic and copies ran while one was open for 1% of the time, Pallas kernels for 8%

profile of v4, /device:TPU:2, one launch (start us, length us, event | category | flops | bytes accessed | tf_op | source)
XLA Modules:
  0.0 179.3 jit_solution(9806654971729154504)
XLA Ops:
  8.1 5.9 %collective-permute-start = (bf16[30,768]{1,0:T(8,128)(2,1)S(1)}, bf16[30,768]{1,0:T(8,128)(2,1)S(1)}, u32[]{:S(2)}, u32[]{:S(2)}) collective-permute-start(bf16[30,768]{1,0:T(8,128)(2,1)S(1)} %get-tuple-element.69), channel_id=1, source_target_pairs={{1,0},{2,1},{3,2},{4,3},{5,4},{6,5},{7,6},{0,7},{9,8},{10,9},{11,1... | collective-permute-start | bytes 138248 | tf_op jit(solution)/shard_map/ppermute | solution.py:50
  14.0 3.4 %collective-permute-start.4 = (bf16[30,768]{1,0:T(8,128)(2,1)S(1)}, bf16[30,768]{1,0:T(8,128)(2,1)S(1)}, u32[]{:S(2)}, u32[]{:S(2)}) collective-permute-start(bf16[30,768]{1,0:T(8,128)(2,1)S(1)} %get-tuple-element.69), channel_id=1, source_target_pairs={{5,0},{6,1},{7,2},{0,3},{1,4},{2,5},{3,6},{4,7},{13,8},{14,9},{15,... | collective-permute-start | bytes 138248 | tf_op jit(solution)/shard_map/ppermute | solution.py:50
  18.3 4.6 %collective-permute-start.2 = (bf16[30,768]{1,0:T(8,128)(2,1)S(1)}, bf16[30,768]{1,0:T(8,128)(2,1)S(1)}, u32[]{:S(2)}, u32[]{:S(2)}) collective-permute-start(bf16[30,768]{1,0:T(8,128)(2,1)S(1)} %get-tuple-element.69), channel_id=1, source_target_pairs={{3,0},{4,1},{5,2},{6,3},{7,4},{0,5},{1,6},{2,7},{11,8},{12,9},{13,... | collective-permute-start | bytes 138248 | tf_op jit(solution)/shard_map/ppermute | solution.py:50
  24.6 4.7 %collective-permute-done.1 = bf16[30,768]{1,0:T(8,128)(2,1)S(1)} collective-permute-done((bf16[30,768]{1,0:T(8,128)(2,1)S(1)}, bf16[30,768]{1,0:T(8,128)(2,1)S(1)}, u32[]{:S(2)}, u32[]{:S(2)}) %collective-permute-start.1) | collective-permute-done | bytes 46112 | tf_op jit(solution)/shard_map/ppermute | solution.py:50
  29.4 5.2 %collective-permute-done.6 = bf16[30,768]{1,0:T(8,128)(2,1)S(1)} collective-permute-done((bf16[30,768]{1,0:T(8,128)(2,1)S(1)}, bf16[30,768]{1,0:T(8,128)(2,1)S(1)}, u32[]{:S(2)}, u32[]{:S(2)}) %collective-permute-start.6) | collective-permute-done | bytes 46112 | tf_op jit(solution)/shard_map/ppermute | solution.py:50
  35.7 4.9 %collective-permute-start.14 = (bf16[3,32,384]{2,1,0:T(8,128)(2,1)S(1)}, bf16[3,32,384]{2,1,0:T(8,128)(2,1)S(1)}, u32[]{:S(2)}, u32[]{:S(2)}) collective-permute-start(bf16[3,32,384]{2,1,0:T(8,128)(2,1)S(1)} %get-tuple-element.78), channel_id=1, source_target_pairs={{8,0},{16,8},{24,16},{32,24},{40,32},{48,40},{56,48},{64,56},{72,6... | collective-permute-start | bytes 221192 | tf_op jit(solution)/shard_map/ppermute | solution.py:18
  43.9 5.0 %collective-permute-start.8 = (bf16[48,768]{1,0:T(8,128)(2,1)S(1)}, bf16[48,768]{1,0:T(8,128)(2,1)S(1)}, u32[]{:S(2)}, u32[]{:S(2)}) collective-permute-start(bf16[48,768]{1,0:T(8,128)(2,1)S(1)} %reshape.63), channel_id=1, source_target_pairs={{16,0},{24,8},{0,16},{8,24},{48,32},{56,40},{32,48},{40,56},{80,64... | collective-permute-start | bytes 221192 | tf_op jit(solution)/shard_map/ppermute | solution.py:50
  49.5 3.7 %collective-permute-done.7 = bf16[48,768]{1,0:T(8,128)(2,1)S(1)} collective-permute-done((bf16[48,768]{1,0:T(8,128)(2,1)S(1)}, bf16[48,768]{1,0:T(8,128)(2,1)S(1)}, u32[]{:S(2)}, u32[]{:S(2)}) %collective-permute-start.7) | collective-permute-done | bytes 73760 | tf_op jit(solution)/shard_map/ppermute | solution.py:50
  63.2 3.5 %shard_map.221 = (bf16[512,384]{1,0:T(8,128)(2,1)S(1)}, f32[512,384]{1,0:T(8,128)S(1)}, bf16[512,384]{1,0:T(8,128)(2,1)S(1)}) custom-call(bf16[16,32,384]{2,1,0:T(8,128)(2,1)S(1)} %bitcast.61, bf16[3,32,384]{2,1,0:T(8,128)(2,1)S(1)} %collective-permute-done.13.top, bf16[3,32,384]{2,1,0:T(8,128)(2,1)S(1)} %collective-permute-done.14.bottom, ...), custom_call_target="tpu_custom_call" | custom-call | tf_op jit(solution)/shard_map/pallas_call | solution.py:419
  71.7 3.4 %shard_map.223 = (bf16[512,384]{1,0:T(8,128)(2,1)S(1)}, bf16[128,768]{1,0:T(8,128)(2,1)S(1)}) custom-call(bf16[512,384]{1,0:T(8,128)(2,1)S(1)} %get-tuple-element.37.normed, bf16[768,768]{1,0:T(8,128)(2,1)S(1)} %collective-permute-done.17.weights.other, f32[1,768]{1,0:T(1,128)S(1)} %select_n.192.bias.bias_other, f32[512,384]{1,0:T(8,128)S(1)} %shard_map.222.partial, ...), custom_call_target="tpu_custom_call" | custom-call | tf_op jit(solution)/shard_map/pallas_call | solution.py:419
  75.9 2.9 %collective-permute-start.18 = (bf16[3,16,768]{2,1,0:T(8,128)(2,1)S(1)}, bf16[3,16,768]{2,1,0:T(8,128)(2,1)S(1)}, u32[]{:S(2)}, u32[]{:S(2)}) collective-permute-start(bf16[3,16,768]{2,1,0:T(8,128)(2,1)S(1)} %bitcast.76), channel_id=1, source_target_pairs={{0,8},{8,16},{16,24},{24,32},{32,40},{40,48},{48,56},{56,64},{64,7... | collective-permute-start | bytes 221192 | tf_op jit(solution)/shard_map/ppermute | solution.py:15
  78.8 6.3 %collective-permute-start.19 = (bf16[3,16,768]{2,1,0:T(8,128)(2,1)S(1)}, bf16[3,16,768]{2,1,0:T(8,128)(2,1)S(1)}, u32[]{:S(2)}, u32[]{:S(2)}) collective-permute-start(bf16[3,16,768]{2,1,0:T(8,128)(2,1)S(1)} %bitcast.73), channel_id=1, source_target_pairs={{8,0},{16,8},{24,16},{32,24},{40,32},{48,40},{56,48},{64,56},{72,6... | collective-permute-start | bytes 221192 | tf_op jit(solution)/shard_map/ppermute | solution.py:18
  89.2 3.8 %collective-permute-start.20 = (bf16[14,3,768]{2,1,0:T(4,128)(2,1)S(1)}, bf16[14,3,768]{2,1,0:T(4,128)(2,1)S(1)}, u32[]{:S(2)}, u32[]{:S(2)}) collective-permute-start(bf16[14,3,768]{2,1,0:T(4,128)(2,1)S(1)} %pad_maximum_fusion.1), channel_id=1, source_target_pairs={{0,1},{1,2},{2,3},{3,4},{4,5},{5,6},{6,7},{8,9},{9,10},{10,11},{11... | collective-permute-start | bytes 193544 | tf_op jit(solution)/shard_map/ppermute | solution.py:34
  95.1 4.4 %collective-permute-done.21.right = bf16[14,3,768]{2,1,0:T(4,128)(2,1)S(1)} collective-permute-done((bf16[14,3,768]{2,1,0:T(4,128)(2,1)S(1)}, bf16[14,3,768]{2,1,0:T(4,128)(2,1)S(1)}, u32[]{:S(2)}, u32[]{:S(2)}) %collective-permute-start.21) | collective-permute-done | bytes 64544 | tf_op jit(solution)/shard_map/ppermute | solution.py:35
  106.0 6.4 %shard_map.225 = (f32[256,768]{1,0:T(8,128)S(1)}, f32[256,768]{1,0:T(8,128)S(1)}) custom-call(bf16[256,768]{1,0:T(8,128)(2,1)S(1)} %copy-done.10, bf16[256,768]{1,0:T(8,128)(2,1)S(1)} %collective-permute-done.22.theirs, bf16[1536,1536]{1,0:T(8,128)(2,1)} %all-gather.2.cloned.1.call-done.weights, f32[1,1536]{1,0:T(1,128)S(1)} %select_n.195.bias), custom_call_target="tpu_custom_call" | custom-call | tf_op jit(solution)/shard_map/pallas_call | solution.py:419
  117.8 6.5 %collective-permute-start.25 = (bf16[3,16,768]{2,1,0:T(8,128)(2,1)S(1)}, bf16[3,16,768]{2,1,0:T(8,128)(2,1)S(1)}, u32[]{:S(2)}, u32[]{:S(2)}) collective-permute-start(bf16[3,16,768]{2,1,0:T(8,128)(2,1)S(1)} %bitcast.74), channel_id=1, source_target_pairs={{8,0},{16,8},{24,16},{32,24},{40,32},{48,40},{56,48},{64,56},{72,6... | collective-permute-start | bytes 221192 | tf_op jit(solution)/shard_map/ppermute | solution.py:18
  126.4 3.8 %collective-permute-start.26 = (bf16[14,3,768]{2,1,0:T(4,128)(2,1)S(1)}, bf16[14,3,768]{2,1,0:T(4,128)(2,1)S(1)}, u32[]{:S(2)}, u32[]{:S(2)}) collective-permute-start(bf16[14,3,768]{2,1,0:T(4,128)(2,1)S(1)} %pad_maximum_fusion.3), channel_id=1, source_target_pairs={{0,1},{1,2},{2,3},{3,4},{4,5},{5,6},{6,7},{8,9},{9,10},{10,11},{11... | collective-permute-start | bytes 193544 | tf_op jit(solution)/shard_map/ppermute | solution.py:34
  133.7 3.8 %collective-permute-done.27.right = bf16[14,3,768]{2,1,0:T(4,128)(2,1)S(1)} collective-permute-done((bf16[14,3,768]{2,1,0:T(4,128)(2,1)S(1)}, bf16[14,3,768]{2,1,0:T(4,128)(2,1)S(1)}, u32[]{:S(2)}, u32[]{:S(2)}) %collective-permute-start.27) | collective-permute-done | bytes 64544 | tf_op jit(solution)/shard_map/ppermute | solution.py:35
  139.3 7.6 %shard_map.229 = (bf16[512,384]{1,0:T(8,128)(2,1)S(1)}, f32[512,384]{1,0:T(8,128)S(1)}) custom-call(bf16[128,768]{1,0:T(8,128)(2,1)S(1)} %shard_map.227.d_merged, bf16[1536,768]{1,0:T(8,128)(2,1)} %merge.3, bf16[512,384]{1,0:T(8,128)(2,1)S(1)} %copy-done.8, f32[1,384]{1,0:T(1,128)S(1)} %broadcast_in_dim.117.gain.gain_mid, ...), custom_call_target="tpu_custom_call" | custom-call | tf_op jit(solution)/shard_map/pallas_call | solution.py:419
  146.9 4.2 %collective-permute-start.28 = (bf16[3,2,16,384]{3,2,1,0:T(8,128)(2,1)S(1)}, bf16[3,2,16,384]{3,2,1,0:T(8,128)(2,1)S(1)}, u32[]{:S(2)}, u32[]{:S(2)}) collective-permute-start(bf16[3,2,16,384]{3,2,1,0:T(8,128)(2,1)S(1)} %bitcast.78), channel_id=1, source_target_pairs={{0,8},{8,16},{16,24},{24,32},{32,40},{40,48},{48,56},{56,64},{64,7... | collective-permute-start | bytes 221192 | tf_op jit(solution)/shard_map/ppermute | solution.py:15
  151.1 4.2 %collective-permute-start.29 = (bf16[3,2,16,384]{3,2,1,0:T(8,128)(2,1)S(1)}, bf16[3,2,16,384]{3,2,1,0:T(8,128)(2,1)S(1)}, u32[]{:S(2)}, u32[]{:S(2)}) collective-permute-start(bf16[3,2,16,384]{3,2,1,0:T(8,128)(2,1)S(1)} %bitcast.75), channel_id=1, source_target_pairs={{8,0},{16,8},{24,16},{32,24},{40,32},{48,40},{56,48},{64,56},{72,6... | collective-permute-start | bytes 221192 | tf_op jit(solution)/shard_map/ppermute | solution.py:18
  157.5 5.1 %collective-permute-start.30 = (bf16[22,2,2,384]{3,2,1,0:T(2,128)(2,1)S(1)}, bf16[22,2,2,384]{3,2,1,0:T(2,128)(2,1)S(1)}, u32[]{:S(2)}, u32[]{:S(2)}) collective-permute-start(bf16[22,2,2,384]{3,2,1,0:T(2,128)(2,1)S(1)} %pad_maximum_fusion.7), channel_id=1, source_target_pairs={{0,1},{1,2},{2,3},{3,4},{4,5},{5,6},{6,7},{8,9},{9,10},{10,11},{11... | collective-permute-start | bytes 202760 | tf_op jit(solution)/shard_map/ppermute | solution.py:34
  164.6 4.4 %collective-permute-done.31.right = bf16[22,2,2,384]{3,2,1,0:T(2,128)(2,1)S(1)} collective-permute-done((bf16[22,2,2,384]{3,2,1,0:T(2,128)(2,1)S(1)}, bf16[22,2,2,384]{3,2,1,0:T(2,128)(2,1)S(1)}, u32[]{:S(2)}, u32[]{:S(2)}) %collective-permute-start.31) | collective-permute-done | bytes 67616 | tf_op jit(solution)/shard_map/ppermute | solution.py:35
  169.0 3.5 %shard_map.230 = bf16[16,32,384]{2,1,0:T(8,128)(2,1)} custom-call(bf16[16,2,16,384]{3,2,1,0:T(8,128)(2,1)S(1)} %bitcast.63, bf16[3,2,16,384]{3,2,1,0:T(8,128)(2,1)S(1)} %collective-permute-done.28.top, bf16[3,2,16,384]{3,2,1,0:T(8,128)(2,1)S(1)} %collective-permute-done.29.bottom, bf16[22,2,2,384]{3,2,1,0:T(2,128)(2,1)S(1)} %collective-permute-done.30.left, ...), custom_call_target="tpu_custom_call" | custom-call | tf_op jit(solution)/shard_map/pallas_call | solution.py:419
  (173 shorter events, 53.1 us)
Async XLA Ops:
  7.2 95.9 %all-gather.2.cloned.1.call-start = ((), (), s32[]{:S(2)}) async-start(), calls=%async_computation | async-start | bytes 5013504 | tf_op jit(solution)/shard_map/all_gather | solution.py:492
  8.1 14.8 %collective-permute-start = (bf16[30,768]{1,0:T(8,128)(2,1)S(1)}, bf16[30,768]{1,0:T(8,128)(2,1)S(1)}, u32[]{:S(2)}, u32[]{:S(2)}) collective-permute-start(bf16[30,768]{1,0:T(8,128)(2,1)S(1)} %get-tuple-element.69), channel_id=1, source_target_pairs={{1,0},{2,1},{3,2},{4,3},{5,4},{6,5},{7,6},{0,7},{9,8},{10,9},{11,1... | collective-permute-start | bytes 138248 | tf_op jit(solution)/shard_map/ppermute | solution.py:50
  14.0 15.4 %collective-permute-start.5 = (bf16[30,768]{1,0:T(8,128)(2,1)S(1)}, bf16[30,768]{1,0:T(8,128)(2,1)S(1)}, u32[]{:S(2)}, u32[]{:S(2)}) collective-permute-start(bf16[30,768]{1,0:T(8,128)(2,1)S(1)} %get-tuple-element.69), channel_id=1, source_target_pairs={{6,0},{7,1},{0,2},{1,3},{2,4},{3,5},{4,6},{5,7},{14,8},{15,9},{8,1... | collective-permute-start | bytes 138248 | tf_op jit(solution)/shard_map/ppermute | solution.py:50
  14.0 15.3 %collective-permute-start.4 = (bf16[30,768]{1,0:T(8,128)(2,1)S(1)}, bf16[30,768]{1,0:T(8,128)(2,1)S(1)}, u32[]{:S(2)}, u32[]{:S(2)}) collective-permute-start(bf16[30,768]{1,0:T(8,128)(2,1)S(1)} %get-tuple-element.69), channel_id=1, source_target_pairs={{5,0},{6,1},{7,2},{0,3},{1,4},{2,5},{3,6},{4,7},{13,8},{14,9},{15,... | collective-permute-start | bytes 138248 | tf_op jit(solution)/shard_map/ppermute | solution.py:50
  17.4 12.0 %collective-permute-start.3 = (bf16[30,768]{1,0:T(8,128)(2,1)S(1)}, bf16[30,768]{1,0:T(8,128)(2,1)S(1)}, u32[]{:S(2)}, u32[]{:S(2)}) collective-permute-start(bf16[30,768]{1,0:T(8,128)(2,1)S(1)} %get-tuple-element.69), channel_id=1, source_target_pairs={{4,0},{5,1},{6,2},{7,3},{0,4},{1,5},{2,6},{3,7},{12,8},{13,9},{14,... | collective-permute-start | bytes 138248 | tf_op jit(solution)/shard_map/ppermute | solution.py:50
  18.3 11.0 %collective-permute-start.2 = (bf16[30,768]{1,0:T(8,128)(2,1)S(1)}, bf16[30,768]{1,0:T(8,128)(2,1)S(1)}, u32[]{:S(2)}, u32[]{:S(2)}) collective-permute-start(bf16[30,768]{1,0:T(8,128)(2,1)S(1)} %get-tuple-element.69), channel_id=1, source_target_pairs={{3,0},{4,1},{5,2},{6,3},{7,4},{0,5},{1,6},{2,7},{11,8},{12,9},{13,... | collective-permute-start | bytes 138248 | tf_op jit(solution)/shard_map/ppermute | solution.py:50
  22.9 6.4 %collective-permute-start.1 = (bf16[30,768]{1,0:T(8,128)(2,1)S(1)}, bf16[30,768]{1,0:T(8,128)(2,1)S(1)}, u32[]{:S(2)}, u32[]{:S(2)}) collective-permute-start(bf16[30,768]{1,0:T(8,128)(2,1)S(1)} %get-tuple-element.69), channel_id=1, source_target_pairs={{2,0},{3,1},{4,2},{5,3},{6,4},{7,5},{0,6},{1,7},{10,8},{11,9},{12,... | collective-permute-start | bytes 138248 | tf_op jit(solution)/shard_map/ppermute | solution.py:50
  35.7 13.2 %collective-permute-start.14 = (bf16[3,32,384]{2,1,0:T(8,128)(2,1)S(1)}, bf16[3,32,384]{2,1,0:T(8,128)(2,1)S(1)}, u32[]{:S(2)}, u32[]{:S(2)}) collective-permute-start(bf16[3,32,384]{2,1,0:T(8,128)(2,1)S(1)} %get-tuple-element.78), channel_id=1, source_target_pairs={{8,0},{16,8},{24,16},{32,24},{40,32},{48,40},{56,48},{64,56},{72,6... | collective-permute-start | bytes 221192 | tf_op jit(solution)/shard_map/ppermute | solution.py:18
  40.6 8.9 %collective-permute-start.13 = (bf16[3,32,384]{2,1,0:T(8,128)(2,1)S(1)}, bf16[3,32,384]{2,1,0:T(8,128)(2,1)S(1)}, u32[]{:S(2)}, u32[]{:S(2)}) collective-permute-start(bf16[3,32,384]{2,1,0:T(8,128)(2,1)S(1)} %get-tuple-element.79), channel_id=1, source_target_pairs={{0,8},{8,16},{16,24},{24,32},{32,40},{40,48},{48,56},{56,64},{64,7... | collective-permute-start | bytes 221192 | tf_op jit(solution)/shard_map/ppermute | solution.py:15
  43.2 10.1 %collective-permute-start.9 = (bf16[48,768]{1,0:T(8,128)(2,1)S(1)}, bf16[48,768]{1,0:T(8,128)(2,1)S(1)}, u32[]{:S(2)}, u32[]{:S(2)}) collective-permute-start(bf16[48,768]{1,0:T(8,128)(2,1)S(1)} %reshape.63), channel_id=1, source_target_pairs={{24,0},{0,8},{8,16},{16,24},{56,32},{32,40},{40,48},{48,56},{88,64... | collective-permute-start | bytes 221192 | tf_op jit(solution)/shard_map/ppermute | solution.py:50
  43.9 9.4 %collective-permute-start.8 = (bf16[48,768]{1,0:T(8,128)(2,1)S(1)}, bf16[48,768]{1,0:T(8,128)(2,1)S(1)}, u32[]{:S(2)}, u32[]{:S(2)}) collective-permute-start(bf16[48,768]{1,0:T(8,128)(2,1)S(1)} %reshape.63), channel_id=1, source_target_pairs={{16,0},{24,8},{0,16},{8,24},{48,32},{56,40},{32,48},{40,56},{80,64... | collective-permute-start | bytes 221192 | tf_op jit(solution)/shard_map/ppermute | solution.py:50
  53.4 13.3 %collective-permute-start.10 = (bf16[192,768]{1,0:T(8,128)(2,1)S(1)}, bf16[192,768]{1,0:T(8,128)(2,1)S(1)}, u32[]{:S(2)}, u32[]{:S(2)}) collective-permute-start(bf16[192,768]{1,0:T(8,128)(2,1)S(1)} %bitcast.68), channel_id=1, source_target_pairs={{32,0},{40,8},{48,16},{56,24},{64,32},{72,40},{80,48},{88,56},{96,... | collective-permute-start | bytes 884744 | tf_op jit(solution)/shard_map/ppermute | solution.py:50
  54.0 7.2 %collective-permute-start.15 = (bf16[22,3,384]{2,1,0:T(4,128)(2,1)S(1)}, bf16[22,3,384]{2,1,0:T(4,128)(2,1)S(1)}, u32[]{:S(2)}, u32[]{:S(2)}) collective-permute-start(bf16[22,3,384]{2,1,0:T(4,128)(2,1)S(1)} %pad_maximum_fusion.5), channel_id=1, source_target_pairs={{0,1},{1,2},{2,3},{3,4},{4,5},{5,6},{6,7},{8,9},{9,10},{10,11},{11... | collective-permute-start | bytes 152072 | tf_op jit(solution)/shard_map/ppermute | solution.py:34
  58.2 10.5 %collective-permute-start.12 = (bf16[192,768]{1,0:T(8,128)(2,1)S(1)}, bf16[192,768]{1,0:T(8,128)(2,1)S(1)}, u32[]{:S(2)}, u32[]{:S(2)}) collective-permute-start(bf16[192,768]{1,0:T(8,128)(2,1)S(1)} %bitcast.69), channel_id=1, source_target_pairs={{96,0},{104,8},{112,16},{120,24},{0,32},{8,40},{16,48},{24,56},{32... | collective-permute-start | bytes 884744 | tf_op jit(solution)/shard_map/ppermute | solution.py:50
  59.8 8.8 %collective-permute-start.11 = (bf16[192,768]{1,0:T(8,128)(2,1)S(1)}, bf16[192,768]{1,0:T(8,128)(2,1)S(1)}, u32[]{:S(2)}, u32[]{:S(2)}) collective-permute-start(bf16[192,768]{1,0:T(8,128)(2,1)S(1)} %bitcast.70), channel_id=1, source_target_pairs={{64,0},{72,8},{80,16},{88,24},{96,32},{104,40},{112,48},{120,56},{... | collective-permute-start | bytes 884744 | tf_op jit(solution)/shard_map/ppermute | solution.py:50
  75.9 11.7 %collective-permute-start.18 = (bf16[3,16,768]{2,1,0:T(8,128)(2,1)S(1)}, bf16[3,16,768]{2,1,0:T(8,128)(2,1)S(1)}, u32[]{:S(2)}, u32[]{:S(2)}) collective-permute-start(bf16[3,16,768]{2,1,0:T(8,128)(2,1)S(1)} %bitcast.76), channel_id=1, source_target_pairs={{0,8},{8,16},{16,24},{24,32},{32,40},{40,48},{48,56},{56,64},{64,7... | collective-permute-start | bytes 221192 | tf_op jit(solution)/shard_map/ppermute | solution.py:15
  78.8 10.3 %collective-permute-start.19 = (bf16[3,16,768]{2,1,0:T(8,128)(2,1)S(1)}, bf16[3,16,768]{2,1,0:T(8,128)(2,1)S(1)}, u32[]{:S(2)}, u32[]{:S(2)}) collective-permute-start(bf16[3,16,768]{2,1,0:T(8,128)(2,1)S(1)} %bitcast.73), channel_id=1, source_target_pairs={{8,0},{16,8},{24,16},{32,24},{40,32},{48,40},{56,48},{64,56},{72,6... | collective-permute-start | bytes 221192 | tf_op jit(solution)/shard_map/ppermute | solution.py:18
  93.1 6.4 %collective-permute-start.21 = (bf16[14,3,768]{2,1,0:T(4,128)(2,1)S(1)}, bf16[14,3,768]{2,1,0:T(4,128)(2,1)S(1)}, u32[]{:S(2)}, u32[]{:S(2)}) collective-permute-start(bf16[14,3,768]{2,1,0:T(4,128)(2,1)S(1)} %pad_maximum_fusion.2), channel_id=1, source_target_pairs={{1,0},{2,1},{3,2},{4,3},{5,4},{6,5},{7,6},{9,8},{10,9},{11,10},{12... | collective-permute-start | bytes 193544 | tf_op jit(solution)/shard_map/ppermute | solution.py:35
  115.8 9.1 %collective-permute-start.24 = (bf16[3,16,768]{2,1,0:T(8,128)(2,1)S(1)}, bf16[3,16,768]{2,1,0:T(8,128)(2,1)S(1)}, u32[]{:S(2)}, u32[]{:S(2)}) collective-permute-start(bf16[3,16,768]{2,1,0:T(8,128)(2,1)S(1)} %bitcast.77), channel_id=1, source_target_pairs={{0,8},{8,16},{16,24},{24,32},{32,40},{40,48},{48,56},{56,64},{64,7... | collective-permute-start | bytes 221192 | tf_op jit(solution)/shard_map/ppermute | solution.py:15
  117.8 8.5 %collective-permute-start.25 = (bf16[3,16,768]{2,1,0:T(8,128)(2,1)S(1)}, bf16[3,16,768]{2,1,0:T(8,128)(2,1)S(1)}, u32[]{:S(2)}, u32[]{:S(2)}) collective-permute-start(bf16[3,16,768]{2,1,0:T(8,128)(2,1)S(1)} %bitcast.74), channel_id=1, source_target_pairs={{8,0},{16,8},{24,16},{32,24},{40,32},{48,40},{56,48},{64,56},{72,6... | collective-permute-start | bytes 221192 | tf_op jit(solution)/shard_map/ppermute | solution.py:18
  126.4 7.3 %collective-permute-start.26 = (bf16[14,3,768]{2,1,0:T(4,128)(2,1)S(1)}, bf16[14,3,768]{2,1,0:T(4,128)(2,1)S(1)}, u32[]{:S(2)}, u32[]{:S(2)}) collective-permute-start(bf16[14,3,768]{2,1,0:T(4,128)(2,1)S(1)} %pad_maximum_fusion.3), channel_id=1, source_target_pairs={{0,1},{1,2},{2,3},{3,4},{4,5},{5,6},{6,7},{8,9},{9,10},{10,11},{11... | collective-permute-start | bytes 193544 | tf_op jit(solution)/shard_map/ppermute | solution.py:34
  130.2 7.3 %collective-permute-start.27 = (bf16[14,3,768]{2,1,0:T(4,128)(2,1)S(1)}, bf16[14,3,768]{2,1,0:T(4,128)(2,1)S(1)}, u32[]{:S(2)}, u32[]{:S(2)}) collective-permute-start(bf16[14,3,768]{2,1,0:T(4,128)(2,1)S(1)} %pad_maximum_fusion.4), channel_id=1, source_target_pairs={{1,0},{2,1},{3,2},{4,3},{5,4},{6,5},{7,6},{9,8},{10,9},{11,10},{12... | collective-permute-start | bytes 193544 | tf_op jit(solution)/shard_map/ppermute | solution.py:35
  146.9 8.7 %collective-permute-start.28 = (bf16[3,2,16,384]{3,2,1,0:T(8,128)(2,1)S(1)}, bf16[3,2,16,384]{3,2,1,0:T(8,128)(2,1)S(1)}, u32[]{:S(2)}, u32[]{:S(2)}) collective-permute-start(bf16[3,2,16,384]{3,2,1,0:T(8,128)(2,1)S(1)} %bitcast.78), channel_id=1, source_target_pairs={{0,8},{8,16},{16,24},{24,32},{32,40},{40,48},{48,56},{56,64},{64,7... | collective-permute-start | bytes 221192 | tf_op jit(solution)/shard_map/ppermute | solution.py:15
  157.5 7.1 %collective-permute-start.30 = (bf16[22,2,2,384]{3,2,1,0:T(2,128)(2,1)S(1)}, bf16[22,2,2,384]{3,2,1,0:T(2,128)(2,1)S(1)}, u32[]{:S(2)}, u32[]{:S(2)}) collective-permute-start(bf16[22,2,2,384]{3,2,1,0:T(2,128)(2,1)S(1)} %pad_maximum_fusion.7), channel_id=1, source_target_pairs={{0,1},{1,2},{2,3},{3,4},{4,5},{5,6},{6,7},{8,9},{9,10},{10,11},{11... | collective-permute-start | bytes 202760 | tf_op jit(solution)/shard_map/ppermute | solution.py:34
  (36 other events, 304.0 us)
Sparse Core Ops, SparseCore 0:
  35.8 61.8 all-gather.1

commit v5 on v4

--- a/solution.py
+++ b/solution.py
@@ -480,7 +480,9 @@
     share_two = up_two.shape[1]
     packed_one = jnp.concatenate([up_one.T, down_one.T], axis=1)
     packed = jnp.concatenate([up_two.T, down_two.T, packed_one], axis=0)
-    column = ring_collect(packed, "col", col_count, 1)
+    pair = 2 if col_count % 2 == 0 else 1
+    column = ring_collect(ring_collect(packed, "col", pair, 1), "col", col_count // pair, pair)
+    column = column.reshape(col_count, *packed.shape)
     part_one = column[:, 2 * share_two :].reshape(-1, 2 * width_one)
     part_two = jnp.concatenate(
         [

time: 182 us -> 188 us (1.033)
  waiting for transfers between devices: 44.1 us -> 52.6 us
  starting transfers between devices: 79.5 us -> 77.3 us
    ppermute x4, waiting for transfers between devices: 3.92 us -> 9.34 us  [exchange(): lax.ppermute(lax.slice_in_dim(block, block.shape[dim] - width, None, axis...]
    ppermute x13 -> x10, starting transfers between devices: 25.7 us -> 22.3 us  [ring_collect(): arrived = lax.ppermute(piece, axis, pairs)]
    ppermute x4, waiting for transfers between devices: 4.53 us -> 7.82 us  [exchange(): lax.ppermute(lax.slice_in_dim(block, 0, width, axis=dim), axis, backward)]
    ppermute x4, waiting for transfers between devices: 14.6 us -> 11.7 us  [halo_of(): right = lax.ppermute(edge(0, width), 'col', backward)]
    ppermute x13 -> x10, waiting for transfers between devices: 15.5 us -> 18.2 us  [ring_collect(): arrived = lax.ppermute(piece, axis, pairs)]
  transfers between devices with their start and end apart: 33 -> 30, of which waited for: 20 -> 18; matrix products, arithmetic and copies ran while one was open for 1% -> 1% of each run, Pallas kernels for 8% -> 7%
where the time goes in v5:
time: 188 us; the launch traced here: 186 us
  starting transfers between devices  77.3 us (41%)
  waiting for transfers between devices  52.6 us (28%)
  Pallas kernels  34.1 us (18%)
  between operations  15.3 us (8%)
  local copies, waits for them, and re-layouts  4.37 us (2%)
  other arithmetic  2.16 us (1%)
    pallas_call x10, Pallas kernels, block_call(): pl.pallas_call(kernel, out_shape=outputs, in_specs=[whole] * len(operands...  34.1 us
    ppermute x10, starting transfers between devices, ring_collect(): arrived = lax.ppermute(piece, axis, pairs)  22.3 us
    ppermute x4, starting transfers between devices, exchange(): lax.ppermute(lax.slice_in_dim(block, 0, width, axis=dim), axis, backward)  21.1 us
    ppermute x10, waiting for transfers between devices, ring_collect(): arrived = lax.ppermute(piece, axis, pairs)  18.2 us
    ppermute x4, starting transfers between devices, halo_of(): left = lax.ppermute(edge(extent - width, extent), 'col', forward)  15.8 us
    ppermute x4, starting transfers between devices, exchange(): lax.ppermute(lax.slice_in_dim(block, block.shape[dim] - width, None, axis...  12.4 us
    ppermute x4, waiting for transfers between devices, halo_of(): right = lax.ppermute(edge(0, width), 'col', backward)  11.7 us
    ppermute x4, waiting for transfers between devices, exchange(): lax.ppermute(lax.slice_in_dim(block, block.shape[dim] - width, None, axis...  9.34 us
  transfers between devices with their start and end apart: 30, of which 18 were waited for; matrix products, arithmetic and copies ran while one was open for 1% of the time, Pallas kernels for 7%

profile of v5, /device:TPU:2, one launch (start us, length us, event | category | flops | bytes accessed | tf_op | source)
XLA Modules:
  0.0 185.8 jit_solution(16186012608355220195)
XLA Ops:
  12.2 3.3 %collective-permute-start.3 = (bf16[2,30,768]{2,1,0:T(8,128)(2,1)S(1)}, bf16[2,30,768]{2,1,0:T(8,128)(2,1)S(1)}, u32[]{:S(2)}, u32[]{:S(2)}) collective-permute-start(bf16[2,30,768]{2,1,0:T(8,128)(2,1)S(1)} %bitcast_dynamic-update-slice_fusion.11), channel_id=1, source_target_pairs={{6,0},{7,1},{0,2},{1,3},{2,4},{3,5},{4,6},{5,7},{14,8},{15,9},{8,1... | collective-permute-start | bytes 276488 | tf_op jit(solution)/shard_map/ppermute | solution.py:50
  15.5 5.4 %collective-permute-start.2 = (bf16[2,30,768]{2,1,0:T(8,128)(2,1)S(1)}, bf16[2,30,768]{2,1,0:T(8,128)(2,1)S(1)}, u32[]{:S(2)}, u32[]{:S(2)}) collective-permute-start(bf16[2,30,768]{2,1,0:T(8,128)(2,1)S(1)} %bitcast_dynamic-update-slice_fusion.11), channel_id=1, source_target_pairs={{4,0},{5,1},{6,2},{7,3},{0,4},{1,5},{2,6},{3,7},{12,8},{13,9},{14,... | collective-permute-start | bytes 276488 | tf_op jit(solution)/shard_map/ppermute | solution.py:50
  23.6 5.6 %collective-permute-done.1 = bf16[2,30,768]{2,1,0:T(8,128)(2,1)S(1)} collective-permute-done((bf16[2,30,768]{2,1,0:T(8,128)(2,1)S(1)}, bf16[2,30,768]{2,1,0:T(8,128)(2,1)S(1)}, u32[]{:S(2)}, u32[]{:S(2)}) %collective-permute-start.1) | collective-permute-done | bytes 92192 | tf_op jit(solution)/shard_map/ppermute | solution.py:50
  30.5 5.0 %collective-permute-start.11 = (bf16[3,32,384]{2,1,0:T(8,128)(2,1)S(1)}, bf16[3,32,384]{2,1,0:T(8,128)(2,1)S(1)}, u32[]{:S(2)}, u32[]{:S(2)}) collective-permute-start(bf16[3,32,384]{2,1,0:T(8,128)(2,1)S(1)} %get-tuple-element.78), channel_id=1, source_target_pairs={{8,0},{16,8},{24,16},{32,24},{40,32},{48,40},{56,48},{64,56},{72,6... | collective-permute-start | bytes 221192 | tf_op jit(solution)/shard_map/ppermute | solution.py:18
  37.7 6.2 %collective-permute-done.10.top = bf16[3,32,384]{2,1,0:T(8,128)(2,1)S(1)} collective-permute-done((bf16[3,32,384]{2,1,0:T(8,128)(2,1)S(1)}, bf16[3,32,384]{2,1,0:T(8,128)(2,1)S(1)}, u32[]{:S(2)}, u32[]{:S(2)}) %collective-permute-start.10) | collective-permute-done | bytes 73760 | tf_op jit(solution)/shard_map/ppermute | solution.py:15
  50.5 4.5 %collective-permute-done.4 = bf16[48,768]{1,0:T(8,128)(2,1)S(1)} collective-permute-done((bf16[48,768]{1,0:T(8,128)(2,1)S(1)}, bf16[48,768]{1,0:T(8,128)(2,1)S(1)}, u32[]{:S(2)}, u32[]{:S(2)}) %collective-permute-start.4) | collective-permute-done | bytes 73760 | tf_op jit(solution)/shard_map/ppermute | solution.py:50
  55.6 3.5 %shard_map.221 = (bf16[512,384]{1,0:T(8,128)(2,1)S(1)}, f32[512,384]{1,0:T(8,128)S(1)}, bf16[512,384]{1,0:T(8,128)(2,1)S(1)}) custom-call(bf16[16,32,384]{2,1,0:T(8,128)(2,1)S(1)} %bitcast.58, bf16[3,32,384]{2,1,0:T(8,128)(2,1)S(1)} %collective-permute-done.10.top, bf16[3,32,384]{2,1,0:T(8,128)(2,1)S(1)} %collective-permute-done.11.bottom, ...), custom_call_target="tpu_custom_call" | custom-call | tf_op jit(solution)/shard_map/pallas_call | solution.py:419
  61.1 3.6 %collective-permute-start.8 = (bf16[192,768]{1,0:T(8,128)(2,1)S(1)}, bf16[192,768]{1,0:T(8,128)(2,1)S(1)}, u32[]{:S(2)}, u32[]{:S(2)}) collective-permute-start(bf16[192,768]{1,0:T(8,128)(2,1)S(1)} %bitcast.69), channel_id=1, source_target_pairs={{64,0},{72,8},{80,16},{88,24},{96,32},{104,40},{112,48},{120,56},{... | collective-permute-start | bytes 884744 | tf_op jit(solution)/shard_map/ppermute | solution.py:50
  64.9 5.9 %collective-permute-done.8 = bf16[192,768]{1,0:T(8,128)(2,1)S(1)} collective-permute-done((bf16[192,768]{1,0:T(8,128)(2,1)S(1)}, bf16[192,768]{1,0:T(8,128)(2,1)S(1)}, u32[]{:S(2)}, u32[]{:S(2)}) %collective-permute-start.8) | collective-permute-done | bytes 294944 | tf_op jit(solution)/shard_map/ppermute | solution.py:50
  74.0 3.4 %shard_map.223 = (bf16[512,384]{1,0:T(8,128)(2,1)S(1)}, bf16[128,768]{1,0:T(8,128)(2,1)S(1)}) custom-call(bf16[512,384]{1,0:T(8,128)(2,1)S(1)} %get-tuple-element.37.normed, bf16[768,768]{1,0:T(8,128)(2,1)S(1)} %collective-permute-done.14.weights.other, f32[1,768]{1,0:T(1,128)S(1)} %select_n.179.bias.bias_other, f32[512,384]{1,0:T(8,128)S(1)} %shard_map.222.partial, ...), custom_call_target="tpu_custom_call" | custom-call | tf_op jit(solution)/shard_map/pallas_call | solution.py:419
  80.9 8.0 %collective-permute-start.16 = (bf16[3,16,768]{2,1,0:T(8,128)(2,1)S(1)}, bf16[3,16,768]{2,1,0:T(8,128)(2,1)S(1)}, u32[]{:S(2)}, u32[]{:S(2)}) collective-permute-start(bf16[3,16,768]{2,1,0:T(8,128)(2,1)S(1)} %bitcast.72), channel_id=1, source_target_pairs={{8,0},{16,8},{24,16},{32,24},{40,32},{48,40},{56,48},{64,56},{72,6... | collective-permute-start | bytes 221192 | tf_op jit(solution)/shard_map/ppermute | solution.py:18
  91.4 6.9 %collective-permute-start.17 = (bf16[14,3,768]{2,1,0:T(4,128)(2,1)S(1)}, bf16[14,3,768]{2,1,0:T(4,128)(2,1)S(1)}, u32[]{:S(2)}, u32[]{:S(2)}) collective-permute-start(bf16[14,3,768]{2,1,0:T(4,128)(2,1)S(1)} %pad_maximum_fusion.1), channel_id=1, source_target_pairs={{0,1},{1,2},{2,3},{3,4},{4,5},{5,6},{6,7},{8,9},{9,10},{10,11},{11... | collective-permute-start | bytes 193544 | tf_op jit(solution)/shard_map/ppermute | solution.py:34
  100.3 4.4 %collective-permute-done.18.right = bf16[14,3,768]{2,1,0:T(4,128)(2,1)S(1)} collective-permute-done((bf16[14,3,768]{2,1,0:T(4,128)(2,1)S(1)}, bf16[14,3,768]{2,1,0:T(4,128)(2,1)S(1)}, u32[]{:S(2)}, u32[]{:S(2)}) %collective-permute-start.18) | collective-permute-done | bytes 64544 | tf_op jit(solution)/shard_map/ppermute | solution.py:35
  111.3 6.4 %shard_map.225 = (f32[256,768]{1,0:T(8,128)S(1)}, f32[256,768]{1,0:T(8,128)S(1)}) custom-call(bf16[256,768]{1,0:T(8,128)(2,1)S(1)} %copy-done.10, bf16[256,768]{1,0:T(8,128)(2,1)S(1)} %collective-permute-done.19.theirs, bf16[1536,1536]{1,0:T(8,128)(2,1)} %all-gather.2.cloned.1.call-done.weights, f32[1,1536]{1,0:T(1,128)S(1)} %select_n.182.bias), custom_call_target="tpu_custom_call" | custom-call | tf_op jit(solution)/shard_map/pallas_call | solution.py:419
  123.1 6.0 %collective-permute-start.22 = (bf16[3,16,768]{2,1,0:T(8,128)(2,1)S(1)}, bf16[3,16,768]{2,1,0:T(8,128)(2,1)S(1)}, u32[]{:S(2)}, u32[]{:S(2)}) collective-permute-start(bf16[3,16,768]{2,1,0:T(8,128)(2,1)S(1)} %bitcast.73), channel_id=1, source_target_pairs={{8,0},{16,8},{24,16},{32,24},{40,32},{48,40},{56,48},{64,56},{72,6... | collective-permute-start | bytes 221192 | tf_op jit(solution)/shard_map/ppermute | solution.py:18
  129.7 3.9 %collective-permute-done.22.bottom = bf16[3,16,768]{2,1,0:T(8,128)(2,1)S(1)} collective-permute-done((bf16[3,16,768]{2,1,0:T(8,128)(2,1)S(1)}, bf16[3,16,768]{2,1,0:T(8,128)(2,1)S(1)}, u32[]{:S(2)}, u32[]{:S(2)}) %collective-permute-start.22) | collective-permute-done | bytes 73760 | tf_op jit(solution)/shard_map/ppermute | solution.py:18
  133.7 3.9 %collective-permute-start.23 = (bf16[14,3,768]{2,1,0:T(4,128)(2,1)S(1)}, bf16[14,3,768]{2,1,0:T(4,128)(2,1)S(1)}, u32[]{:S(2)}, u32[]{:S(2)}) collective-permute-start(bf16[14,3,768]{2,1,0:T(4,128)(2,1)S(1)} %pad_maximum_fusion.3), channel_id=1, source_target_pairs={{0,1},{1,2},{2,3},{3,4},{4,5},{5,6},{6,7},{8,9},{9,10},{10,11},{11... | collective-permute-start | bytes 193544 | tf_op jit(solution)/shard_map/ppermute | solution.py:34
  141.2 2.9 %collective-permute-done.24.right = bf16[14,3,768]{2,1,0:T(4,128)(2,1)S(1)} collective-permute-done((bf16[14,3,768]{2,1,0:T(4,128)(2,1)S(1)}, bf16[14,3,768]{2,1,0:T(4,128)(2,1)S(1)}, u32[]{:S(2)}, u32[]{:S(2)}) %collective-permute-start.24) | collective-permute-done | bytes 64544 | tf_op jit(solution)/shard_map/ppermute | solution.py:35
  145.8 7.6 %shard_map.229 = (bf16[512,384]{1,0:T(8,128)(2,1)S(1)}, f32[512,384]{1,0:T(8,128)S(1)}) custom-call(bf16[128,768]{1,0:T(8,128)(2,1)S(1)} %shard_map.227.d_merged, bf16[1536,768]{1,0:T(8,128)(2,1)} %merge.3, bf16[512,384]{1,0:T(8,128)(2,1)S(1)} %copy-done.8, f32[1,384]{1,0:T(1,128)S(1)} %broadcast_in_dim.114.gain.gain_mid, ...), custom_call_target="tpu_custom_call" | custom-call | tf_op jit(solution)/shard_map/pallas_call | solution.py:419
  153.4 5.9 %collective-permute-start.25 = (bf16[3,2,16,384]{3,2,1,0:T(8,128)(2,1)S(1)}, bf16[3,2,16,384]{3,2,1,0:T(8,128)(2,1)S(1)}, u32[]{:S(2)}, u32[]{:S(2)}) collective-permute-start(bf16[3,2,16,384]{3,2,1,0:T(8,128)(2,1)S(1)} %bitcast.77), channel_id=1, source_target_pairs={{0,8},{8,16},{16,24},{24,32},{32,40},{40,48},{48,56},{56,64},{64,7... | collective-permute-start | bytes 221192 | tf_op jit(solution)/shard_map/ppermute | solution.py:15
  161.8 3.9 %collective-permute-done.26.bottom = bf16[3,2,16,384]{3,2,1,0:T(8,128)(2,1)S(1)} collective-permute-done((bf16[3,2,16,384]{3,2,1,0:T(8,128)(2,1)S(1)}, bf16[3,2,16,384]{3,2,1,0:T(8,128)(2,1)S(1)}, u32[]{:S(2)}, u32[]{:S(2)}) %collective-permute-start.26) | collective-permute-done | bytes 73760 | tf_op jit(solution)/shard_map/ppermute | solution.py:18
  165.8 3.3 %collective-permute-start.27 = (bf16[22,2,2,384]{3,2,1,0:T(2,128)(2,1)S(1)}, bf16[22,2,2,384]{3,2,1,0:T(2,128)(2,1)S(1)}, u32[]{:S(2)}, u32[]{:S(2)}) collective-permute-start(bf16[22,2,2,384]{3,2,1,0:T(2,128)(2,1)S(1)} %pad_maximum_fusion.7), channel_id=1, source_target_pairs={{0,1},{1,2},{2,3},{3,4},{4,5},{5,6},{6,7},{8,9},{9,10},{10,11},{11... | collective-permute-start | bytes 202760 | tf_op jit(solution)/shard_map/ppermute | solution.py:34
  171.0 4.4 %collective-permute-done.28.right = bf16[22,2,2,384]{3,2,1,0:T(2,128)(2,1)S(1)} collective-permute-done((bf16[22,2,2,384]{3,2,1,0:T(2,128)(2,1)S(1)}, bf16[22,2,2,384]{3,2,1,0:T(2,128)(2,1)S(1)}, u32[]{:S(2)}, u32[]{:S(2)}) %collective-permute-start.28) | collective-permute-done | bytes 67616 | tf_op jit(solution)/shard_map/ppermute | solution.py:35
  175.4 3.5 %shard_map.230 = bf16[16,32,384]{2,1,0:T(8,128)(2,1)} custom-call(bf16[16,2,16,384]{3,2,1,0:T(8,128)(2,1)S(1)} %bitcast.60, bf16[3,2,16,384]{3,2,1,0:T(8,128)(2,1)S(1)} %collective-permute-done.25.top, bf16[3,2,16,384]{3,2,1,0:T(8,128)(2,1)S(1)} %collective-permute-done.26.bottom, bf16[22,2,2,384]{3,2,1,0:T(2,128)(2,1)S(1)} %collective-permute-done.27.left, ...), custom_call_target="tpu_custom_call" | custom-call | tf_op jit(solution)/shard_map/pallas_call | solution.py:419
  (166 shorter events, 53.0 us)
Async XLA Ops:
  7.2 101.2 %all-gather.2.cloned.1.call-start = ((), (), s32[]{:S(2)}) async-start(), calls=%async_computation | async-start | bytes 5013504 | tf_op jit(solution)/shard_map/all_gather | solution.py:494
  12.2 17.1 %collective-permute-start.3 = (bf16[2,30,768]{2,1,0:T(8,128)(2,1)S(1)}, bf16[2,30,768]{2,1,0:T(8,128)(2,1)S(1)}, u32[]{:S(2)}, u32[]{:S(2)}) collective-permute-start(bf16[2,30,768]{2,1,0:T(8,128)(2,1)S(1)} %bitcast_dynamic-update-slice_fusion.11), channel_id=1, source_target_pairs={{6,0},{7,1},{0,2},{1,3},{2,4},{3,5},{4,6},{5,7},{14,8},{15,9},{8,1... | collective-permute-start | bytes 276488 | tf_op jit(solution)/shard_map/ppermute | solution.py:50
  15.5 13.8 %collective-permute-start.2 = (bf16[2,30,768]{2,1,0:T(8,128)(2,1)S(1)}, bf16[2,30,768]{2,1,0:T(8,128)(2,1)S(1)}, u32[]{:S(2)}, u32[]{:S(2)}) collective-permute-start(bf16[2,30,768]{2,1,0:T(8,128)(2,1)S(1)} %bitcast_dynamic-update-slice_fusion.11), channel_id=1, source_target_pairs={{4,0},{5,1},{6,2},{7,3},{0,4},{1,5},{2,6},{3,7},{12,8},{13,9},{14,... | collective-permute-start | bytes 276488 | tf_op jit(solution)/shard_map/ppermute | solution.py:50
  20.9 8.4 %collective-permute-start.1 = (bf16[2,30,768]{2,1,0:T(8,128)(2,1)S(1)}, bf16[2,30,768]{2,1,0:T(8,128)(2,1)S(1)}, u32[]{:S(2)}, u32[]{:S(2)}) collective-permute-start(bf16[2,30,768]{2,1,0:T(8,128)(2,1)S(1)} %bitcast_dynamic-update-slice_fusion.11), channel_id=1, source_target_pairs={{2,0},{3,1},{4,2},{5,3},{6,4},{7,5},{0,6},{1,7},{10,8},{11,9},{12,... | collective-permute-start | bytes 276488 | tf_op jit(solution)/shard_map/ppermute | solution.py:50
  30.5 7.1 %collective-permute-start.11 = (bf16[3,32,384]{2,1,0:T(8,128)(2,1)S(1)}, bf16[3,32,384]{2,1,0:T(8,128)(2,1)S(1)}, u32[]{:S(2)}, u32[]{:S(2)}) collective-permute-start(bf16[3,32,384]{2,1,0:T(8,128)(2,1)S(1)} %get-tuple-element.78), channel_id=1, source_target_pairs={{8,0},{16,8},{24,16},{32,24},{40,32},{48,40},{56,48},{64,56},{72,6... | collective-permute-start | bytes 221192 | tf_op jit(solution)/shard_map/ppermute | solution.py:18
  35.5 8.4 %collective-permute-start.10 = (bf16[3,32,384]{2,1,0:T(8,128)(2,1)S(1)}, bf16[3,32,384]{2,1,0:T(8,128)(2,1)S(1)}, u32[]{:S(2)}, u32[]{:S(2)}) collective-permute-start(bf16[3,32,384]{2,1,0:T(8,128)(2,1)S(1)} %get-tuple-element.79), channel_id=1, source_target_pairs={{0,8},{8,16},{16,24},{24,32},{32,40},{40,48},{48,56},{56,64},{64,7... | collective-permute-start | bytes 221192 | tf_op jit(solution)/shard_map/ppermute | solution.py:15
  44.0 11.6 %collective-permute-start.12 = (bf16[22,3,384]{2,1,0:T(4,128)(2,1)S(1)}, bf16[22,3,384]{2,1,0:T(4,128)(2,1)S(1)}, u32[]{:S(2)}, u32[]{:S(2)}) collective-permute-start(bf16[22,3,384]{2,1,0:T(4,128)(2,1)S(1)} %pad_maximum_fusion.5), channel_id=1, source_target_pairs={{0,1},{1,2},{2,3},{3,4},{4,5},{5,6},{6,7},{8,9},{9,10},{10,11},{11... | collective-permute-start | bytes 152072 | tf_op jit(solution)/shard_map/ppermute | solution.py:34
  45.7 9.9 %collective-permute-start.13 = (bf16[22,3,384]{2,1,0:T(4,128)(2,1)S(1)}, bf16[22,3,384]{2,1,0:T(4,128)(2,1)S(1)}, u32[]{:S(2)}, u32[]{:S(2)}) collective-permute-start(bf16[22,3,384]{2,1,0:T(4,128)(2,1)S(1)} %pad_maximum_fusion.6), channel_id=1, source_target_pairs={{1,0},{2,1},{3,2},{4,3},{5,4},{6,5},{7,6},{9,8},{10,9},{11,10},{12... | collective-permute-start | bytes 152072 | tf_op jit(solution)/shard_map/ppermute | solution.py:35
  47.1 7.9 %collective-permute-start.6 = (bf16[48,768]{1,0:T(8,128)(2,1)S(1)}, bf16[48,768]{1,0:T(8,128)(2,1)S(1)}, u32[]{:S(2)}, u32[]{:S(2)}) collective-permute-start(bf16[48,768]{1,0:T(8,128)(2,1)S(1)} %reshape.67), channel_id=1, source_target_pairs={{24,0},{0,8},{8,16},{16,24},{56,32},{32,40},{40,48},{48,56},{88,64... | collective-permute-start | bytes 221192 | tf_op jit(solution)/shard_map/ppermute | solution.py:50
  47.2 7.8 %collective-permute-start.5 = (bf16[48,768]{1,0:T(8,128)(2,1)S(1)}, bf16[48,768]{1,0:T(8,128)(2,1)S(1)}, u32[]{:S(2)}, u32[]{:S(2)}) collective-permute-start(bf16[48,768]{1,0:T(8,128)(2,1)S(1)} %reshape.67), channel_id=1, source_target_pairs={{16,0},{24,8},{0,16},{8,24},{48,32},{56,40},{32,48},{40,56},{80,64... | collective-permute-start | bytes 221192 | tf_op jit(solution)/shard_map/ppermute | solution.py:50
  48.3 6.7 %collective-permute-start.4 = (bf16[48,768]{1,0:T(8,128)(2,1)S(1)}, bf16[48,768]{1,0:T(8,128)(2,1)S(1)}, u32[]{:S(2)}, u32[]{:S(2)}) collective-permute-start(bf16[48,768]{1,0:T(8,128)(2,1)S(1)} %reshape.67), channel_id=1, source_target_pairs={{8,0},{16,8},{24,16},{0,24},{40,32},{48,40},{56,48},{32,56},{72,64... | collective-permute-start | bytes 221192 | tf_op jit(solution)/shard_map/ppermute | solution.py:50
  55.1 9.8 %collective-permute-start.7 = (bf16[192,768]{1,0:T(8,128)(2,1)S(1)}, bf16[192,768]{1,0:T(8,128)(2,1)S(1)}, u32[]{:S(2)}, u32[]{:S(2)}) collective-permute-start(bf16[192,768]{1,0:T(8,128)(2,1)S(1)} %bitcast.67), channel_id=1, source_target_pairs={{32,0},{40,8},{48,16},{56,24},{64,32},{72,40},{80,48},{88,56},{96,... | collective-permute-start | bytes 884744 | tf_op jit(solution)/shard_map/ppermute | solution.py:50
  59.1 11.7 %collective-permute-start.9 = (bf16[192,768]{1,0:T(8,128)(2,1)S(1)}, bf16[192,768]{1,0:T(8,128)(2,1)S(1)}, u32[]{:S(2)}, u32[]{:S(2)}) collective-permute-start(bf16[192,768]{1,0:T(8,128)(2,1)S(1)} %bitcast.68), channel_id=1, source_target_pairs={{96,0},{104,8},{112,16},{120,24},{0,32},{8,40},{16,48},{24,56},{32... | collective-permute-start | bytes 884744 | tf_op jit(solution)/shard_map/ppermute | solution.py:50
  61.1 9.7 %collective-permute-start.8 = (bf16[192,768]{1,0:T(8,128)(2,1)S(1)}, bf16[192,768]{1,0:T(8,128)(2,1)S(1)}, u32[]{:S(2)}, u32[]{:S(2)}) collective-permute-start(bf16[192,768]{1,0:T(8,128)(2,1)S(1)} %bitcast.69), channel_id=1, source_target_pairs={{64,0},{72,8},{80,16},{88,24},{96,32},{104,40},{112,48},{120,56},{... | collective-permute-start | bytes 884744 | tf_op jit(solution)/shard_map/ppermute | solution.py:50
  78.2 13.0 %collective-permute-start.15 = (bf16[3,16,768]{2,1,0:T(8,128)(2,1)S(1)}, bf16[3,16,768]{2,1,0:T(8,128)(2,1)S(1)}, u32[]{:S(2)}, u32[]{:S(2)}) collective-permute-start(bf16[3,16,768]{2,1,0:T(8,128)(2,1)S(1)} %bitcast.75), channel_id=1, source_target_pairs={{0,8},{8,16},{16,24},{24,32},{32,40},{40,48},{48,56},{56,64},{64,7... | collective-permute-start | bytes 221192 | tf_op jit(solution)/shard_map/ppermute | solution.py:15
  80.9 10.3 %collective-permute-start.16 = (bf16[3,16,768]{2,1,0:T(8,128)(2,1)S(1)}, bf16[3,16,768]{2,1,0:T(8,128)(2,1)S(1)}, u32[]{:S(2)}, u32[]{:S(2)}) collective-permute-start(bf16[3,16,768]{2,1,0:T(8,128)(2,1)S(1)} %bitcast.72), channel_id=1, source_target_pairs={{8,0},{16,8},{24,16},{32,24},{40,32},{48,40},{56,48},{64,56},{72,6... | collective-permute-start | bytes 221192 | tf_op jit(solution)/shard_map/ppermute | solution.py:18
  91.4 9.0 %collective-permute-start.17 = (bf16[14,3,768]{2,1,0:T(4,128)(2,1)S(1)}, bf16[14,3,768]{2,1,0:T(4,128)(2,1)S(1)}, u32[]{:S(2)}, u32[]{:S(2)}) collective-permute-start(bf16[14,3,768]{2,1,0:T(4,128)(2,1)S(1)} %pad_maximum_fusion.1), channel_id=1, source_target_pairs={{0,1},{1,2},{2,3},{3,4},{4,5},{5,6},{6,7},{8,9},{9,10},{10,11},{11... | collective-permute-start | bytes 193544 | tf_op jit(solution)/shard_map/ppermute | solution.py:34
  98.3 6.4 %collective-permute-start.18 = (bf16[14,3,768]{2,1,0:T(4,128)(2,1)S(1)}, bf16[14,3,768]{2,1,0:T(4,128)(2,1)S(1)}, u32[]{:S(2)}, u32[]{:S(2)}) collective-permute-start(bf16[14,3,768]{2,1,0:T(4,128)(2,1)S(1)} %pad_maximum_fusion.2), channel_id=1, source_target_pairs={{1,0},{2,1},{3,2},{4,3},{5,4},{6,5},{7,6},{9,8},{10,9},{11,10},{12... | collective-permute-start | bytes 193544 | tf_op jit(solution)/shard_map/ppermute | solution.py:35
  121.1 8.5 %collective-permute-start.21 = (bf16[3,16,768]{2,1,0:T(8,128)(2,1)S(1)}, bf16[3,16,768]{2,1,0:T(8,128)(2,1)S(1)}, u32[]{:S(2)}, u32[]{:S(2)}) collective-permute-start(bf16[3,16,768]{2,1,0:T(8,128)(2,1)S(1)} %bitcast.76), channel_id=1, source_target_pairs={{0,8},{8,16},{16,24},{24,32},{32,40},{40,48},{48,56},{56,64},{64,7... | collective-permute-start | bytes 221192 | tf_op jit(solution)/shard_map/ppermute | solution.py:15
  123.1 10.5 %collective-permute-start.22 = (bf16[3,16,768]{2,1,0:T(8,128)(2,1)S(1)}, bf16[3,16,768]{2,1,0:T(8,128)(2,1)S(1)}, u32[]{:S(2)}, u32[]{:S(2)}) collective-permute-start(bf16[3,16,768]{2,1,0:T(8,128)(2,1)S(1)} %bitcast.73), channel_id=1, source_target_pairs={{8,0},{16,8},{24,16},{32,24},{40,32},{48,40},{56,48},{64,56},{72,6... | collective-permute-start | bytes 221192 | tf_op jit(solution)/shard_map/ppermute | solution.py:18
  133.7 7.5 %collective-permute-start.23 = (bf16[14,3,768]{2,1,0:T(4,128)(2,1)S(1)}, bf16[14,3,768]{2,1,0:T(4,128)(2,1)S(1)}, u32[]{:S(2)}, u32[]{:S(2)}) collective-permute-start(bf16[14,3,768]{2,1,0:T(4,128)(2,1)S(1)} %pad_maximum_fusion.3), channel_id=1, source_target_pairs={{0,1},{1,2},{2,3},{3,4},{4,5},{5,6},{6,7},{8,9},{9,10},{10,11},{11... | collective-permute-start | bytes 193544 | tf_op jit(solution)/shard_map/ppermute | solution.py:34
  137.7 6.4 %collective-permute-start.24 = (bf16[14,3,768]{2,1,0:T(4,128)(2,1)S(1)}, bf16[14,3,768]{2,1,0:T(4,128)(2,1)S(1)}, u32[]{:S(2)}, u32[]{:S(2)}) collective-permute-start(bf16[14,3,768]{2,1,0:T(4,128)(2,1)S(1)} %pad_maximum_fusion.4), channel_id=1, source_target_pairs={{1,0},{2,1},{3,2},{4,3},{5,4},{6,5},{7,6},{9,8},{10,9},{11,10},{12... | collective-permute-start | bytes 193544 | tf_op jit(solution)/shard_map/ppermute | solution.py:35
  153.4 8.4 %collective-permute-start.25 = (bf16[3,2,16,384]{3,2,1,0:T(8,128)(2,1)S(1)}, bf16[3,2,16,384]{3,2,1,0:T(8,128)(2,1)S(1)}, u32[]{:S(2)}, u32[]{:S(2)}) collective-permute-start(bf16[3,2,16,384]{3,2,1,0:T(8,128)(2,1)S(1)} %bitcast.77), channel_id=1, source_target_pairs={{0,8},{8,16},{16,24},{24,32},{32,40},{40,48},{48,56},{56,64},{64,7... | collective-permute-start | bytes 221192 | tf_op jit(solution)/shard_map/ppermute | solution.py:15
  159.4 6.2 %collective-permute-start.26 = (bf16[3,2,16,384]{3,2,1,0:T(8,128)(2,1)S(1)}, bf16[3,2,16,384]{3,2,1,0:T(8,128)(2,1)S(1)}, u32[]{:S(2)}, u32[]{:S(2)}) collective-permute-start(bf16[3,2,16,384]{3,2,1,0:T(8,128)(2,1)S(1)} %bitcast.74), channel_id=1, source_target_pairs={{8,0},{16,8},{24,16},{32,24},{40,32},{48,40},{56,48},{64,56},{72,6... | collective-permute-start | bytes 221192 | tf_op jit(solution)/shard_map/ppermute | solution.py:18
  (33 other events, 508.7 us)
Sparse Core Ops, SparseCore 0:
  30.4 61.7 all-gather.1
